TPU v7x, 32 devices: a whole 2x2x4 slice. The times are simulated.
32 devices in a mesh: dp: 2 (over y), pipe: 2 (over core), gz: 2 (over x), gy: 4 (over z).
Axes of the slice: x: 2, y: 2, z: 4, core: 2. Of those that a mesh axis runs over, the one named last changes fastest.
Arguments:
- volumes: bfloat16 [4, 32, 4, 32, 128], P('dp', None, 'gz', 'gy'), may hold values from -6 to 6
- conv_one: bfloat16 [32, 4, 3, 3, 3], replicated, may hold values from -0.625 to 0.625
- conv_two: bfloat16 [64, 32, 3, 3, 3], replicated, may hold values from -0.21875 to 0.21875
- cotangent: bfloat16 [4, 64, 2, 16, 64], P('dp', None, 'gz', 'gy'), may hold values from -24 to 24
Outputs:
- boundary_acts: bfloat16 [4, 32, 4, 32, 128], P('dp', None, 'gz', 'gy')
- boundary_grads: bfloat16 [4, 32, 4, 32, 128], P('dp', None, 'gz', 'gy')
- grad_conv_one: float32 [32, 4, 3, 3, 3], replicated
- grad_conv_two: float32 [64, 32, 3, 3, 3], replicated
All inputs are finite; a program needn't handle non-finite values.
Results may differ from a plain program's by a relative error of at most 0.0085.
Values may be sent and summed in bfloat16 or wider, within the bound.
No kernel may reach another device: no remote copies, remote signals or barrier semaphores. Data moves between devices by JAX's collectives and lax.ppermute only.
A program may use at most 128 MiB of HBM per device.

v0:
```python
import functools

import jax
import jax.numpy as jnp
from jax import lax
from jax.experimental import pallas as pl
from jax.experimental.pallas import tpu as pltpu
from jax.sharding import PartitionSpec as P

LEAK = 0.3
REACH = 3
F32 = jnp.float32
BF16 = jnp.bfloat16
PARAMS = pltpu.CompilerParams(vmem_limit_bytes=48 * 1024 * 1024)


def pairs(count, odd):
    out = []
    for i in range(odd, count - 1, 2):
        out += [(i, i + 1), (i + 1, i)]
    return out


def swap(cells, z_count, y_count, z_pairs, y_pairs):
    z_list = [(i, i) for i in range(z_count)] if z_pairs is None else z_pairs
    y_list = [(i, i) for i in range(y_count)] if y_pairs is None else y_pairs
    perm = [(a * y_count + c, b * y_count + d) for a, b in z_list for c, d in y_list]
    return lax.ppermute(cells, ("gz", "gy"), perm)


def shift(block, step, width):
    parts = []
    for at in range(0, block.shape[1], width):
        part = block[:, at : at + width]
        lane = lax.broadcasted_iota(jnp.int32, part.shape, 1)
        edge = 0 if step > 0 else width - 1
        parts.append(jnp.where(lane == edge, 0.0, pltpu.roll(part, step % width, 1)))
    return parts[0] if len(parts) == 1 else jnp.concatenate(parts, axis=1)


class Plan:
    def __init__(self, volumes, cotangent, conv_one, conv_two):
        _, self.fold, self.z, self.y, self.x = volumes.shape
        self.c_one, self.c_in = conv_one.shape[:2]
        self.c_two = conv_two.shape[0]
        self.cz, self.cy = cotangent.shape[2:4]
        self.gz, self.gy = lax.axis_size("gz"), lax.axis_size("gy")
        self.h = min(REACH, self.z)
        sides = min(self.gz - 1, 2)
        self.win = self.z + sides * self.h
        self.planes = self.z + sides
        self.wide = self.y + 2 * REACH
        self.mid = self.y + 4
        self.slim = self.y + 2
        self.z_kinds = [None] + [k for k in (0, 1) if len(pairs(self.gz, k)) > 0]
        self.y_kinds = [None] + [k for k in (0, 1) if len(pairs(self.gy, k)) > 0]
        self.kinds = [(a, b) for a in self.z_kinds for b in self.y_kinds]

    def at_z(self):
        if self.gz > 2:
            return self.h, self.h - 1
        if self.gz == 1:
            return 0, 0
        me = lax.axis_index("gz")
        return me * self.h, me * (self.h - 1)

    def blocks(self, kind):
        z_kind, y_kind = kind
        nz, nc = (self.z, self.cz) if z_kind is None else (self.h, 1)
        ny, np_ = (self.y, self.cy // 2) if y_kind is None else (REACH, 1)
        return nz, ny, nc, np_

    def rows(self, kind):
        nz, ny, nc, np_ = self.blocks(kind)
        return nz * ny * self.fold + nc * np_ * self.c_two


def message_key(plan, kind):
    z_kind, y_kind = kind
    if z_kind is not None and plan.h == plan.z and plan.cz == 1:
        z_kind = None
    return z_kind, y_kind


def pack_kernel(plan, keys, vol_ref, cot_ref, *refs):
    out_refs, (cells, cots) = refs[: len(keys)], refs[len(keys) :]
    me = lax.axis_index("pipe")
    for z in range(plan.z):
        block = jnp.swapaxes(vol_ref[me, :, z].astype(F32), 0, 1).astype(BF16)
        for y in range(plan.y):
            cells[z, y] = block[y]
    for z in range(plan.cz):
        block = jnp.swapaxes(cot_ref[me, :, z].astype(F32), 0, 1)
        for m in range(plan.cy // 2):
            cots[z, m] = jnp.concatenate([block[2 * m], block[2 * m + 1]], axis=1).astype(BF16)
    odd_z, odd_y = lax.axis_index("gz") % 2, lax.axis_index("gy") % 2
    for key, out_ref in zip(keys, out_refs):
        nz, ny, nc, np_ = plan.blocks(key)
        z_low = 0 if key[0] is None else (odd_z == 1 - key[0])
        y_low = 0 if key[1] is None else (odd_y == 1 - key[1])
        z0 = jnp.where(z_low, 0, plan.z - nz) if key[0] is not None else 0
        c0 = jnp.where(z_low, 0, plan.cz - nc) if key[0] is not None else 0
        y0 = jnp.where(y_low, 0, plan.y - ny) if key[1] is not None else 0
        p0 = jnp.where(y_low, 0, plan.cy // 2 - np_) if key[1] is not None else 0
        at = 0
        for i in range(nz):
            for j in range(ny):
                out_ref[at : at + plan.fold] = cells[z0 + i, y0 + j]
                at += plan.fold
        for i in range(nc):
            for j in range(np_):
                out_ref[at : at + plan.c_two] = cots[c0 + i, p0 + j]
                at += plan.c_two


def weight_kernel(plan, one_ref, two_ref, w1_ref, w2_ref, wb_ref):
    c_in, c_one, c_two = plan.c_in, plan.c_one, plan.c_two
    none = jnp.zeros((c_in, c_one), F32)
    pairs_x = {}
    for dz in range(3):
        for dy in range(3):
            tap = [one_ref[(dz * 3 + dy) * 3 + dx].astype(F32) * 0.5 for dx in range(3)]
            pairs_x[dz, dy, 0] = jnp.concatenate(
                [jnp.concatenate([tap[1], tap[0]], 1), jnp.concatenate([tap[2], tap[1]], 1)], 0
            )
            pairs_x[dz, dy, 1] = jnp.concatenate(
                [jnp.concatenate([none, tap[2]], 1), jnp.concatenate([tap[0], none], 1)], 0
            )
    blank = jnp.zeros((2 * c_in, 2 * c_one), F32)
    rows = []
    for fz in range(4):
        for s in range(2):
            for fy in (1, 2, 3, 0):
                rows.append(
                    jnp.concatenate(
                        [
                            pairs_x.get((fz - a, fy - b, s), blank)
                            for a in range(2)
                            for b in range(2)
                        ],
                        axis=1,
                    )
                )
    w1_ref[...] = jnp.concatenate(rows, axis=0).T.astype(BF16)
    for dx in range(3):
        taps = [two_ref[zy * 3 + dx] for zy in range(9)]
        wb_ref[dx * c_one : (dx + 1) * c_one] = jnp.concatenate(taps, axis=1)
        tall = jnp.concatenate([t.astype(F32) * 0.5 for t in taps], axis=0)
        w2_ref[dx * c_two : (dx + 1) * c_two] = tall.T.astype(BF16)


def main_kernel(plan, count, *refs):
    msgs = refs[:count]
    w1_ref, w2_ref, wb_ref, out_ref, keep_ref, give_ref = refs[count : count + 6]
    cells, fine, act, sg, cot, tan, back, first, sgx, total = refs[count + 6 :]
    X, Y, Z = plan.x, plan.y, plan.z
    fold, c_in, c_one, c_two = plan.fold, plan.c_in, plan.c_one, plan.c_two
    me, my_z, my_y = lax.axis_index("pipe"), lax.axis_index("gz"), lax.axis_index("gy")
    own, first_sg = plan.at_z()
    odd_z, odd_y = my_z % 2, my_y % 2

    pick = (
        lax.broadcasted_iota(jnp.int32, (X, 2 * X), 1) // 2
        == lax.broadcasted_iota(jnp.int32, (X, 2 * X), 0)
    )
    pick = jnp.where(pick, 0.125, 0.0).astype(BF16)
    if plan.gz > 1:
        cot[...] = jnp.zeros_like(cot)
    for kind, msg in zip(plan.kinds, msgs):
        nz, ny, nc, np_ = plan.blocks(kind)
        z_kind, y_kind = kind
        if z_kind is None:
            z0, c0 = own, 1
        else:
            before = odd_z == 1 - z_kind
            z0 = jnp.where(before, own - plan.h, own + Z)
            z0 = jnp.clip(z0, 0, plan.win - plan.h)
            c0 = jnp.where(before, 0, plan.cz + 1)
        at = 0
        below = None if y_kind is None else odd_y == 1 - y_kind
        y0 = REACH if y_kind is None else jnp.where(below, 0, Y + REACH)
        for i in range(nz):
            for j in range(ny):
                cells[z0 + i, y0 + j] = msg[at : at + fold]
                at += fold
        for i in range(nc):
            for j in range(np_):
                up = jnp.dot(msg[at : at + c_two], pick, preferred_element_type=F32).astype(BF16)
                at += c_two
                one, two = up[:, :X], up[:, X:]
                if y_kind is None:
                    for r, piece in enumerate((one, one, two, two)):
                        lane = (4 * j + r + 1) * X
                        cot[c0 + i, :, lane : lane + X] = piece
                else:
                    lane = pl.multiple_of(jnp.where(below, 0, (Y + 1) * X), X)
                    cot[c0 + i, :, pl.ds(lane, X)] = jnp.where(below, two, one)

    quarter = 2 * c_in
    fine[0 : 8 * quarter] = jnp.zeros((8 * quarter, plan.mid * X), BF16)
    last = 8 * quarter + plan.win * 16 * quarter
    fine[last : last + 8 * quarter] = jnp.zeros((8 * quarter, plan.mid * X), BF16)
    is_c = (lax.broadcasted_iota(jnp.int32, (fold, X), 0) // c_in) % 2 == 1

    def spread(w, carry):
        base = pl.multiple_of(8 * quarter + w * 16 * quarter, 8 * quarter)
        kept = []
        for r in range(plan.wide):
            mid = cells[w, r].astype(F32)
            side = jnp.where(is_c, shift(mid, 1, X), shift(mid, -1, X))
            kept.append((mid, side))
            if r < 2:
                continue
            lane = (r - 2) * X
            for a in range(2):
                for s in range(2):
                    lo, here, hi = kept[r - 2][s], kept[r - 1][s], kept[r][s]
                    at = a * 2 * quarter
                    near = here[at : at + 2 * quarter]
                    far = jnp.concatenate(
                        [hi[at : at + quarter], lo[at + quarter : at + 2 * quarter]], axis=0
                    )
                    row = base + (a * 8 + s * 4) * quarter
                    fine[pl.ds(row, 2 * quarter), lane : lane + X] = near.astype(BF16)
                    fine[pl.ds(row + 2 * quarter, 2 * quarter), lane : lane + X] = far.astype(BF16)
        return carry

    lax.fori_loop(0, plan.win, spread, 0)

    w1 = w1_ref[...]
    act[0] = jnp.zeros(act.shape[1:], BF16)
    act[plan.win + 1] = jnp.zeros(act.shape[1:], BF16)

    def first_section(w, carry):
        row0 = pl.multiple_of(w * 16 * quarter, 8 * quarter)
        z_abs = my_z * Z + w - own
        z_ok = (z_abs >= 0) & (z_abs < plan.gz * Z)
        for q in range(plan.mid // 2):
            lane = 2 * q * X
            half = jnp.dot(
                w1, fine[pl.ds(row0, 32 * quarter), lane : lane + 2 * X], preferred_element_type=F32
            )
            line, prod = None, None
            for g in range(8):
                v = half[g * c_one : (g + 1) * c_one]
                t = jnp.tanh(v)
                if 0 < q < plan.mid // 2 - 1:
                    tan[w, g * c_one : (g + 1) * c_one, lane - 2 * X : lane] = t
                bent = jnp.maximum(v, LEAK * v)
                grown = 1.0 + jnp.abs(t)
                line = bent if line is None else line + bent
                prod = grown if prod is None else prod * grown
            mean = 0.25 * line - ((1.0 - LEAK) / 8.0) * jnp.log(prod)
            ok = z_ok
            if q == 0:
                ok = ok & (my_y > 0)
            if q == plan.mid // 2 - 1:
                ok = ok & (my_y < plan.gy - 1)
            act[w + 1, :, lane : lane + 2 * X] = jnp.where(ok, mean, 0.0).astype(BF16)
        return carry

    lax.fori_loop(0, plan.win, first_section, 0)

    w2 = w2_ref[...]
    sg[0] = jnp.zeros(sg.shape[1:], BF16)
    sg[plan.planes + 1] = jnp.zeros(sg.shape[1:], BF16)

    def around(ref, w, lane, size, sign):
        return jnp.concatenate(
            [
                ref[w + 1 + sign * dz, :, lane + sign * dy * X : lane + sign * dy * X + size]
                for dz in (-1, 0, 1)
                for dy in (-1, 0, 1)
            ],
            axis=0,
        )

    def second_section(j, carry):
        w = first_sg + j
        c_at = (w - own + 2) // 2
        for q in range(plan.slim // 2):
            lane = 2 * q * X
            taps = jnp.dot(w2, around(act, w, lane + X, 2 * X, 1), preferred_element_type=F32)
            half = (
                taps[c_two : 2 * c_two]
                + shift(taps[:c_two], 1, X)
                + shift(taps[2 * c_two :], -1, X)
            )
            slope = (LEAK + 1.0) / 2 + ((1.0 - LEAK) / 2) * jnp.tanh(half)
            part = cot[c_at, :, lane : lane + 2 * X].astype(F32)
            sg[j + 1, :, lane : lane + 2 * X] = (slope * part).astype(BF16)
        return carry

    lax.fori_loop(0, plan.planes, second_section, 0)

    grad_two = None
    for i in range(Z):
        w, j = own + i, own + i - first_sg
        for y in range(Y):
            mid = sg[j + 1, :, (y + 1) * X : (y + 2) * X]
            wide = mid.astype(F32)
            at = slice(y * X, (y + 1) * X)
            sgx[0:c_two, at] = shift(wide, -1, X).astype(BF16)
            sgx[c_two : 2 * c_two, at] = mid
            sgx[2 * c_two : 3 * c_two, at] = shift(wide, 1, X).astype(BF16)
        term = lax.dot_general(
            around(act, w, 2 * X, Y * X, 1),
            sgx[...],
            (((1,), (1,)), ((), ())),
            preferred_element_type=F32,
        )
        grad_two = term if grad_two is None else grad_two + term
    nine = 9 * c_one
    total[0:nine] = grad_two[:, : 2 * c_two]
    total[nine : nine + nine // 2] = jnp.concatenate(
        [grad_two[: nine // 2, 2 * c_two :], grad_two[nine // 2 :, 2 * c_two :]], axis=1
    )

    wb = wb_ref[...]
    grad_one = None
    for i in range(Z):
        w, j = own + i, own + i - first_sg
        for q in range(Y // 2):
            lane = 2 * q * X
            taps = jnp.dot(wb, around(sg, j, lane + X, 2 * X, -1), preferred_element_type=F32)
            grad = (
                taps[c_one : 2 * c_one]
                + shift(taps[:c_one], -1, X)
                + shift(taps[2 * c_one :], 1, X)
            ).astype(BF16)
            back[i, :, lane : lane + 2 * X] = grad
            grad = grad.astype(F32) * 0.125
            for g in range(8):
                t = tan[w, g * c_one : (g + 1) * c_one, lane : lane + 2 * X]
                slope = (LEAK + 1.0) / 2 + ((1.0 - LEAK) / 2) * t
                first[g * c_one : (g + 1) * c_one, lane : lane + 2 * X] = (slope * grad).astype(BF16)
        row0 = pl.multiple_of(w * 16 * quarter, 8 * quarter)
        term = lax.dot_general(
            fine[pl.ds(row0, 32 * quarter), 2 * X : (2 + Y) * X],
            first[...],
            (((1,), (1,)), ((), ())),
            preferred_element_type=F32,
        )
        grad_one = term if grad_one is None else grad_one + term
    half = 4 * c_one
    third = 8 * quarter
    folded = grad_one[: 3 * third, :half] + grad_one[third:, half:]
    at = nine + nine // 2
    low = lax.broadcasted_iota(jnp.int32, (quarter, half), 1) < half // 2
    place = {1: 0, 2: 1, 3: 2, 0: 3}

    def piece(dz, s, fy):
        row = dz * third + (s * 4 + place[fy]) * quarter
        return folded[row : row + quarter]

    for dz in range(3):
        for dy in range(3):
            left = piece(dz, 0, dy) + pltpu.roll(piece(dz, 0, dy + 1), half // 2, 1)
            right = pltpu.roll(piece(dz, 1, dy), half // 2, 1) + piece(dz, 1, dy + 1)
            total[at : at + quarter] = jnp.where(low, left, right)
            at += quarter
    if at < total.shape[0]:
        total[at:] = jnp.zeros((total.shape[0] - at, total.shape[1]), F32)
    rows = total.shape[0] // 2
    keep_ref[...] = total[pl.ds(pl.multiple_of(me * rows, rows), rows)]
    give_ref[...] = total[pl.ds(pl.multiple_of((1 - me) * rows, rows), rows)]

    for i in range(Z):
        lines = [act[own + i + 1, :, (2 + y) * X : (3 + y) * X] for y in range(Y)]
        lines = jnp.stack([line.astype(F32) for line in lines])
        out_ref[0, :, i] = jnp.swapaxes(lines, 0, 1).astype(BF16)
        lines = [back[i, :, y * X : (y + 1) * X] for y in range(Y)]
        lines = jnp.stack([line.astype(F32) for line in lines])
        out_ref[1, :, i] = jnp.swapaxes(lines, 0, 1).astype(BF16)


def join_kernel(own_ref, other_ref, act_ref, back_ref):
    me = lax.axis_index("pipe")
    act_ref[me] = own_ref[0]
    act_ref[1 - me] = other_ref[0]
    back_ref[me] = own_ref[1]
    back_ref[1 - me] = other_ref[1]


def unpack_kernel(plan, batch, own_ref, other_ref, one_ref, two_ref, full):
    c_in, c_one, c_two = plan.c_in, plan.c_one, plan.c_two
    me = lax.axis_index("pipe")
    rows = own_ref.shape[0]
    full[pl.ds(pl.multiple_of(me * rows, rows), rows)] = own_ref[...] * (1.0 / batch)
    full[pl.ds(pl.multiple_of((1 - me) * rows, rows), rows)] = other_ref[...] * (1.0 / batch)
    nine = 9 * c_one
    for zy in range(9):
        block = full[zy * c_one : (zy + 1) * c_one]
        two_ref[zy * 3] = block[:, :c_two]
        two_ref[zy * 3 + 1] = block[:, c_two:]
    part = c_one // 2
    for p in range(18):
        at = nine + (p % 9) * part
        lane = (p // 9) * c_two
        two_ref[(p // 2) * 3 + 2, (p % 2) * part : (p % 2 + 1) * part] = full[
            at : at + part, lane : lane + c_two
        ]
    for zy in range(9):
        at = nine + nine // 2 + zy * 2 * c_in
        block = full[at : at + 2 * c_in]
        mid, side = block[:, : 2 * c_one], block[:, 2 * c_one :]
        up, down = slice(0, c_in), slice(c_in, 2 * c_in)
        left, right = slice(0, c_one), slice(c_one, 2 * c_one)
        one_ref[zy * 3] = side[down, left] + mid[up, right]
        one_ref[zy * 3 + 1] = mid[up, left] + mid[down, right]
        one_ref[zy * 3 + 2] = mid[down, left] + side[up, right]


def vmem(count):
    return [pl.BlockSpec(memory_space=pltpu.VMEM)] * count


def shape(dims, dtype):
    return jax.ShapeDtypeStruct(dims, dtype)


def per_device(volumes, conv_one, conv_two, cotangent):
    plan = Plan(volumes, cotangent, conv_one, conv_two)
    X, Y, Z = plan.x, plan.y, plan.z
    c_in, c_one, c_two = plan.c_in, plan.c_one, plan.c_two
    keys = sorted({message_key(plan, k) for k in plan.kinds}, key=str)
    sent = pl.pallas_call(
        functools.partial(pack_kernel, plan, keys),
        out_shape=[shape((plan.rows(k), X), BF16) for k in keys],
        in_specs=vmem(2),
        out_specs=vmem(len(keys)),
        scratch_shapes=[
            pltpu.VMEM((Z, Y, plan.fold, X), BF16),
            pltpu.VMEM((plan.cz, plan.cy // 2, c_two, X), BF16),
        ],
        compiler_params=PARAMS,
        name="pack",
    )(volumes, cotangent)
    sent = dict(zip(keys, sent))
    msgs = []
    for kind in plan.kinds:
        cells = sent[message_key(plan, kind)]
        if kind != (None, None):
            z_pairs = None if kind[0] is None else pairs(plan.gz, kind[0])
            y_pairs = None if kind[1] is None else pairs(plan.gy, kind[1])
            cells = swap(cells, plan.gz, plan.gy, z_pairs, y_pairs)
        msgs.append(cells)

    w1, w2, wb = pl.pallas_call(
        functools.partial(weight_kernel, plan),
        out_shape=[
            shape((8 * c_one, 64 * c_in), BF16),
            shape((3 * c_two, 9 * c_one), BF16),
            shape((3 * c_one, 9 * c_two), BF16),
        ],
        in_specs=vmem(2),
        out_specs=vmem(3),
        compiler_params=PARAMS,
        cost_estimate=pl.CostEstimate(flops=10**7, bytes_accessed=10**6, transcendentals=0),
        name="weights",
    )(
        conv_one.transpose(2, 3, 4, 1, 0).reshape(27, c_in, c_one),
        conv_two.transpose(2, 3, 4, 1, 0).reshape(27, c_one, c_two),
    )

    used = 9 * c_one + 9 * c_one // 2 + 9 * 2 * c_in
    half_rows = -(-used // 32) * 16
    wide = 2 * c_two
    out, keep, give = pl.pallas_call(
        functools.partial(main_kernel, plan, len(msgs)),
        out_shape=[
            shape((2, c_one, Z, Y, X), BF16),
            shape((half_rows, wide), F32),
            shape((half_rows, wide), F32),
        ],
        in_specs=vmem(len(msgs) + 3),
        out_specs=vmem(3),
        scratch_shapes=[
            pltpu.VMEM((plan.win, plan.wide, plan.fold, X), BF16),
            pltpu.VMEM(((plan.win + 1) * 32 * c_in, plan.mid * X), BF16),
            pltpu.VMEM((plan.win + 2, c_one, plan.mid * X), BF16),
            pltpu.VMEM((plan.planes + 2, c_two, plan.slim * X), BF16),
            pltpu.VMEM((plan.cz + 2, c_two, plan.slim * X), BF16),
            pltpu.VMEM((plan.win, 8 * c_one, Y * X), F32),
            pltpu.VMEM((Z, c_one, Y * X), BF16),
            pltpu.VMEM((8 * c_one, Y * X), BF16),
            pltpu.VMEM((3 * c_two, Y * X), BF16),
            pltpu.VMEM((2 * half_rows, wide), F32),
        ],
        compiler_params=PARAMS,
        name="sections",
    )(*msgs, w1, w2, wb)

    both = pairs(lax.axis_size("pipe"), 0)
    other = lax.ppermute(out, "pipe", both)
    part = keep + lax.ppermute(give, "pipe", both)
    for axis in ("dp", "gz", "gy"):
        step = 1
        while step < lax.axis_size(axis):
            perm = [(i, i ^ step) for i in range(lax.axis_size(axis))]
            part = part + lax.ppermute(part, axis, perm)
            step *= 2
    rest = lax.ppermute(part, "pipe", both)
    size = (2, c_one, Z, Y, X)
    all_act, all_back = pl.pallas_call(
        join_kernel,
        out_shape=[shape(size, BF16)] * 2,
        in_specs=vmem(2),
        out_specs=vmem(2),
        compiler_params=PARAMS,
        name="join",
    )(out, other)
    grad_one, grad_two = pl.pallas_call(
        functools.partial(unpack_kernel, plan, volumes.shape[0] * lax.axis_size("dp")),
        out_shape=[shape((27, c_in, c_one), F32), shape((27, c_one, c_two), F32)],
        in_specs=vmem(2),
        out_specs=vmem(2),
        scratch_shapes=[pltpu.VMEM((2 * half_rows, wide), F32)],
        compiler_params=PARAMS,
        name="unpack",
    )(part, rest)
    grad_one = grad_one.reshape(3, 3, 3, c_in, c_one).transpose(4, 3, 0, 1, 2)
    grad_two = grad_two.reshape(3, 3, 3, c_one, c_two).transpose(4, 3, 0, 1, 2)
    return all_act, all_back, grad_one, grad_two


def solution(mesh):
    in_specs = (P("dp", None, "gz", "gy", None), P(), P(), P("dp", None, "gz", "gy", None))
    out_specs = (P("dp", None, "gz", "gy", None), P("dp", None, "gz", "gy", None), P(), P())
    return jax.shard_map(
        per_device, mesh=mesh, in_specs=in_specs, out_specs=out_specs, check_vma=False
    )
```

profile of v0, /device:TPU:0, one launch (start us, length us, event | category | flops | bytes accessed | tf_op | source)
XLA Modules:
  0.0 49.8 jit_solution(14984977148500127195)
XLA Ops:
  0.6 0.0 copy-start
  0.6 0.9 %copy-done = bf16[2,32,2,8,128]{4,3,2,1,0:T(8,128)(2,1)S(1)} copy-done((bf16[2,32,2,8,128]{4,3,2,1,0:T(8,128)(2,1)S(1)}, bf16[2,32,2,8,128]{4,3,2,1,0:T(8,128)(2,1)}, u32[]{:S(2)}) %copy-start) | copy-done | bytes 262168
  1.6 0.9 %copy-done.2 = bf16[2,64,1,4,64]{4,3,2,1,0:T(4,128)(2,1)S(1)} copy-done((bf16[2,64,1,4,64]{4,3,2,1,0:T(4,128)(2,1)S(1)}, bf16[2,64,1,4,64]{4,3,2,1,0:T(4,128)(2,1)}, u32[]{:S(2)}) %copy-start.2) | copy-done | bytes 65560
  2.5 0.1 pack.1
  2.6 3.0 %collective-permute-start.2 = (bf16[640,128]{1,0:T(8,128)(2,1)S(1)}, bf16[640,128]{1,0:T(8,128)(2,1)S(1)}, u32[]{:S(2)}, u32[]{:S(2)}) collective-permute-start(bf16[640,128]{1,0:T(8,128)(2,1)S(1)} %get-tuple-element.17.refs_0_), channel_id=1, source_target_pairs={{0,4},{1,5},{2,6},{3,7},{4,0},{5,1},{6,2},{7,3},{8,12},{9,13},{10,... | collective-permute-start | bytes 491528 | tf_op jit(solution)/shard_map/ppermute | solution.py:28
  5.6 1.6 %collective-permute-start = (bf16[256,128]{1,0:T(8,128)(2,1)S(1)}, bf16[256,128]{1,0:T(8,128)(2,1)S(1)}, u32[]{:S(2)}, u32[]{:S(2)}) collective-permute-start(bf16[256,128]{1,0:T(8,128)(2,1)S(1)} %get-tuple-element.18), channel_id=1, source_target_pairs={{0,1},{1,0},{2,3},{3,2},{4,5},{5,4},{6,7},{7,6},{8,9},{9,8},{10,11... | collective-permute-start | bytes 196616 | tf_op jit(solution)/shard_map/ppermute | solution.py:28
  7.2 0.7 %collective-permute-start.1 = (bf16[256,128]{1,0:T(8,128)(2,1)S(1)}, bf16[256,128]{1,0:T(8,128)(2,1)S(1)}, u32[]{:S(2)}, u32[]{:S(2)}) collective-permute-start(bf16[256,128]{1,0:T(8,128)(2,1)S(1)} %get-tuple-element.19), channel_id=1, source_target_pairs={{1,2},{2,1},{5,6},{6,5},{9,10},{10,9},{13,14},{14,13},{17,18},{18,... | collective-permute-start | bytes 196616 | tf_op jit(solution)/shard_map/ppermute | solution.py:28
  7.9 4.4 %collective-permute-start.3 = (bf16[256,128]{1,0:T(8,128)(2,1)S(1)}, bf16[256,128]{1,0:T(8,128)(2,1)S(1)}, u32[]{:S(2)}, u32[]{:S(2)}) collective-permute-start(bf16[256,128]{1,0:T(8,128)(2,1)S(1)} %get-tuple-element.18), channel_id=1, source_target_pairs={{0,5},{1,4},{2,7},{3,6},{4,1},{5,0},{6,3},{7,2},{8,13},{9,12},{10,... | collective-permute-start | bytes 196616 | tf_op jit(solution)/shard_map/ppermute | solution.py:28
  12.3 0.7 %collective-permute-start.4 = (bf16[256,128]{1,0:T(8,128)(2,1)S(1)}, bf16[256,128]{1,0:T(8,128)(2,1)S(1)}, u32[]{:S(2)}, u32[]{:S(2)}) collective-permute-start(bf16[256,128]{1,0:T(8,128)(2,1)S(1)} %get-tuple-element.19), channel_id=1, source_target_pairs={{1,6},{2,5},{5,2},{6,1},{9,14},{10,13},{13,10},{14,9},{17,22},{18,... | collective-permute-start | bytes 196616 | tf_op jit(solution)/shard_map/ppermute | solution.py:28
  13.0 0.3 weights.1
  13.3 0.0 collective-permute-done.refs_1_
  13.3 0.0 collective-permute-done.1.refs_2_
  13.4 1.2 %collective-permute-done.3.refs_4_ = bf16[256,128]{1,0:T(8,128)(2,1)S(1)} collective-permute-done((bf16[256,128]{1,0:T(8,128)(2,1)S(1)}, bf16[256,128]{1,0:T(8,128)(2,1)S(1)}, u32[]{:S(2)}, u32[]{:S(2)}) %collective-permute-start.3) | collective-permute-done | bytes 65568 | tf_op jit(solution)/shard_map/ppermute | solution.py:28
  14.5 0.0 collective-permute-done.4.refs_5_
  14.5 0.0 collective-permute-done.2.refs_3_
  14.6 6.6 %sections.1 = (bf16[2,32,2,8,128]{4,3,2,1,0:T(8,128)(2,1)S(1)}, f32[256,128]{1,0:T(8,128)S(1)}, f32[256,128]{1,0:T(8,128)S(1)}) custom-call(bf16[640,128]{1,0:T(8,128)(2,1)S(1)} %get-tuple-element.17.refs_0_, bf16[256,128]{1,0:T(8,128)(2,1)S(1)} %collective-permute-done.refs_1_, bf16[256,128]{1,0:T(8,128)(2,1)S(1)} %collective-permute-done.1.refs_2_, ...), custom_call_target="tpu_custom_call" | custom-call | tf_op jit(solution)/shard_map/sections/pallas_call | solution.py:469
  21.1 0.1 collective-permute-start.6
  21.2 1.3 %collective-permute-done.6 = f32[256,128]{1,0:T(8,128)S(1)} collective-permute-done((f32[256,128]{1,0:T(8,128)S(1)}, f32[256,128]{1,0:T(8,128)S(1)}, u32[]{:S(2)}, u32[]{:S(2)}) %collective-permute-start.6) | collective-permute-done | bytes 131104 | tf_op jit(solution)/shard_map/ppermute | solution.py:496
  22.5 1.6 %collective-permute-start.7 = (f32[256,128]{1,0:T(8,128)S(1)}, f32[256,128]{1,0:T(8,128)S(1)}, u32[]{:S(2)}, u32[]{:S(2)}) collective-permute-start(f32[256,128]{1,0:T(8,128)S(1)} %add.15), channel_id=1, source_target_pairs={{0,16},{16,0},{1,17},{17,1},{2,18},{18,2},{3,19},{19,3},{4,20},{20... | collective-permute-start | bytes 393224 | tf_op jit(solution)/shard_map/ppermute | solution.py:501
  24.1 4.0 %collective-permute-done.7 = f32[256,128]{1,0:T(8,128)S(1)} collective-permute-done((f32[256,128]{1,0:T(8,128)S(1)}, f32[256,128]{1,0:T(8,128)S(1)}, u32[]{:S(2)}, u32[]{:S(2)}) %collective-permute-start.7) | collective-permute-done | bytes 131104 | tf_op jit(solution)/shard_map/ppermute | solution.py:501
  28.2 1.6 %collective-permute-start.8 = (f32[256,128]{1,0:T(8,128)S(1)}, f32[256,128]{1,0:T(8,128)S(1)}, u32[]{:S(2)}, u32[]{:S(2)}) collective-permute-start(f32[256,128]{1,0:T(8,128)S(1)} %add.16), channel_id=1, source_target_pairs={{0,4},{4,0},{1,5},{5,1},{2,6},{6,2},{3,7},{7,3},{8,12},{12,8},{9,1... | collective-permute-start | bytes 393224 | tf_op jit(solution)/shard_map/ppermute | solution.py:501
  29.7 3.5 %collective-permute-done.8 = f32[256,128]{1,0:T(8,128)S(1)} collective-permute-done((f32[256,128]{1,0:T(8,128)S(1)}, f32[256,128]{1,0:T(8,128)S(1)}, u32[]{:S(2)}, u32[]{:S(2)}) %collective-permute-start.8) | collective-permute-done | bytes 131104 | tf_op jit(solution)/shard_map/ppermute | solution.py:501
  33.2 4.9 %collective-permute-start.9 = (f32[256,128]{1,0:T(8,128)S(1)}, f32[256,128]{1,0:T(8,128)S(1)}, u32[]{:S(2)}, u32[]{:S(2)}) collective-permute-start(f32[256,128]{1,0:T(8,128)S(1)} %add.17), channel_id=1, source_target_pairs={{0,1},{1,0},{2,3},{3,2},{4,5},{5,4},{6,7},{7,6},{8,9},{9,8},{10,11... | collective-permute-start | bytes 393224 | tf_op jit(solution)/shard_map/ppermute | solution.py:501
  38.1 0.0 collective-permute-start.5
  38.1 3.4 %collective-permute-done.9 = f32[256,128]{1,0:T(8,128)S(1)} collective-permute-done((f32[256,128]{1,0:T(8,128)S(1)}, f32[256,128]{1,0:T(8,128)S(1)}, u32[]{:S(2)}, u32[]{:S(2)}) %collective-permute-start.9) | collective-permute-done | bytes 131104 | tf_op jit(solution)/shard_map/ppermute | solution.py:501
  41.5 1.1 %collective-permute-start.10 = (f32[256,128]{1,0:T(8,128)S(1)}, f32[256,128]{1,0:T(8,128)S(1)}, u32[]{:S(2)}, u32[]{:S(2)}) collective-permute-start(f32[256,128]{1,0:T(8,128)S(1)} %add.18), channel_id=1, source_target_pairs={{0,2},{1,3},{2,0},{3,1},{4,6},{5,7},{6,4},{7,5},{8,10},{9,11},{10,... | collective-permute-start | bytes 393224 | tf_op jit(solution)/shard_map/ppermute | solution.py:501
  42.6 4.9 %collective-permute-done.10 = f32[256,128]{1,0:T(8,128)S(1)} collective-permute-done((f32[256,128]{1,0:T(8,128)S(1)}, f32[256,128]{1,0:T(8,128)S(1)}, u32[]{:S(2)}, u32[]{:S(2)}) %collective-permute-start.10) | collective-permute-done | bytes 131104 | tf_op jit(solution)/shard_map/ppermute | solution.py:501
  47.5 0.1 collective-permute-start.11
  47.6 0.0 collective-permute-done.5.other_ref
  47.6 0.8 %join.1 = (bf16[2,32,2,8,128]{4,3,2,1,0:T(8,128)(2,1)}, bf16[2,32,2,8,128]{4,3,2,1,0:T(8,128)(2,1)}) custom-call(bf16[2,32,2,8,128]{4,3,2,1,0:T(8,128)(2,1)S(1)} %get-tuple-element.23.own_ref, bf16[2,32,2,8,128]{4,3,2,1,0:T(8,128)(2,1)S(1)} %collective-permute-done.5.other_ref), custom_call_target="tpu_custom_call" | custom-call | tf_op jit(solution)/shard_map/join/pallas_call | solution.py:505
  48.4 0.5 collective-permute-done.11.other_ref
  48.9 0.9 %unpack.1 = (f32[27,4,32]{2,1,0:T(4,128)}, f32[27,32,64]{2,1,0:T(8,128)}) custom-call(f32[256,128]{1,0:T(8,128)S(1)} %add.19.own_ref, f32[256,128]{1,0:T(8,128)S(1)} %collective-permute-done.11.other_ref), custom_call_target="tpu_custom_call" | custom-call | tf_op jit(solution)/shard_map/unpack/pallas_call | solution.py:513
  (10 shorter events, 0.1 us)
Async XLA Ops:
  0.6 1.0 %copy-start = (bf16[2,32,2,8,128]{4,3,2,1,0:T(8,128)(2,1)S(1)}, bf16[2,32,2,8,128]{4,3,2,1,0:T(8,128)(2,1)}, u32[]{:S(2)}) copy-start(bf16[2,32,2,8,128]{4,3,2,1,0:T(8,128)(2,1)} %vol_ref.1) | copy-start | bytes 786436
  1.6 0.9 %copy-start.2 = (bf16[2,64,1,4,64]{4,3,2,1,0:T(4,128)(2,1)S(1)}, bf16[2,64,1,4,64]{4,3,2,1,0:T(4,128)(2,1)}, u32[]{:S(2)}) copy-start(bf16[2,64,1,4,64]{4,3,2,1,0:T(4,128)(2,1)} %cot_ref.1) | copy-start | bytes 196612
  2.5 10.5 %copy-start.1 = (bf16[64,32,3,3,3]{0,1,4,3,2:T(8,128)(2,1)S(1)}, bf16[64,32,3,3,3]{0,1,4,3,2:T(8,128)(2,1)}, u32[]{:S(2)}) copy-start(bf16[64,32,3,3,3]{0,1,4,3,2:T(8,128)(2,1)} %param.6) | copy-start | bytes 331780
  2.5 10.5 %copy-start.3 = (bf16[32,4,3,3,3]{0,1,4,3,2:T(4,128)(2,1)S(1)}, bf16[32,4,3,3,3]{0,1,4,3,2:T(4,128)(2,1)}, u32[]{:S(2)}) copy-start(bf16[32,4,3,3,3]{0,1,4,3,2:T(4,128)(2,1)} %param.5) | copy-start | bytes 20740
  2.6 11.9 %collective-permute-start.2 = (bf16[640,128]{1,0:T(8,128)(2,1)S(1)}, bf16[640,128]{1,0:T(8,128)(2,1)S(1)}, u32[]{:S(2)}, u32[]{:S(2)}) collective-permute-start(bf16[640,128]{1,0:T(8,128)(2,1)S(1)} %get-tuple-element.17.refs_0_), channel_id=1, source_target_pairs={{0,4},{1,5},{2,6},{3,7},{4,0},{5,1},{6,2},{7,3},{8,12},{9,13},{10,... | collective-permute-start | bytes 491528 | tf_op jit(solution)/shard_map/ppermute | solution.py:28
  5.6 7.7 %collective-permute-start = (bf16[256,128]{1,0:T(8,128)(2,1)S(1)}, bf16[256,128]{1,0:T(8,128)(2,1)S(1)}, u32[]{:S(2)}, u32[]{:S(2)}) collective-permute-start(bf16[256,128]{1,0:T(8,128)(2,1)S(1)} %get-tuple-element.18), channel_id=1, source_target_pairs={{0,1},{1,0},{2,3},{3,2},{4,5},{5,4},{6,7},{7,6},{8,9},{9,8},{10,11... | collective-permute-start | bytes 196616 | tf_op jit(solution)/shard_map/ppermute | solution.py:28
  7.2 6.1 %collective-permute-start.1 = (bf16[256,128]{1,0:T(8,128)(2,1)S(1)}, bf16[256,128]{1,0:T(8,128)(2,1)S(1)}, u32[]{:S(2)}, u32[]{:S(2)}) collective-permute-start(bf16[256,128]{1,0:T(8,128)(2,1)S(1)} %get-tuple-element.19), channel_id=1, source_target_pairs={{1,2},{2,1},{5,6},{6,5},{9,10},{10,9},{13,14},{14,13},{17,18},{18,... | collective-permute-start | bytes 196616 | tf_op jit(solution)/shard_map/ppermute | solution.py:28
  7.9 6.7 %collective-permute-start.3 = (bf16[256,128]{1,0:T(8,128)(2,1)S(1)}, bf16[256,128]{1,0:T(8,128)(2,1)S(1)}, u32[]{:S(2)}, u32[]{:S(2)}) collective-permute-start(bf16[256,128]{1,0:T(8,128)(2,1)S(1)} %get-tuple-element.18), channel_id=1, source_target_pairs={{0,5},{1,4},{2,7},{3,6},{4,1},{5,0},{6,3},{7,2},{8,13},{9,12},{10,... | collective-permute-start | bytes 196616 | tf_op jit(solution)/shard_map/ppermute | solution.py:28
  12.3 2.2 %collective-permute-start.4 = (bf16[256,128]{1,0:T(8,128)(2,1)S(1)}, bf16[256,128]{1,0:T(8,128)(2,1)S(1)}, u32[]{:S(2)}, u32[]{:S(2)}) collective-permute-start(bf16[256,128]{1,0:T(8,128)(2,1)S(1)} %get-tuple-element.19), channel_id=1, source_target_pairs={{1,6},{2,5},{5,2},{6,1},{9,14},{10,13},{13,10},{14,9},{17,22},{18,... | collective-permute-start | bytes 196616 | tf_op jit(solution)/shard_map/ppermute | solution.py:28
  21.1 1.4 %collective-permute-start.6 = (f32[256,128]{1,0:T(8,128)S(1)}, f32[256,128]{1,0:T(8,128)S(1)}, u32[]{:S(2)}, u32[]{:S(2)}) collective-permute-start(f32[256,128]{1,0:T(8,128)S(1)} %get-tuple-element.27), channel_id=1, source_target_pairs={{0,8},{8,0},{1,9},{9,1},{2,10},{10,2},{3,11},{11,3},{4,12},{12,4},... | collective-permute-start | bytes 393224 | tf_op jit(solution)/shard_map/ppermute | solution.py:496
  22.5 5.6 %collective-permute-start.7 = (f32[256,128]{1,0:T(8,128)S(1)}, f32[256,128]{1,0:T(8,128)S(1)}, u32[]{:S(2)}, u32[]{:S(2)}) collective-permute-start(f32[256,128]{1,0:T(8,128)S(1)} %add.15), channel_id=1, source_target_pairs={{0,16},{16,0},{1,17},{17,1},{2,18},{18,2},{3,19},{19,3},{4,20},{20... | collective-permute-start | bytes 393224 | tf_op jit(solution)/shard_map/ppermute | solution.py:501
  28.2 5.0 %collective-permute-start.8 = (f32[256,128]{1,0:T(8,128)S(1)}, f32[256,128]{1,0:T(8,128)S(1)}, u32[]{:S(2)}, u32[]{:S(2)}) collective-permute-start(f32[256,128]{1,0:T(8,128)S(1)} %add.16), channel_id=1, source_target_pairs={{0,4},{4,0},{1,5},{5,1},{2,6},{6,2},{3,7},{7,3},{8,12},{12,8},{9,1... | collective-permute-start | bytes 393224 | tf_op jit(solution)/shard_map/ppermute | solution.py:501
  33.2 8.3 %collective-permute-start.9 = (f32[256,128]{1,0:T(8,128)S(1)}, f32[256,128]{1,0:T(8,128)S(1)}, u32[]{:S(2)}, u32[]{:S(2)}) collective-permute-start(f32[256,128]{1,0:T(8,128)S(1)} %add.17), channel_id=1, source_target_pairs={{0,1},{1,0},{2,3},{3,2},{4,5},{5,4},{6,7},{7,6},{8,9},{9,8},{10,11... | collective-permute-start | bytes 393224 | tf_op jit(solution)/shard_map/ppermute | solution.py:501
  38.1 9.5 %collective-permute-start.5 = (bf16[2,32,2,8,128]{4,3,2,1,0:T(8,128)(2,1)S(1)}, bf16[2,32,2,8,128]{4,3,2,1,0:T(8,128)(2,1)S(1)}, u32[]{:S(2)}, u32[]{:S(2)}) collective-permute-start(bf16[2,32,2,8,128]{4,3,2,1,0:T(8,128)(2,1)S(1)} %get-tuple-element.23.own_ref), channel_id=1, source_target_pairs={{0,8},{8,0},{1,9},{9,1},{2,10},{10,2},{3,11},{11,3},{4,12},{12,4},... | collective-permute-start | bytes 786440 | tf_op jit(solution)/shard_map/ppermute | solution.py:495
  41.5 5.9 %collective-permute-start.10 = (f32[256,128]{1,0:T(8,128)S(1)}, f32[256,128]{1,0:T(8,128)S(1)}, u32[]{:S(2)}, u32[]{:S(2)}) collective-permute-start(f32[256,128]{1,0:T(8,128)S(1)} %add.18), channel_id=1, source_target_pairs={{0,2},{1,3},{2,0},{3,1},{4,6},{5,7},{6,4},{7,5},{8,10},{9,11},{10,... | collective-permute-start | bytes 393224 | tf_op jit(solution)/shard_map/ppermute | solution.py:501
  47.5 1.4 %collective-permute-start.11 = (f32[256,128]{1,0:T(8,128)S(1)}, f32[256,128]{1,0:T(8,128)S(1)}, u32[]{:S(2)}, u32[]{:S(2)}) collective-permute-start(f32[256,128]{1,0:T(8,128)S(1)} %add.19.own_ref), channel_id=1, source_target_pairs={{0,8},{8,0},{1,9},{9,1},{2,10},{10,2},{3,11},{11,3},{4,12},{12,4},... | collective-permute-start | bytes 393224 | tf_op jit(solution)/shard_map/ppermute | solution.py:503
where the time goes:
time: 50 us; the launch traced here: 49.8 us
  starting transfers between devices  19.6 us (39%)
  waiting for transfers between devices  18.8 us (38%)
  Pallas kernels  8.82 us (18%)
  local copies, waits for them, and re-layouts  1.85 us (4%)
  between operations  0.75 us (2%)
    ppermute x4, waiting for transfers between devices, per_device(): part = part + lax.ppermute(part, axis, perm)  15.7 us
    ppermute x5, starting transfers between devices, swap(): return lax.ppermute(cells, ('gz', 'gy'), perm)  10.3 us
    ppermute x4, starting transfers between devices, per_device(): part = part + lax.ppermute(part, axis, perm)  9.12 us
    pallas_call x1, Pallas kernels, per_device(): pl.pallas_call(functools.partial(main_kernel, plan, len(msgs)), out_shape...  6.56 us
    unnamed x8, local copies, waits for them, and re-layouts  1.85 us
    ppermute x1, waiting for transfers between devices, per_device(): part = keep + lax.ppermute(give, 'pipe', both)  1.33 us
    ppermute x5, waiting for transfers between devices, swap(): return lax.ppermute(cells, ('gz', 'gy'), perm)  1.2 us
  transfers between devices with their start and end apart: 12, of which 7 were waited for; matrix products, arithmetic and copies ran while one was open for 0% of the time, Pallas kernels for 2%

commit v1 on v0

v1 whole, which is shorter than its diff:
```python
import functools

import jax
import jax.numpy as jnp
from jax import lax
from jax.experimental import pallas as pl
from jax.experimental.pallas import tpu as pltpu
from jax.sharding import PartitionSpec as P

LEAK = 0.3
REACH = 3
AXES = ("dp", "pipe", "gz", "gy")
F32 = jnp.float32
BF16 = jnp.bfloat16
PARAMS = pltpu.CompilerParams(vmem_limit_bytes=48 * 1024 * 1024)


def pairs(count, odd):
    out = []
    for i in range(odd, count - 1, 2):
        out += [(i, i + 1), (i + 1, i)]
    return out


def swap(cells, plan, kind):
    z_kind, y_kind = kind
    if plan.split:
        perm = []
        for d in range(plan.dp):
            for p in range(2):
                for a in range(plan.gz):
                    for c in range(plan.gy):
                        to = [d, p, a if z_kind is None else 1 - a, c]
                        if y_kind is not None:
                            near = c + 2 * p - 1
                            if 0 <= near < plan.gy:
                                to[1], to[3] = 1 - p, near
                            else:
                                to = [d ^ 1 if d ^ 1 < plan.dp else d, p, a, c]
                        perm.append((plan.index(d, p, a, c), plan.index(*to)))
        return lax.ppermute(cells, AXES, perm)
    z_list = [(i, i) for i in range(plan.gz)] if z_kind is None else pairs(plan.gz, z_kind)
    y_list = [(i, i) for i in range(plan.gy)] if y_kind is None else pairs(plan.gy, y_kind)
    perm = [(a * plan.gy + c, b * plan.gy + d) for a, b in z_list for c, d in y_list]
    return lax.ppermute(cells, ("gz", "gy"), perm)


def shift(block, step, width):
    parts = []
    for at in range(0, block.shape[1], width):
        part = block[:, at : at + width]
        lane = lax.broadcasted_iota(jnp.int32, part.shape, 1)
        edge = 0 if step > 0 else width - 1
        parts.append(jnp.where(lane == edge, 0.0, pltpu.roll(part, step % width, 1)))
    return parts[0] if len(parts) == 1 else jnp.concatenate(parts, axis=1)


class Plan:
    def __init__(self, volumes, cotangent, conv_one, conv_two):
        count, self.fold, self.z, self.y, self.x = volumes.shape
        self.c_one, self.c_in = conv_one.shape[:2]
        self.c_two = conv_two.shape[0]
        self.cz, self.cy = cotangent.shape[2:4]
        self.dp, self.pipe = lax.axis_size("dp"), lax.axis_size("pipe")
        self.gz, self.gy = lax.axis_size("gz"), lax.axis_size("gy")
        self.batch = count * self.dp
        self.split = count == self.gz == self.pipe == 2 and self.y % 4 == 0 and self.y >= 2 * REACH
        self.h = min(REACH, self.z)
        sides = min(self.gz - 1, 2)
        if self.split:
            self.r, self.o = self.y // 2, 2 * self.z
            self.win = self.planes = self.o
            self.cot_planes = 2 * self.cz + 2
            self.kinds = [(None, None), (0, 0), (None, 0), (0, None)]
        else:
            self.r, self.o = self.y, self.z
            self.win = self.z + sides * self.h
            self.planes = self.z + sides
            self.cot_planes = self.cz + 2
            z_kinds = [None] + [k for k in (0, 1) if len(pairs(self.gz, k)) > 0]
            y_kinds = [None] + [k for k in (0, 1) if len(pairs(self.gy, k)) > 0]
            self.kinds = [(a, b) for a in z_kinds for b in y_kinds]
        self.wide = self.r + 2 * REACH
        self.mid = self.r + 4
        self.slim = self.r + 2

    def index(self, d, p, a, c):
        return ((d * self.pipe + p) * self.gz + a) * self.gy + c

    def at_z(self):
        if self.split or self.gz == 1:
            return 0, 0
        if self.gz > 2:
            return self.h, self.h - 1
        me = lax.axis_index("gz")
        return me * self.h, me * (self.h - 1)

    def row0(self):
        return lax.axis_index("pipe") * self.r if self.split else 0

    def blocks(self, kind):
        z_kind, y_kind = kind
        nz, nc = (self.z, self.cz) if z_kind is None or self.split else (self.h, 1)
        ny, np_ = (self.y, self.cy // 2) if y_kind is None else (REACH, 1)
        return nz, ny, nc, np_

    def rows(self, kind):
        nz, ny, nc, np_ = self.blocks(kind)
        return nz * ny * self.fold + nc * np_ * self.c_two


def message_key(plan, kind):
    z_kind, y_kind = kind
    if not plan.split and z_kind is not None and plan.h == plan.z and plan.cz == 1:
        z_kind = None
    return z_kind, y_kind


def pack_kernel(plan, keys, vol_hbm, cot_hbm, *refs):
    out_refs, (vol_ref, cot_ref, cells, cots, sems) = refs[: len(keys)], refs[len(keys) :]
    count = vol_ref.shape[0]
    me, my_z, my_y = lax.axis_index("pipe"), lax.axis_index("gz"), lax.axis_index("gy")
    first = 0 if plan.split else me
    loads = [
        pltpu.make_async_copy(vol_hbm.at[pl.ds(first, count)], vol_ref, sems.at[0]),
        pltpu.make_async_copy(cot_hbm.at[pl.ds(first, count)], cot_ref, sems.at[1]),
    ]
    for load in loads:
        load.start()
    loads[0].wait()
    for v in range(count):
        for z in range(plan.z):
            block = jnp.swapaxes(vol_ref[v, :, z].astype(F32), 0, 1).astype(BF16)
            for y in range(plan.y):
                cells[v, z, y] = block[y]
    loads[1].wait()
    for v in range(count):
        for z in range(plan.cz):
            block = jnp.swapaxes(cot_ref[v, :, z].astype(F32), 0, 1)
            for m in range(plan.cy // 2):
                pair = jnp.concatenate([block[2 * m], block[2 * m + 1]], axis=1)
                cots[v, z, m] = pair.astype(BF16)
    for key, out_ref in zip(keys, out_refs):
        nz, ny, nc, np_ = plan.blocks(key)
        v = z0 = c0 = y0 = p0 = 0
        if plan.split:
            v = my_z if key[0] is None else 1 - my_z
            y_low = me == 0
        else:
            if key[0] is not None:
                z_low = my_z % 2 == 1 - key[0]
                z0 = jnp.where(z_low, 0, plan.z - nz)
                c0 = jnp.where(z_low, 0, plan.cz - nc)
            if key[1] is not None:
                y_low = my_y % 2 == 1 - key[1]
        if key[1] is not None:
            y0 = jnp.where(y_low, 0, plan.y - ny)
            p0 = jnp.where(y_low, 0, plan.cy // 2 - np_)
        at = 0
        for i in range(nz):
            for j in range(ny):
                out_ref[at : at + plan.fold] = cells[v, z0 + i, y0 + j]
                at += plan.fold
        for i in range(nc):
            for j in range(np_):
                out_ref[at : at + plan.c_two] = cots[v, c0 + i, p0 + j]
                at += plan.c_two


def weight_kernel(plan, one_ref, two_ref, w1_ref, w2_ref, wb_ref):
    c_in, c_one, c_two = plan.c_in, plan.c_one, plan.c_two
    none = jnp.zeros((c_in, c_one), F32)
    pairs_x = {}
    for dz in range(3):
        for dy in range(3):
            tap = [one_ref[(dz * 3 + dy) * 3 + dx].astype(F32) * 0.5 for dx in range(3)]
            pairs_x[dz, dy, 0] = jnp.concatenate(
                [jnp.concatenate([tap[1], tap[0]], 1), jnp.concatenate([tap[2], tap[1]], 1)], 0
            )
            pairs_x[dz, dy, 1] = jnp.concatenate(
                [jnp.concatenate([none, tap[2]], 1), jnp.concatenate([tap[0], none], 1)], 0
            )
    blank = jnp.zeros((2 * c_in, 2 * c_one), F32)
    rows = []
    for fz in range(4):
        for s in range(2):
            for fy in (1, 2, 3, 0):
                rows.append(
                    jnp.concatenate(
                        [
                            pairs_x.get((fz - a, fy - b, s), blank)
                            for a in range(2)
                            for b in range(2)
                        ],
                        axis=1,
                    )
                )
    w1_ref[...] = jnp.concatenate(rows, axis=0).T.astype(BF16)
    for dx in range(3):
        taps = [two_ref[zy * 3 + dx] for zy in range(9)]
        wb_ref[dx * c_one : (dx + 1) * c_one] = jnp.concatenate(taps, axis=1)
        tall = jnp.concatenate([t.astype(F32) * 0.5 for t in taps], axis=0)
        w2_ref[dx * c_two : (dx + 1) * c_two] = tall.T.astype(BF16)


def around(ref, w, lane, size, step, sign):
    return jnp.concatenate(
        [
            ref[w + 1 + sign * dz, :, lane + sign * dy * step : lane + sign * dy * step + size]
            for dz in (-1, 0, 1)
            for dy in (-1, 0, 1)
        ],
        axis=0,
    )


def forward_kernel(plan, count, *refs):
    msgs = refs[:count]
    w1_ref, w2_ref, keep_ref, give_ref, fine, act, sg, tan = refs[count : count + 8]
    cells, cot, sgx, total = refs[count + 8 :]
    X, Y, Z, R = plan.x, plan.y, plan.z, plan.r
    fold, c_in, c_one, c_two = plan.fold, plan.c_in, plan.c_one, plan.c_two
    me, my_z, my_y = lax.axis_index("pipe"), lax.axis_index("gz"), lax.axis_index("gy")
    own, first_sg = plan.at_z()
    row0 = plan.row0()
    low_ok, high_ok = my_y > 0, my_y < plan.gy - 1
    if plan.split:
        low_ok, high_ok = low_ok | (me == 1), high_ok | (me == 0)

    pick = (
        lax.broadcasted_iota(jnp.int32, (X, 2 * X), 1) // 2
        == lax.broadcasted_iota(jnp.int32, (X, 2 * X), 0)
    )
    pick = jnp.where(pick, 0.125, 0.0).astype(BF16)
    if not plan.split:
        cot[...] = jnp.zeros_like(cot)
    for kind, msg in zip(plan.kinds, msgs):
        nz, ny, nc, np_ = plan.blocks(kind)
        z_kind, y_kind = kind
        below, used = None, None
        if plan.split:
            half = my_z if z_kind is None else 1 - my_z
            z0, c0 = half * Z, half * plan.cz + 1
            if y_kind is not None:
                below = me == 0
                used = (below & (my_y > 0)) | ((me == 1) & (my_y < plan.gy - 1))
        else:
            z0, c0 = own, 1
            if z_kind is not None:
                before = my_z % 2 == 1 - z_kind
                z0 = jnp.clip(jnp.where(before, own - plan.h, own + Z), 0, plan.win - plan.h)
                c0 = jnp.where(before, 0, plan.cz + 1)
            if y_kind is not None:
                below = my_y % 2 == 1 - y_kind
        y0 = REACH if y_kind is None else jnp.where(below, 0, Y + REACH)
        at = 0
        for i in range(nz):
            for j in range(ny):
                block = msg[at : at + fold]
                if used is not None:
                    block = jnp.where(used, block, jnp.zeros_like(block))
                cells[z0 + i, y0 + j] = block
                at += fold
        for i in range(nc):
            for j in range(np_):
                up = jnp.dot(msg[at : at + c_two], pick, preferred_element_type=F32)
                if used is not None:
                    up = jnp.where(used, up, 0.0)
                up = up.astype(BF16)
                at += c_two
                one, two = up[:, :X], up[:, X:]
                if y_kind is None:
                    for r, piece in enumerate((one, one, two, two)):
                        lane = (4 * j + r + 2) * X
                        cot[c0 + i, :, lane : lane + X] = piece
                else:
                    piece = jnp.where(below, two, one)
                    lane = pl.multiple_of(jnp.where(below, X, (Y + 2) * X), X)
                    cot[c0 + i, :, pl.ds(lane, X)] = piece

    quarter = 2 * c_in
    fine[0 : 8 * quarter] = jnp.zeros((8 * quarter, plan.mid * X), BF16)
    last = 8 * quarter + plan.win * 16 * quarter
    fine[last : last + 8 * quarter] = jnp.zeros((8 * quarter, plan.mid * X), BF16)
    is_c = (lax.broadcasted_iota(jnp.int32, (fold, X), 0) // c_in) % 2 == 1

    def spread(w, carry):
        base = pl.multiple_of(8 * quarter + w * 16 * quarter, 8 * quarter)
        kept = []
        for r in range(plan.wide):
            mid = cells[w, row0 + r].astype(F32)
            side = jnp.where(is_c, shift(mid, 1, X), shift(mid, -1, X))
            kept.append((mid, side))
            if r < 2:
                continue
            lane = (r - 2) * X
            for a in range(2):
                for s in range(2):
                    lo, here, hi = kept[r - 2][s], kept[r - 1][s], kept[r][s]
                    at = a * 2 * quarter
                    near = here[at : at + 2 * quarter]
                    far = jnp.concatenate(
                        [hi[at : at + quarter], lo[at + quarter : at + 2 * quarter]], axis=0
                    )
                    row = base + (a * 8 + s * 4) * quarter
                    fine[pl.ds(row, 2 * quarter), lane : lane + X] = near.astype(BF16)
                    fine[pl.ds(row + 2 * quarter, 2 * quarter), lane : lane + X] = far.astype(BF16)
        return carry

    lax.fori_loop(0, plan.win, spread, 0)

    w1 = w1_ref[...]
    last_q = plan.mid // 2 - 1
    act[0] = jnp.zeros(act.shape[1:], BF16)
    act[plan.win + 1] = jnp.zeros(act.shape[1:], BF16)

    def first_section(w, carry):
        top = pl.multiple_of(w * 16 * quarter, 8 * quarter)
        z_abs = my_z * Z + w - own
        z_ok = None if plan.split else (z_abs >= 0) & (z_abs < plan.gz * Z)
        for q in range(plan.mid // 2):
            lane = 2 * q * X
            half = jnp.dot(
                w1, fine[pl.ds(top, 32 * quarter), lane : lane + 2 * X], preferred_element_type=F32
            )
            line, prod = None, None
            for g in range(8):
                v = half[g * c_one : (g + 1) * c_one]
                t = jnp.tanh(v)
                if 0 < q < last_q:
                    tan[w, g * c_one : (g + 1) * c_one, lane - 2 * X : lane] = t
                bent = jnp.maximum(v, LEAK * v)
                grown = 1.0 + jnp.abs(t)
                line = bent if line is None else line + bent
                prod = grown if prod is None else prod * grown
            mean = 0.25 * line - ((1.0 - LEAK) / 8.0) * jnp.log(prod)
            for ok in (z_ok, low_ok if q == 0 else None, high_ok if q == last_q else None):
                if ok is not None:
                    mean = jnp.where(ok, mean, 0.0)
            act[w + 1, :, lane : lane + 2 * X] = mean.astype(BF16)
        return carry

    lax.fori_loop(0, plan.win, first_section, 0)

    w2 = w2_ref[...]
    sg[0] = jnp.zeros(sg.shape[1:], BF16)
    sg[plan.planes + 1] = jnp.zeros(sg.shape[1:], BF16)

    def second_section(j, carry):
        w = first_sg + j
        c_at = (w - own + 2) // 2
        for q in range(plan.slim // 2):
            lane = 2 * q * X
            taps = jnp.dot(w2, around(act, w, lane + X, 2 * X, X, 1), preferred_element_type=F32)
            half = (
                taps[c_two : 2 * c_two]
                + shift(taps[:c_two], 1, X)
                + shift(taps[2 * c_two :], -1, X)
            )
            slope = (LEAK + 1.0) / 2 + ((1.0 - LEAK) / 2) * jnp.tanh(half)
            near = pl.multiple_of((row0 + 1) * X + lane, X)
            part = cot[c_at, :, pl.ds(near, 2 * X)].astype(F32)
            sg[j + 1, :, lane : lane + 2 * X] = (slope * part).astype(BF16)
        return carry

    lax.fori_loop(0, plan.planes, second_section, 0)

    grad_two = None
    for i in range(plan.o):
        w, j = own + i, own + i - first_sg
        for y in range(R):
            mid = sg[j + 1, :, (y + 1) * X : (y + 2) * X]
            wide = mid.astype(F32)
            at = slice(y * X, (y + 1) * X)
            sgx[0:c_two, at] = shift(wide, -1, X).astype(BF16)
            sgx[c_two : 2 * c_two, at] = mid
            sgx[2 * c_two : 3 * c_two, at] = shift(wide, 1, X).astype(BF16)
        term = lax.dot_general(
            around(act, w, 2 * X, R * X, X, 1),
            sgx[...],
            (((1,), (1,)), ((), ())),
            preferred_element_type=F32,
        )
        grad_two = term if grad_two is None else grad_two + term
    nine = 9 * c_one
    total[0:nine] = grad_two[:, : 2 * c_two]
    total[nine : nine + nine // 2] = jnp.concatenate(
        [grad_two[: nine // 2, 2 * c_two :], grad_two[nine // 2 :, 2 * c_two :]], axis=1
    )
    rest = total.shape[0] - nine - nine // 2
    if rest > 0:
        total[nine + nine // 2 :] = jnp.zeros((rest, total.shape[1]), F32)
    rows = total.shape[0] // 2
    keep_ref[...] = total[pl.ds(pl.multiple_of(me * rows, rows), rows)]
    give_ref[...] = total[pl.ds(pl.multiple_of((1 - me) * rows, rows), rows)].astype(BF16)


def backward_kernel(plan, wb_ref, fine, act, sg, tan, one_ref, *refs):
    out_refs, (back, first) = refs[:-2], refs[-2:]
    X, Z, R = plan.x, plan.z, plan.r
    c_in, c_one = plan.c_in, plan.c_one
    quarter = 2 * c_in
    own, first_sg = plan.at_z()
    wb = wb_ref[...]
    grad_one = None
    for i in range(plan.o):
        w, j = own + i, own + i - first_sg
        for q in range(R // 2):
            lane = 2 * q * X
            taps = jnp.dot(wb, around(sg, j, lane + X, 2 * X, X, -1), preferred_element_type=F32)
            grad = (
                taps[c_one : 2 * c_one]
                + shift(taps[:c_one], -1, X)
                + shift(taps[2 * c_one :], 1, X)
            ).astype(BF16)
            back[i, :, lane : lane + 2 * X] = grad
            grad = grad.astype(F32) * 0.125
            for g in range(8):
                t = tan[w, g * c_one : (g + 1) * c_one, lane : lane + 2 * X]
                slope = (LEAK + 1.0) / 2 + ((1.0 - LEAK) / 2) * t
                first[g * c_one : (g + 1) * c_one, lane : lane + 2 * X] = (slope * grad).astype(BF16)
        top = w * 16 * quarter
        if not isinstance(top, int):
            top = pl.multiple_of(top, 8 * quarter)
        term = lax.dot_general(
            fine[pl.ds(top, 32 * quarter), 2 * X : (2 + R) * X],
            first[...],
            (((1,), (1,)), ((), ())),
            preferred_element_type=F32,
        )
        grad_one = term if grad_one is None else grad_one + term
    half = 4 * c_one
    third = 8 * quarter
    folded = grad_one[: 3 * third, :half] + grad_one[third:, half:]
    place = {1: 0, 2: 1, 3: 2, 0: 3}

    def piece(dz, s, fy):
        row = dz * third + (s * 4 + place[fy]) * quarter
        return folded[row : row + quarter]

    taps = []
    up, down = slice(0, c_in), slice(c_in, 2 * c_in)
    left, right = slice(0, c_one), slice(c_one, 2 * c_one)
    for dz in range(3):
        for dy in range(3):
            mid, side = (
                piece(dz, s, dy)[:, : half // 2] + piece(dz, s, dy + 1)[:, half // 2 :]
                for s in range(2)
            )
            taps.append(side[down, left] + mid[up, right])
            taps.append(mid[up, left] + mid[down, right])
            taps.append(mid[down, left] + side[up, right])
    per = one_ref.shape[1] // c_one
    taps += [jnp.zeros((c_in, c_one), F32)] * (-len(taps) % (2 * per))
    for at in range(0, len(taps), 2 * per):
        pair = [jnp.concatenate(taps[at + k : at + k + per], axis=1) for k in (0, per)]
        row = at // per * c_in
        one_ref[row : row + 2 * c_in] = jnp.concatenate(pair, axis=0)
    done = len(taps) // per * c_in
    if done < one_ref.shape[0]:
        one_ref[done:] = jnp.zeros((one_ref.shape[0] - done, one_ref.shape[1]), F32)

    for k, out_ref in enumerate(out_refs):
        z0 = 0
        if plan.split:
            my_z = lax.axis_index("gz")
            z0 = (my_z if k == 0 else 1 - my_z) * Z
        for i in range(Z):
            for y in range(R):
                out_ref[0, i, y] = act[own + z0 + i + 1, :, (2 + y) * X : (3 + y) * X]
                out_ref[1, i, y] = back[z0 + i, :, y * X : (y + 1) * X]


def join_kernel(plan, *refs):
    parts, outs = refs[:-2], refs[-2:]
    me = lax.axis_index("pipe")
    my_z = lax.axis_index("gz")
    for i in range(plan.z):
        for kind, out_ref in enumerate(outs):
            if plan.split:
                mine, theirs, mine_far, theirs_far = parts
                for v, (here, far) in enumerate(((mine, mine_far), (theirs, theirs_far))):
                    one, two = here[kind, i].astype(F32), far[kind, i].astype(F32)
                    low, high = jnp.where(me == 0, one, two), jnp.where(me == 0, two, one)
                    lines = jnp.concatenate([low, high], axis=0)
                    at = my_z if v == 0 else 1 - my_z
                    out_ref[at, :, i] = jnp.swapaxes(lines, 0, 1).astype(BF16)
            else:
                for v, part in enumerate(parts):
                    at = me if v == 0 else 1 - me
                    lines = part[kind, i].astype(F32)
                    out_ref[at, :, i] = jnp.swapaxes(lines, 0, 1).astype(BF16)


def unpack_kernel(plan, own_ref, other_ref, one_ref, two_ref, full):
    c_in, c_one, c_two = plan.c_in, plan.c_one, plan.c_two
    me = lax.axis_index("pipe")
    rows = full.shape[0] // 2
    scale = 1.0 / plan.batch
    full[pl.ds(pl.multiple_of(me * rows, rows), rows)] = own_ref[:rows] * scale
    full[pl.ds(pl.multiple_of((1 - me) * rows, rows), rows)] = other_ref[:rows] * scale
    nine = 9 * c_one
    for zy in range(9):
        block = full[zy * c_one : (zy + 1) * c_one]
        two_ref[zy * 3] = block[:, :c_two]
        two_ref[zy * 3 + 1] = block[:, c_two:]
    part = c_one // 2
    for p in range(18):
        at = nine + (p % 9) * part
        lane = (p // 9) * c_two
        two_ref[(p // 2) * 3 + 2, (p % 2) * part : (p % 2 + 1) * part] = full[
            at : at + part, lane : lane + c_two
        ]
    ones = (own_ref[rows:] + other_ref[rows:]) * scale
    per = ones.shape[1] // c_one
    for t in range(27):
        row, lane = t // per * c_in, t % per * c_one
        one_ref[t] = ones[row : row + c_in, lane : lane + c_one]


def vmem(count):
    return [pl.BlockSpec(memory_space=pltpu.VMEM)] * count


def shape(dims, dtype):
    return jax.ShapeDtypeStruct(dims, dtype)


def bits(axis):
    return [(axis, 1 << k) for k in range((lax.axis_size(axis) - 1).bit_length())]


def partner(plan, part, moves):
    perm = []
    for d in range(plan.dp):
        for p in range(plan.pipe):
            for a in range(plan.gz):
                for c in range(plan.gy):
                    at = {"dp": d, "pipe": p, "gz": a, "gy": c}
                    to = dict(at)
                    for axis, step in moves:
                        to[axis] ^= step
                    perm.append((plan.index(d, p, a, c), plan.index(*to.values())))
    return lax.ppermute(part, AXES, perm)


def sum_replicas(plan, part):
    moves = bits("dp") + bits("gz") + bits("gy")
    while moves:
        first, moves = moves[0], moves[1:]
        sent = part.astype(BF16)
        part = sent.astype(F32) + partner(plan, sent, [first]).astype(F32)
        if moves:
            second, moves = moves[0], moves[1:]
            part = part + (
                partner(plan, sent, [second]).astype(F32)
                + partner(plan, sent, [first, second]).astype(F32)
            )
    return part


def per_device(volumes, conv_one, conv_two, cotangent):
    plan = Plan(volumes, cotangent, conv_one, conv_two)
    X, Y, Z, R = plan.x, plan.y, plan.z, plan.r
    c_in, c_one, c_two = plan.c_in, plan.c_one, plan.c_two
    keys = sorted({message_key(plan, k) for k in plan.kinds}, key=str)
    count = 2 if plan.split else 1
    sent = pl.pallas_call(
        functools.partial(pack_kernel, plan, keys),
        out_shape=[shape((plan.rows(k), X), BF16) for k in keys],
        in_specs=[pl.BlockSpec(memory_space=pltpu.HBM)] * 2,
        out_specs=vmem(len(keys)),
        scratch_shapes=[
            pltpu.VMEM((count,) + volumes.shape[1:], BF16),
            pltpu.VMEM((count,) + cotangent.shape[1:], BF16),
            pltpu.VMEM((count, Z, Y, plan.fold, X), BF16),
            pltpu.VMEM((count, plan.cz, plan.cy // 2, c_two, X), BF16),
            pltpu.SemaphoreType.DMA((2,)),
        ],
        compiler_params=PARAMS,
        name="pack",
    )(volumes, cotangent)
    sent = dict(zip(keys, sent))
    msgs = []
    for kind in plan.kinds:
        cells = sent[message_key(plan, kind)]
        msgs.append(cells if kind == (None, None) else swap(cells, plan, kind))

    w1, w2, wb = pl.pallas_call(
        functools.partial(weight_kernel, plan),
        out_shape=[
            shape((8 * c_one, 64 * c_in), BF16),
            shape((3 * c_two, 9 * c_one), BF16),
            shape((3 * c_one, 9 * c_two), BF16),
        ],
        in_specs=vmem(2),
        out_specs=vmem(3),
        compiler_params=PARAMS,
        cost_estimate=pl.CostEstimate(flops=10**7, bytes_accessed=10**6, transcendentals=0),
        name="weights",
    )(
        conv_one.transpose(2, 3, 4, 1, 0).reshape(27, c_in, c_one),
        conv_two.transpose(2, 3, 4, 1, 0).reshape(27, c_one, c_two),
    )

    wide = 2 * c_two
    two_rows = -(-27 * c_one // 64) * 16
    one_rows = -(-27 * c_in * c_one // (16 * wide)) * 16
    keep, give, fine, act, sg, tan = pl.pallas_call(
        functools.partial(forward_kernel, plan, len(msgs)),
        out_shape=[
            shape((two_rows, wide), F32),
            shape((two_rows, wide), BF16),
            shape(((plan.win + 1) * 32 * c_in, plan.mid * X), BF16),
            shape((plan.win + 2, c_one, plan.mid * X), BF16),
            shape((plan.planes + 2, c_two, plan.slim * X), BF16),
            shape((plan.win, 8 * c_one, R * X), F32),
        ],
        in_specs=vmem(len(msgs) + 2),
        out_specs=vmem(6),
        scratch_shapes=[
            pltpu.VMEM((plan.win, Y + 2 * REACH, plan.fold, X), BF16),
            pltpu.VMEM((plan.cot_planes, c_two, (Y + 4) * X), BF16),
            pltpu.VMEM((3 * c_two, R * X), BF16),
            pltpu.VMEM((2 * two_rows, wide), F32),
        ],
        compiler_params=PARAMS,
        name="forward",
    )(*msgs, w1, w2)

    both = [("pipe", 1)]
    part = keep + partner(plan, give, both).astype(F32)
    blocks = shape((2, Z, R, c_one, X), BF16)
    one, *outs = pl.pallas_call(
        functools.partial(backward_kernel, plan),
        out_shape=[shape((one_rows, wide), F32)] + [blocks] * (2 if plan.split else 1),
        in_specs=vmem(5),
        out_specs=vmem(3 if plan.split else 2),
        scratch_shapes=[
            pltpu.VMEM((plan.o, c_one, R * X), BF16),
            pltpu.VMEM((8 * c_one, R * X), BF16),
        ],
        compiler_params=PARAMS,
        cost_estimate=pl.CostEstimate(flops=10**9, bytes_accessed=10**7, transcendentals=0),
        name="backward",
    )(wb, fine, act, sg, tan)

    part = sum_replicas(plan, jnp.concatenate([part, one], axis=0))
    rest = partner(plan, part, both)
    if plan.split:
        outs = [outs[0], partner(plan, outs[1], [("gz", 1)])]
    outs = outs + [partner(plan, out, both) for out in outs]
    size = (2, c_one, Z, Y, X)
    all_act, all_back = pl.pallas_call(
        functools.partial(join_kernel, plan),
        out_shape=[shape(size, BF16)] * 2,
        in_specs=vmem(len(outs)),
        out_specs=vmem(2),
        compiler_params=PARAMS,
        name="join",
    )(*outs)
    grad_one, grad_two = pl.pallas_call(
        functools.partial(unpack_kernel, plan),
        out_shape=[shape((27, c_in, c_one), F32), shape((27, c_one, c_two), F32)],
        in_specs=vmem(2),
        out_specs=vmem(2),
        scratch_shapes=[pltpu.VMEM((2 * two_rows, wide), F32)],
        compiler_params=PARAMS,
        name="unpack",
    )(part, rest)
    grad_one = grad_one.reshape(3, 3, 3, c_in, c_one).transpose(4, 3, 0, 1, 2)
    grad_two = grad_two.reshape(3, 3, 3, c_one, c_two).transpose(4, 3, 0, 1, 2)
    return all_act, all_back, grad_one, grad_two


def solution(mesh):
    in_specs = (P("dp", None, "gz", "gy", None), P(), P(), P("dp", None, "gz", "gy", None))
    out_specs = (P("dp", None, "gz", "gy", None), P("dp", None, "gz", "gy", None), P(), P())
    return jax.shard_map(
        per_device, mesh=mesh, in_specs=in_specs, out_specs=out_specs, check_vma=False
    )
```

time: 50 us -> 38.6 us (0.77)
  waiting for transfers between devices: 18.8 us -> 9.95 us
  starting transfers between devices: 19.6 us -> 14.7 us
  local copies, waits for them, and re-layouts: 1.85 us -> 3.53 us
  Pallas kernels: 8.82 us -> 9.33 us
    ppermute x12 -> x14, waiting for transfers between devices: 18.8 us -> 9.95 us  [the longest x11 8.21 us: partner(): return lax.ppermute(part, AXES, perm)]
    ppermute x12 -> x14, starting transfers between devices: 19.6 us -> 14.7 us  [the longest x11 9.71 us: partner(): return lax.ppermute(part, AXES, perm)]
    unnamed x8, local copies, waits for them, and re-layouts: 1.85 us -> 3.53 us
    pallas_call x3 -> x4, Pallas kernels: 8.34 us -> 8.51 us  [the longest x1 4.87 us: per_device(): pl.pallas_call(functools.partial(forward_kernel, plan, len(msgs)), out_sh...]
  transfers between devices with their start and end apart: 12 -> 14, of which waited for: 7 -> 7; matrix products, arithmetic and copies ran while one was open for 0% -> 0% of each run, Pallas kernels for 2% -> 8%
where the time goes in v1:
time: 38.6 us; the launch traced here: 38.4 us
  starting transfers between devices  14.7 us (38%)
  waiting for transfers between devices  9.95 us (26%)
  Pallas kernels  9.33 us (24%)
  local copies, waits for them, and re-layouts  3.53 us (9%)
  between operations  0.74 us (2%)
    ppermute x11, starting transfers between devices, partner(): return lax.ppermute(part, AXES, perm)  9.71 us
    ppermute x11, waiting for transfers between devices, partner(): return lax.ppermute(part, AXES, perm)  8.21 us
    ppermute x3, starting transfers between devices, swap(): return lax.ppermute(cells, AXES, perm)  5.03 us
    pallas_call x1, Pallas kernels, per_device(): pl.pallas_call(functools.partial(forward_kernel, plan, len(msgs)), out_sh...  4.87 us
    unnamed x8, local copies, waits for them, and re-layouts  3.53 us
    ppermute x3, waiting for transfers between devices, swap(): return lax.ppermute(cells, AXES, perm)  1.73 us
    pallas_call x1, Pallas kernels, per_device(): pl.pallas_call(functools.partial(backward_kernel, plan), out_shape=[shape...  1.66 us
    pallas_call x1, Pallas kernels, per_device(): pl.pallas_call(functools.partial(join_kernel, plan), out_shape=[shape(siz...  1.06 us
  transfers between devices with their start and end apart: 14, of which 7 were waited for; matrix products, arithmetic and copies ran while one was open for 0% of the time, Pallas kernels for 8%

profile of v1, /device:TPU:0, one launch (start us, length us, event | category | flops | bytes accessed | tf_op | source)
XLA Modules:
  0.0 38.4 jit_solution(13041823558381807080)
XLA Ops:
  0.6 0.9 %copy-done = bf16[2,32,2,8,128]{4,3,2,1,0:T(8,128)(2,1)S(1)} copy-done((bf16[2,32,2,8,128]{4,3,2,1,0:T(8,128)(2,1)S(1)}, bf16[2,32,2,8,128]{4,3,2,1,0:T(8,128)(2,1)}, u32[]{:S(2)}) %copy-start) | copy-done | bytes 262168
  1.6 0.9 %copy-done.2 = bf16[2,64,1,4,64]{4,3,2,1,0:T(4,128)(2,1)S(1)} copy-done((bf16[2,64,1,4,64]{4,3,2,1,0:T(4,128)(2,1)S(1)}, bf16[2,64,1,4,64]{4,3,2,1,0:T(4,128)(2,1)}, u32[]{:S(2)}) %copy-start.2) | copy-done | bytes 65560
  2.5 0.5 %pack.1 = (bf16[256,128]{1,0:T(8,128)(2,1)S(1)}, bf16[640,128]{1,0:T(8,128)(2,1)S(1)}, bf16[256,128]{1,0:T(8,128)(2,1)S(1)}, bf16[640,128]{1,0:T(8,128)(2,1)S(1)}) custom-call(bf16[2,32,2,8,128]{4,3,2,1,0:T(8,128)(2,1)S(1)} %copy-done, bf16[2,64,1,4,64]{4,3,2,1,0:T(4,128)(2,1)S(1)} %copy-done.2), custom_call_target="tpu_custom_call" | custom-call | tf_op jit(solution)/shard_map/pack/pallas_call | solution.py:568
  3.0 3.0 %collective-permute-start.2 = (bf16[640,128]{1,0:T(8,128)(2,1)S(1)}, bf16[640,128]{1,0:T(8,128)(2,1)S(1)}, u32[]{:S(2)}, u32[]{:S(2)}) collective-permute-start(bf16[640,128]{1,0:T(8,128)(2,1)S(1)} %get-tuple-element.28), channel_id=1, source_target_pairs={{0,4},{1,5},{2,6},{3,7},{4,0},{5,1},{6,2},{7,3},{8,12},{9,13},{10,... | collective-permute-start | bytes 491528 | tf_op jit(solution)/shard_map/ppermute | solution.py:41
  6.0 1.5 %collective-permute-start = (bf16[256,128]{1,0:T(8,128)(2,1)S(1)}, bf16[256,128]{1,0:T(8,128)(2,1)S(1)}, u32[]{:S(2)}, u32[]{:S(2)}) collective-permute-start(bf16[256,128]{1,0:T(8,128)(2,1)S(1)} %get-tuple-element.26), channel_id=1, source_target_pairs={{0,16},{1,12},{2,13},{3,14},{4,20},{5,8},{6,9},{7,10},{8,5},{9,6},... | collective-permute-start | bytes 196616 | tf_op jit(solution)/shard_map/ppermute | solution.py:41
  7.5 0.5 %collective-permute-start.1 = (bf16[256,128]{1,0:T(8,128)(2,1)S(1)}, bf16[256,128]{1,0:T(8,128)(2,1)S(1)}, u32[]{:S(2)}, u32[]{:S(2)}) collective-permute-start(bf16[256,128]{1,0:T(8,128)(2,1)S(1)} %get-tuple-element.27), channel_id=1, source_target_pairs={{0,16},{1,8},{2,9},{3,10},{4,20},{5,12},{6,13},{7,14},{8,1},{9,2},... | collective-permute-start | bytes 196616 | tf_op jit(solution)/shard_map/ppermute | solution.py:41
  8.0 0.9 %copy-done.1 = bf16[64,32,3,3,3]{0,1,4,3,2:T(8,128)(2,1)S(1)} copy-done((bf16[64,32,3,3,3]{0,1,4,3,2:T(8,128)(2,1)S(1)}, bf16[64,32,3,3,3]{0,1,4,3,2:T(8,128)(2,1)}, u32[]{:S(2)}) %copy-start.1) | copy-done | bytes 110616
  8.9 0.7 %copy-done.3 = bf16[32,4,3,3,3]{0,1,4,3,2:T(4,128)(2,1)S(1)} copy-done((bf16[32,4,3,3,3]{0,1,4,3,2:T(4,128)(2,1)S(1)}, bf16[32,4,3,3,3]{0,1,4,3,2:T(4,128)(2,1)}, u32[]{:S(2)}) %copy-start.3) | copy-done | bytes 6936
  9.7 0.3 weights.1
  10.0 0.2 collective-permute-done.refs_1_
  10.2 1.5 %collective-permute-done.1.refs_2_ = bf16[256,128]{1,0:T(8,128)(2,1)S(1)} collective-permute-done((bf16[256,128]{1,0:T(8,128)(2,1)S(1)}, bf16[256,128]{1,0:T(8,128)(2,1)S(1)}, u32[]{:S(2)}, u32[]{:S(2)}) %collective-permute-start.1) | collective-permute-done | bytes 65568 | tf_op jit(solution)/shard_map/ppermute | solution.py:41
  11.8 4.9 %forward.1 = (f32[224,128]{1,0:T(8,128)S(1)}, bf16[224,128]{1,0:T(8,128)(2,1)S(1)}, bf16[640,1024]{1,0:T(8,128)(2,1)S(1)}, bf16[6,32,1024]{2,1,0:T(8,128)(2,1)S(...) custom-call(bf16[640,128]{1,0:T(8,128)(2,1)S(1)} %get-tuple-element.25.refs_0_, ...), custom_call_target="tpu_custom_call" | custom-call | tf_op jit(solution)/shard_map/forward/pallas_call | solution.py:609
  16.6 0.1 collective-permute-start.6
  16.7 1.7 %backward.1 = (f32[32,128]{1,0:T(8,128)S(1)}, bf16[2,2,4,32,128]{4,3,2,1,0:T(8,128)(2,1)S(1)}, bf16[2,2,4,32,128]{4,3,2,1,0:T(8,128)(2,1)S(1)}) custom-call(bf16[96,576]{1,0:T(8,128)(2,1)S(1)} %get-tuple-element.24.wb_ref, bf16[640,1024]{1,0:T(8,128)(2,1)S(1)} %get-tuple-element.31.fine, bf16[6,32,1024]{2,1,0:T(8,128)(2,1)S(1)} %get-tuple-element.32.act, ...), custom_call_target="tpu_custom_call" | custom-call | flops 1000000000 | bytes 10000000 | tf_op jit(solution)/shard_map/backward/pallas_call | solution.py:634
  18.4 0.0 collective-permute-done.6
  18.4 1.1 %collective-permute-start.8 = (bf16[256,128]{1,0:T(8,128)(2,1)S(1)}, bf16[256,128]{1,0:T(8,128)(2,1)S(1)}, u32[]{:S(2)}, u32[]{:S(2)}) collective-permute-start(bf16[256,128]{1,0:T(8,128)(2,1)S(1)} %pad_maximum_fusion), channel_id=1, source_target_pairs={{0,4},{1,5},{2,6},{3,7},{4,0},{5,1},{6,2},{7,3},{8,12},{9,13},{10,... | collective-permute-start | bytes 196616 | tf_op jit(solution)/shard_map/ppermute | solution.py:544
  19.6 1.5 %collective-permute-start.7 = (bf16[256,128]{1,0:T(8,128)(2,1)S(1)}, bf16[256,128]{1,0:T(8,128)(2,1)S(1)}, u32[]{:S(2)}, u32[]{:S(2)}) collective-permute-start(bf16[256,128]{1,0:T(8,128)(2,1)S(1)} %pad_maximum_fusion), channel_id=1, source_target_pairs={{0,16},{1,17},{2,18},{3,19},{4,20},{5,21},{6,22},{7,23},{8,24},{9,... | collective-permute-start | bytes 196616 | tf_op jit(solution)/shard_map/ppermute | solution.py:544
  21.1 0.9 %collective-permute-start.9 = (bf16[256,128]{1,0:T(8,128)(2,1)S(1)}, bf16[256,128]{1,0:T(8,128)(2,1)S(1)}, u32[]{:S(2)}, u32[]{:S(2)}) collective-permute-start(bf16[256,128]{1,0:T(8,128)(2,1)S(1)} %pad_maximum_fusion), channel_id=1, source_target_pairs={{0,20},{1,21},{2,22},{3,23},{4,16},{5,17},{6,18},{7,19},{8,28},{9,... | collective-permute-start | bytes 196616 | tf_op jit(solution)/shard_map/ppermute | solution.py:544
  22.0 1.1 %collective-permute-start.3 = (bf16[2,2,4,32,128]{4,3,2,1,0:T(8,128)(2,1)S(1)}, bf16[2,2,4,32,128]{4,3,2,1,0:T(8,128)(2,1)S(1)}, u32[]{:S(2)}, u32[]{:S(2)}) collective-permute-start(bf16[2,2,4,32,128]{4,3,2,1,0:T(8,128)(2,1)S(1)} %get-tuple-element.36), channel_id=1, source_target_pairs={{0,4},{1,5},{2,6},{3,7},{4,0},{5,1},{6,2},{7,3},{8,12},{9,13},{10,... | collective-permute-start | bytes 393224 | tf_op jit(solution)/shard_map/ppermute | solution.py:544
  23.0 0.0 collective-permute-done.8
  23.0 0.8 %collective-permute-done.7 = bf16[256,128]{1,0:T(8,128)(2,1)S(1)} collective-permute-done((bf16[256,128]{1,0:T(8,128)(2,1)S(1)}, bf16[256,128]{1,0:T(8,128)(2,1)S(1)}, u32[]{:S(2)}, u32[]{:S(2)}) %collective-permute-start.7) | collective-permute-done | bytes 65568 | tf_op jit(solution)/shard_map/ppermute | solution.py:544
  23.8 3.2 %collective-permute-done.9 = bf16[256,128]{1,0:T(8,128)(2,1)S(1)} collective-permute-done((bf16[256,128]{1,0:T(8,128)(2,1)S(1)}, bf16[256,128]{1,0:T(8,128)(2,1)S(1)}, u32[]{:S(2)}, u32[]{:S(2)}) %collective-permute-start.9) | collective-permute-done | bytes 65568 | tf_op jit(solution)/shard_map/ppermute | solution.py:544
  27.0 3.4 %collective-permute-start.12 = (bf16[256,128]{1,0:T(8,128)(2,1)S(1)}, bf16[256,128]{1,0:T(8,128)(2,1)S(1)}, u32[]{:S(2)}, u32[]{:S(2)}) collective-permute-start(bf16[256,128]{1,0:T(8,128)(2,1)S(1)} %add_convert_fusion), channel_id=1, source_target_pairs={{0,3},{1,2},{2,1},{3,0},{4,7},{5,6},{6,5},{7,4},{8,11},{9,10},{10,... | collective-permute-start | bytes 196616 | tf_op jit(solution)/shard_map/ppermute | solution.py:544
  30.5 0.1 collective-permute-start.11
  30.6 0.9 %collective-permute-start.10 = (bf16[256,128]{1,0:T(8,128)(2,1)S(1)}, bf16[256,128]{1,0:T(8,128)(2,1)S(1)}, u32[]{:S(2)}, u32[]{:S(2)}) collective-permute-start(bf16[256,128]{1,0:T(8,128)(2,1)S(1)} %add_convert_fusion), channel_id=1, source_target_pairs={{0,1},{1,0},{2,3},{3,2},{4,5},{5,4},{6,7},{7,6},{8,9},{9,8},{10,11... | collective-permute-start | bytes 196616 | tf_op jit(solution)/shard_map/ppermute | solution.py:544
  31.5 0.5 %collective-permute-start.5 = (bf16[2,2,4,32,128]{4,3,2,1,0:T(8,128)(2,1)S(1)}, bf16[2,2,4,32,128]{4,3,2,1,0:T(8,128)(2,1)S(1)}, u32[]{:S(2)}, u32[]{:S(2)}) collective-permute-start(bf16[2,2,4,32,128]{4,3,2,1,0:T(8,128)(2,1)S(1)} %collective-permute-done.3.refs_1_), channel_id=1, source_target_pairs={{0,8},{1,9},{2,10},{3,11},{4,12},{5,13},{6,14},{7,15},{8,0},{9,1},... | collective-permute-start | bytes 393224 | tf_op jit(solution)/shard_map/ppermute | solution.py:544
  32.0 1.5 %collective-permute-done.12 = bf16[256,128]{1,0:T(8,128)(2,1)S(1)} collective-permute-done((bf16[256,128]{1,0:T(8,128)(2,1)S(1)}, bf16[256,128]{1,0:T(8,128)(2,1)S(1)}, u32[]{:S(2)}, u32[]{:S(2)}) %collective-permute-start.12) | collective-permute-done | bytes 65568 | tf_op jit(solution)/shard_map/ppermute | solution.py:544
  33.4 2.6 %collective-permute-done.11 = bf16[256,128]{1,0:T(8,128)(2,1)S(1)} collective-permute-done((bf16[256,128]{1,0:T(8,128)(2,1)S(1)}, bf16[256,128]{1,0:T(8,128)(2,1)S(1)}, u32[]{:S(2)}, u32[]{:S(2)}) %collective-permute-start.11) | collective-permute-done | bytes 65568 | tf_op jit(solution)/shard_map/ppermute | solution.py:544
  36.0 0.1 collective-permute-start.13
  36.1 1.1 %join.1 = (bf16[2,32,2,8,128]{4,3,2,1,0:T(8,128)(2,1)}, bf16[2,32,2,8,128]{4,3,2,1,0:T(8,128)(2,1)}) custom-call(bf16[2,2,4,32,128]{4,3,2,1,0:T(8,128)(2,1)S(1)} %get-tuple-element.35.refs_0_, bf16[2,2,4,32,128]{4,3,2,1,0:T(8,128)(2,1)S(1)} %collective-permute-done.3.refs_1_, bf16[2,2,4,32,128]{4,3,2,1,0:T(8,128)(2,1)S(1)} %collective-permute-done.4.refs_2_, ...), custom_call_target="tpu_custom_call" | custom-call | tf_op jit(solution)/shard_map/join/pallas_call | solution.py:654
  37.2 0.3 collective-permute-done.13.other_ref
  37.5 0.9 %unpack.1 = (f32[27,4,32]{2,1,0:T(4,128)}, f32[27,32,64]{2,1,0:T(8,128)}) custom-call(f32[256,128]{1,0:T(8,128)S(1)} %add_add_fusion.own_ref, f32[256,128]{1,0:T(8,128)S(1)} %collective-permute-done.13.other_ref), custom_call_target="tpu_custom_call" | custom-call | tf_op jit(solution)/shard_map/unpack/pallas_call | solution.py:662
  (15 shorter events, 0.1 us)
Async XLA Ops:
  0.6 1.0 %copy-start = (bf16[2,32,2,8,128]{4,3,2,1,0:T(8,128)(2,1)S(1)}, bf16[2,32,2,8,128]{4,3,2,1,0:T(8,128)(2,1)}, u32[]{:S(2)}) copy-start(bf16[2,32,2,8,128]{4,3,2,1,0:T(8,128)(2,1)} %vol_hbm.1) | copy-start | bytes 786436
  1.6 0.9 %copy-start.2 = (bf16[2,64,1,4,64]{4,3,2,1,0:T(4,128)(2,1)S(1)}, bf16[2,64,1,4,64]{4,3,2,1,0:T(4,128)(2,1)}, u32[]{:S(2)}) copy-start(bf16[2,64,1,4,64]{4,3,2,1,0:T(4,128)(2,1)} %cot_hbm.1) | copy-start | bytes 196612
  3.0 8.8 %collective-permute-start.2 = (bf16[640,128]{1,0:T(8,128)(2,1)S(1)}, bf16[640,128]{1,0:T(8,128)(2,1)S(1)}, u32[]{:S(2)}, u32[]{:S(2)}) collective-permute-start(bf16[640,128]{1,0:T(8,128)(2,1)S(1)} %get-tuple-element.28), channel_id=1, source_target_pairs={{0,4},{1,5},{2,6},{3,7},{4,0},{5,1},{6,2},{7,3},{8,12},{9,13},{10,... | collective-permute-start | bytes 491528 | tf_op jit(solution)/shard_map/ppermute | solution.py:41
  6.0 4.3 %collective-permute-start = (bf16[256,128]{1,0:T(8,128)(2,1)S(1)}, bf16[256,128]{1,0:T(8,128)(2,1)S(1)}, u32[]{:S(2)}, u32[]{:S(2)}) collective-permute-start(bf16[256,128]{1,0:T(8,128)(2,1)S(1)} %get-tuple-element.26), channel_id=1, source_target_pairs={{0,16},{1,12},{2,13},{3,14},{4,20},{5,8},{6,9},{7,10},{8,5},{9,6},... | collective-permute-start | bytes 196616 | tf_op jit(solution)/shard_map/ppermute | solution.py:41
  7.5 4.3 %collective-permute-start.1 = (bf16[256,128]{1,0:T(8,128)(2,1)S(1)}, bf16[256,128]{1,0:T(8,128)(2,1)S(1)}, u32[]{:S(2)}, u32[]{:S(2)}) collective-permute-start(bf16[256,128]{1,0:T(8,128)(2,1)S(1)} %get-tuple-element.27), channel_id=1, source_target_pairs={{0,16},{1,8},{2,9},{3,10},{4,20},{5,12},{6,13},{7,14},{8,1},{9,2},... | collective-permute-start | bytes 196616 | tf_op jit(solution)/shard_map/ppermute | solution.py:41
  8.0 0.9 %copy-start.1 = (bf16[64,32,3,3,3]{0,1,4,3,2:T(8,128)(2,1)S(1)}, bf16[64,32,3,3,3]{0,1,4,3,2:T(8,128)(2,1)}, u32[]{:S(2)}) copy-start(bf16[64,32,3,3,3]{0,1,4,3,2:T(8,128)(2,1)} %param.6) | copy-start | bytes 331780
  8.9 0.7 %copy-start.3 = (bf16[32,4,3,3,3]{0,1,4,3,2:T(4,128)(2,1)S(1)}, bf16[32,4,3,3,3]{0,1,4,3,2:T(4,128)(2,1)}, u32[]{:S(2)}) copy-start(bf16[32,4,3,3,3]{0,1,4,3,2:T(4,128)(2,1)} %param.5) | copy-start | bytes 20740
  16.6 1.8 %collective-permute-start.6 = (bf16[224,128]{1,0:T(8,128)(2,1)S(1)}, bf16[224,128]{1,0:T(8,128)(2,1)S(1)}, u32[]{:S(2)}, u32[]{:S(2)}) collective-permute-start(bf16[224,128]{1,0:T(8,128)(2,1)S(1)} %get-tuple-element.40), channel_id=1, source_target_pairs={{0,8},{1,9},{2,10},{3,11},{4,12},{5,13},{6,14},{7,15},{8,0},{9,1},... | collective-permute-start | bytes 172040 | tf_op jit(solution)/shard_map/ppermute | solution.py:544
  18.4 4.6 %collective-permute-start.8 = (bf16[256,128]{1,0:T(8,128)(2,1)S(1)}, bf16[256,128]{1,0:T(8,128)(2,1)S(1)}, u32[]{:S(2)}, u32[]{:S(2)}) collective-permute-start(bf16[256,128]{1,0:T(8,128)(2,1)S(1)} %pad_maximum_fusion), channel_id=1, source_target_pairs={{0,4},{1,5},{2,6},{3,7},{4,0},{5,1},{6,2},{7,3},{8,12},{9,13},{10,... | collective-permute-start | bytes 196616 | tf_op jit(solution)/shard_map/ppermute | solution.py:544
  19.6 4.3 %collective-permute-start.7 = (bf16[256,128]{1,0:T(8,128)(2,1)S(1)}, bf16[256,128]{1,0:T(8,128)(2,1)S(1)}, u32[]{:S(2)}, u32[]{:S(2)}) collective-permute-start(bf16[256,128]{1,0:T(8,128)(2,1)S(1)} %pad_maximum_fusion), channel_id=1, source_target_pairs={{0,16},{1,17},{2,18},{3,19},{4,20},{5,21},{6,22},{7,23},{8,24},{9,... | collective-permute-start | bytes 196616 | tf_op jit(solution)/shard_map/ppermute | solution.py:544
  21.1 5.9 %collective-permute-start.9 = (bf16[256,128]{1,0:T(8,128)(2,1)S(1)}, bf16[256,128]{1,0:T(8,128)(2,1)S(1)}, u32[]{:S(2)}, u32[]{:S(2)}) collective-permute-start(bf16[256,128]{1,0:T(8,128)(2,1)S(1)} %pad_maximum_fusion), channel_id=1, source_target_pairs={{0,20},{1,21},{2,22},{3,23},{4,16},{5,17},{6,18},{7,19},{8,28},{9,... | collective-permute-start | bytes 196616 | tf_op jit(solution)/shard_map/ppermute | solution.py:544
  22.0 9.5 %collective-permute-start.3 = (bf16[2,2,4,32,128]{4,3,2,1,0:T(8,128)(2,1)S(1)}, bf16[2,2,4,32,128]{4,3,2,1,0:T(8,128)(2,1)S(1)}, u32[]{:S(2)}, u32[]{:S(2)}) collective-permute-start(bf16[2,2,4,32,128]{4,3,2,1,0:T(8,128)(2,1)S(1)} %get-tuple-element.36), channel_id=1, source_target_pairs={{0,4},{1,5},{2,6},{3,7},{4,0},{5,1},{6,2},{7,3},{8,12},{9,13},{10,... | collective-permute-start | bytes 393224 | tf_op jit(solution)/shard_map/ppermute | solution.py:544
  27.0 6.4 %collective-permute-start.12 = (bf16[256,128]{1,0:T(8,128)(2,1)S(1)}, bf16[256,128]{1,0:T(8,128)(2,1)S(1)}, u32[]{:S(2)}, u32[]{:S(2)}) collective-permute-start(bf16[256,128]{1,0:T(8,128)(2,1)S(1)} %add_convert_fusion), channel_id=1, source_target_pairs={{0,3},{1,2},{2,1},{3,0},{4,7},{5,6},{6,5},{7,4},{8,11},{9,10},{10,... | collective-permute-start | bytes 196616 | tf_op jit(solution)/shard_map/ppermute | solution.py:544
  30.5 5.6 %collective-permute-start.11 = (bf16[256,128]{1,0:T(8,128)(2,1)S(1)}, bf16[256,128]{1,0:T(8,128)(2,1)S(1)}, u32[]{:S(2)}, u32[]{:S(2)}) collective-permute-start(bf16[256,128]{1,0:T(8,128)(2,1)S(1)} %add_convert_fusion), channel_id=1, source_target_pairs={{0,2},{1,3},{2,0},{3,1},{4,6},{5,7},{6,4},{7,5},{8,10},{9,11},{10,... | collective-permute-start | bytes 196616 | tf_op jit(solution)/shard_map/ppermute | solution.py:544
  30.6 5.4 %collective-permute-start.10 = (bf16[256,128]{1,0:T(8,128)(2,1)S(1)}, bf16[256,128]{1,0:T(8,128)(2,1)S(1)}, u32[]{:S(2)}, u32[]{:S(2)}) collective-permute-start(bf16[256,128]{1,0:T(8,128)(2,1)S(1)} %add_convert_fusion), channel_id=1, source_target_pairs={{0,1},{1,0},{2,3},{3,2},{4,5},{5,4},{6,7},{7,6},{8,9},{9,8},{10,11... | collective-permute-start | bytes 196616 | tf_op jit(solution)/shard_map/ppermute | solution.py:544
  31.5 4.7 %collective-permute-start.4 = (bf16[2,2,4,32,128]{4,3,2,1,0:T(8,128)(2,1)S(1)}, bf16[2,2,4,32,128]{4,3,2,1,0:T(8,128)(2,1)S(1)}, u32[]{:S(2)}, u32[]{:S(2)}) collective-permute-start(bf16[2,2,4,32,128]{4,3,2,1,0:T(8,128)(2,1)S(1)} %get-tuple-element.35.refs_0_), channel_id=1, source_target_pairs={{0,8},{1,9},{2,10},{3,11},{4,12},{5,13},{6,14},{7,15},{8,0},{9,1},... | collective-permute-start | bytes 393224 | tf_op jit(solution)/shard_map/ppermute | solution.py:544
  31.5 4.7 %collective-permute-start.5 = (bf16[2,2,4,32,128]{4,3,2,1,0:T(8,128)(2,1)S(1)}, bf16[2,2,4,32,128]{4,3,2,1,0:T(8,128)(2,1)S(1)}, u32[]{:S(2)}, u32[]{:S(2)}) collective-permute-start(bf16[2,2,4,32,128]{4,3,2,1,0:T(8,128)(2,1)S(1)} %collective-permute-done.3.refs_1_), channel_id=1, source_target_pairs={{0,8},{1,9},{2,10},{3,11},{4,12},{5,13},{6,14},{7,15},{8,0},{9,1},... | collective-permute-start | bytes 393224 | tf_op jit(solution)/shard_map/ppermute | solution.py:544
  36.0 1.4 %collective-permute-start.13 = (f32[256,128]{1,0:T(8,128)S(1)}, f32[256,128]{1,0:T(8,128)S(1)}, u32[]{:S(2)}, u32[]{:S(2)}) collective-permute-start(f32[256,128]{1,0:T(8,128)S(1)} %add_add_fusion.own_ref), channel_id=1, source_target_pairs={{0,8},{1,9},{2,10},{3,11},{4,12},{5,13},{6,14},{7,15},{8,0},{9,1},... | collective-permute-start | bytes 393224 | tf_op jit(solution)/shard_map/ppermute | solution.py:544

commit v2 on v1

--- a/solution.py
+++ b/solution.py
@@ -307,7 +307,7 @@
                     fine[pl.ds(row + 2 * quarter, 2 * quarter), lane : lane + X] = far.astype(BF16)
         return carry
 
-    lax.fori_loop(0, plan.win, spread, 0)
+    lax.fori_loop(0, plan.win, spread, 0, unroll=True)
 
     w1 = w1_ref[...]
     last_q = plan.mid // 2 - 1
@@ -340,7 +340,7 @@
             act[w + 1, :, lane : lane + 2 * X] = mean.astype(BF16)
         return carry
 
-    lax.fori_loop(0, plan.win, first_section, 0)
+    lax.fori_loop(0, plan.win, first_section, 0, unroll=True)
 
     w2 = w2_ref[...]
     sg[0] = jnp.zeros(sg.shape[1:], BF16)
@@ -363,7 +363,7 @@
             sg[j + 1, :, lane : lane + 2 * X] = (slope * part).astype(BF16)
         return carry
 
-    lax.fori_loop(0, plan.planes, second_section, 0)
+    lax.fori_loop(0, plan.planes, second_section, 0, unroll=True)
 
     grad_two = None
     for i in range(plan.o):
@@ -530,15 +530,14 @@
     return [(axis, 1 << k) for k in range((lax.axis_size(axis) - 1).bit_length())]
 
 
-def partner(plan, part, moves):
+def partner(plan, part, moves, other_moves=None):
     perm = []
     for d in range(plan.dp):
         for p in range(plan.pipe):
             for a in range(plan.gz):
                 for c in range(plan.gy):
-                    at = {"dp": d, "pipe": p, "gz": a, "gy": c}
-                    to = dict(at)
-                    for axis, step in moves:
+                    to = {"dp": d, "pipe": p, "gz": a, "gy": c}
+                    for axis, step in moves if p == 0 or other_moves is None else other_moves:
                         to[axis] ^= step
                     perm.append((plan.index(d, p, a, c), plan.index(*to.values())))
     return lax.ppermute(part, AXES, perm)
@@ -546,16 +545,20 @@
 
 def sum_replicas(plan, part):
     moves = bits("dp") + bits("gz") + bits("gy")
-    while moves:
-        first, moves = moves[0], moves[1:]
+    steps = [moves[i : i + 2] for i in range(0, len(moves), 2)]
+    if any(len(step) == 1 for step in steps):
+        orders = zip(steps, steps)
+    else:
+        orders = zip(steps[::-1], steps)
+    for here, there in orders:
         sent = part.astype(BF16)
-        part = sent.astype(F32) + partner(plan, sent, [first]).astype(F32)
-        if moves:
-            second, moves = moves[0], moves[1:]
-            part = part + (
-                partner(plan, sent, [second]).astype(F32)
-                + partner(plan, sent, [first, second]).astype(F32)
-            )
+        got = [partner(plan, sent, here[:1], there[:1]).astype(F32)]
+        if len(here) > 1:
+            got.append(partner(plan, sent, here[1:], there[1:]).astype(F32))
+            got.append(partner(plan, sent, here, there).astype(F32))
+        part = sent.astype(F32) + got[0]
+        if len(here) > 1:
+            part = part + (got[1] + got[2])
     return part
 
 
@@ -579,7 +582,7 @@
         ],
         compiler_params=PARAMS,
         name="pack",
-    )(volumes, cotangent)
+    )(*[pltpu.with_memory_space_constraint(a, pltpu.HBM) for a in (volumes, cotangent)])
     sent = dict(zip(keys, sent))
     msgs = []
     for kind in plan.kinds:

time: 38.6 us -> 35.2 us (0.912)
  local copies, waits for them, and re-layouts: 3.53 us -> 1.68 us
  Pallas kernels: 9.33 us -> 8.29 us
  waiting for transfers between devices: 9.95 us -> 9.13 us
    unnamed x8 -> x4, local copies, waits for them, and re-layouts: 3.53 us -> 1.68 us
    pallas_call x1, Pallas kernels: 4.87 us -> 3.06 us  [per_device(): pl.pallas_call(functools.partial(forward_kernel, plan, len(msgs)), out_sh...]
    ppermute x11, waiting for transfers between devices: 8.21 us -> 7.4 us  [partner(): return lax.ppermute(part, AXES, perm)]
    pallas_call x1, Pallas kernels: 0.47 us -> 1.24 us  [per_device(): pl.pallas_call(functools.partial(pack_kernel, plan, keys), out_shape=[sha...]
  transfers between devices with their start and end apart: 14 -> 14, of which waited for: 7 -> 8; matrix products, arithmetic and copies ran while one was open for 0% -> 0% of each run, Pallas kernels for 8% -> 9%
where the time goes in v2:
time: 35.2 us; the launch traced here: 34.9 us
  starting transfers between devices  15 us (43%)
  waiting for transfers between devices  9.13 us (26%)
  Pallas kernels  8.29 us (24%)
  local copies, waits for them, and re-layouts  1.68 us (5%)
  between operations  0.73 us (2%)
    ppermute x11, starting transfers between devices, partner(): return lax.ppermute(part, AXES, perm)  9.96 us
    ppermute x11, waiting for transfers between devices, partner(): return lax.ppermute(part, AXES, perm)  7.4 us
    ppermute x3, starting transfers between devices, swap(): return lax.ppermute(cells, AXES, perm)  5.03 us
    pallas_call x1, Pallas kernels, per_device(): pl.pallas_call(functools.partial(forward_kernel, plan, len(msgs)), out_sh...  3.06 us
    ppermute x3, waiting for transfers between devices, swap(): return lax.ppermute(cells, AXES, perm)  1.73 us
    unnamed x4, local copies, waits for them, and re-layouts  1.68 us
    pallas_call x1, Pallas kernels, per_device(): pl.pallas_call(functools.partial(backward_kernel, plan), out_shape=[shape...  1.67 us
    pallas_call x1, Pallas kernels, per_device(): pl.pallas_call(functools.partial(pack_kernel, plan, keys), out_shape=[sha...  1.24 us
  transfers between devices with their start and end apart: 14, of which 8 were waited for; matrix products, arithmetic and copies ran while one was open for 0% of the time, Pallas kernels for 9%

profile of v2, /device:TPU:0, one launch (start us, length us, event | category | flops | bytes accessed | tf_op | source)
XLA Modules:
  0.0 34.9 jit_solution(2507378205515736428)
XLA Ops:
  0.6 1.2 %pack.1 = (bf16[256,128]{1,0:T(8,128)(2,1)S(1)}, bf16[640,128]{1,0:T(8,128)(2,1)S(1)}, bf16[256,128]{1,0:T(8,128)(2,1)S(1)}, bf16[640,128]{1,0:T(8,128)(2,1)S(1)}) custom-call(bf16[2,32,2,8,128]{4,3,2,1,0:T(8,128)(2,1)} %vol_hbm.1, bf16[2,64,1,4,64]{4,3,2,1,0:T(4,128)(2,1)} %cot_hbm.1), custom_call_target="tpu_custom_call" | custom-call | tf_op jit(solution)/shard_map/pack/pallas_call | solution.py:571
  1.9 3.0 %collective-permute-start.2 = (bf16[640,128]{1,0:T(8,128)(2,1)S(1)}, bf16[640,128]{1,0:T(8,128)(2,1)S(1)}, u32[]{:S(2)}, u32[]{:S(2)}) collective-permute-start(bf16[640,128]{1,0:T(8,128)(2,1)S(1)} %get-tuple-element.28), channel_id=1, source_target_pairs={{0,4},{1,5},{2,6},{3,7},{4,0},{5,1},{6,2},{7,3},{8,12},{9,13},{10,... | collective-permute-start | bytes 491528 | tf_op jit(solution)/shard_map/ppermute | solution.py:41
  4.9 1.5 %collective-permute-start = (bf16[256,128]{1,0:T(8,128)(2,1)S(1)}, bf16[256,128]{1,0:T(8,128)(2,1)S(1)}, u32[]{:S(2)}, u32[]{:S(2)}) collective-permute-start(bf16[256,128]{1,0:T(8,128)(2,1)S(1)} %get-tuple-element.26), channel_id=1, source_target_pairs={{0,16},{1,12},{2,13},{3,14},{4,20},{5,8},{6,9},{7,10},{8,5},{9,6},... | collective-permute-start | bytes 196616 | tf_op jit(solution)/shard_map/ppermute | solution.py:41
  6.4 0.5 %collective-permute-start.1 = (bf16[256,128]{1,0:T(8,128)(2,1)S(1)}, bf16[256,128]{1,0:T(8,128)(2,1)S(1)}, u32[]{:S(2)}, u32[]{:S(2)}) collective-permute-start(bf16[256,128]{1,0:T(8,128)(2,1)S(1)} %get-tuple-element.27), channel_id=1, source_target_pairs={{0,16},{1,8},{2,9},{3,10},{4,20},{5,12},{6,13},{7,14},{8,1},{9,2},... | collective-permute-start | bytes 196616 | tf_op jit(solution)/shard_map/ppermute | solution.py:41
  6.9 0.9 %copy-done = bf16[64,32,3,3,3]{0,1,4,3,2:T(8,128)(2,1)S(1)} copy-done((bf16[64,32,3,3,3]{0,1,4,3,2:T(8,128)(2,1)S(1)}, bf16[64,32,3,3,3]{0,1,4,3,2:T(8,128)(2,1)}, u32[]{:S(2)}) %copy-start) | copy-done | bytes 110616
  7.8 0.7 %copy-done.1 = bf16[32,4,3,3,3]{0,1,4,3,2:T(4,128)(2,1)S(1)} copy-done((bf16[32,4,3,3,3]{0,1,4,3,2:T(4,128)(2,1)S(1)}, bf16[32,4,3,3,3]{0,1,4,3,2:T(4,128)(2,1)}, u32[]{:S(2)}) %copy-start.1) | copy-done | bytes 6936
  8.6 0.3 weights.1
  8.9 0.2 collective-permute-done.refs_1_
  9.1 1.5 %collective-permute-done.1.refs_2_ = bf16[256,128]{1,0:T(8,128)(2,1)S(1)} collective-permute-done((bf16[256,128]{1,0:T(8,128)(2,1)S(1)}, bf16[256,128]{1,0:T(8,128)(2,1)S(1)}, u32[]{:S(2)}, u32[]{:S(2)}) %collective-permute-start.1) | collective-permute-done | bytes 65568 | tf_op jit(solution)/shard_map/ppermute | solution.py:41
  10.7 0.0 collective-permute-done.2.refs_3_
  10.7 3.1 %forward.1 = (f32[224,128]{1,0:T(8,128)S(1)}, bf16[224,128]{1,0:T(8,128)(2,1)S(1)}, bf16[640,1024]{1,0:T(8,128)(2,1)S(1)}, bf16[6,32,1024]{2,1,0:T(8,128)(2,1)S(...) custom-call(bf16[640,128]{1,0:T(8,128)(2,1)S(1)} %get-tuple-element.25.refs_0_, ...), custom_call_target="tpu_custom_call" | custom-call | tf_op jit(solution)/shard_map/forward/pallas_call | solution.py:612
  13.7 0.1 collective-permute-start.6
  13.8 1.7 %backward.1 = (f32[32,128]{1,0:T(8,128)S(1)}, bf16[2,2,4,32,128]{4,3,2,1,0:T(8,128)(2,1)S(1)}, bf16[2,2,4,32,128]{4,3,2,1,0:T(8,128)(2,1)S(1)}) custom-call(bf16[96,576]{1,0:T(8,128)(2,1)S(1)} %get-tuple-element.24.wb_ref, bf16[640,1024]{1,0:T(8,128)(2,1)S(1)} %get-tuple-element.31.fine, bf16[6,32,1024]{2,1,0:T(8,128)(2,1)S(1)} %get-tuple-element.32.act, ...), custom_call_target="tpu_custom_call" | custom-call | flops 1000000000 | bytes 10000000 | tf_op jit(solution)/shard_map/backward/pallas_call | solution.py:637
  15.5 0.0 collective-permute-done.6
  15.5 2.7 %collective-permute-start.8 = (bf16[256,128]{1,0:T(8,128)(2,1)S(1)}, bf16[256,128]{1,0:T(8,128)(2,1)S(1)}, u32[]{:S(2)}, u32[]{:S(2)}) collective-permute-start(bf16[256,128]{1,0:T(8,128)(2,1)S(1)} %pad_maximum_fusion), channel_id=1, source_target_pairs={{0,2},{1,3},{2,0},{3,1},{4,6},{5,7},{6,4},{7,5},{8,12},{9,13},{10,... | collective-permute-start | bytes 196616 | tf_op jit(solution)/shard_map/ppermute | solution.py:543
  18.3 0.9 %collective-permute-start.7 = (bf16[256,128]{1,0:T(8,128)(2,1)S(1)}, bf16[256,128]{1,0:T(8,128)(2,1)S(1)}, u32[]{:S(2)}, u32[]{:S(2)}) collective-permute-start(bf16[256,128]{1,0:T(8,128)(2,1)S(1)} %pad_maximum_fusion), channel_id=1, source_target_pairs={{0,1},{1,0},{2,3},{3,2},{4,5},{5,4},{6,7},{7,6},{8,24},{9,25},{10,... | collective-permute-start | bytes 196616 | tf_op jit(solution)/shard_map/ppermute | solution.py:543
  19.1 0.9 %collective-permute-start.9 = (bf16[256,128]{1,0:T(8,128)(2,1)S(1)}, bf16[256,128]{1,0:T(8,128)(2,1)S(1)}, u32[]{:S(2)}, u32[]{:S(2)}) collective-permute-start(bf16[256,128]{1,0:T(8,128)(2,1)S(1)} %pad_maximum_fusion), channel_id=1, source_target_pairs={{0,3},{1,2},{2,1},{3,0},{4,7},{5,6},{6,5},{7,4},{8,28},{9,29},{10,... | collective-permute-start | bytes 196616 | tf_op jit(solution)/shard_map/ppermute | solution.py:543
  20.0 1.3 %collective-permute-start.3 = (bf16[2,2,4,32,128]{4,3,2,1,0:T(8,128)(2,1)S(1)}, bf16[2,2,4,32,128]{4,3,2,1,0:T(8,128)(2,1)S(1)}, u32[]{:S(2)}, u32[]{:S(2)}) collective-permute-start(bf16[2,2,4,32,128]{4,3,2,1,0:T(8,128)(2,1)S(1)} %get-tuple-element.36), channel_id=1, source_target_pairs={{0,4},{1,5},{2,6},{3,7},{4,0},{5,1},{6,2},{7,3},{8,12},{9,13},{10,... | collective-permute-start | bytes 393224 | tf_op jit(solution)/shard_map/ppermute | solution.py:543
  21.3 0.0 collective-permute-done.8
  21.3 1.2 %collective-permute-done.7 = bf16[256,128]{1,0:T(8,128)(2,1)S(1)} collective-permute-done((bf16[256,128]{1,0:T(8,128)(2,1)S(1)}, bf16[256,128]{1,0:T(8,128)(2,1)S(1)}, u32[]{:S(2)}, u32[]{:S(2)}) %collective-permute-start.7) | collective-permute-done | bytes 65568 | tf_op jit(solution)/shard_map/ppermute | solution.py:543
  22.5 2.7 %collective-permute-done.9 = bf16[256,128]{1,0:T(8,128)(2,1)S(1)} collective-permute-done((bf16[256,128]{1,0:T(8,128)(2,1)S(1)}, bf16[256,128]{1,0:T(8,128)(2,1)S(1)}, u32[]{:S(2)}, u32[]{:S(2)}) %collective-permute-start.9) | collective-permute-done | bytes 65568 | tf_op jit(solution)/shard_map/ppermute | solution.py:543
  25.2 2.7 %collective-permute-start.12 = (bf16[256,128]{1,0:T(8,128)(2,1)S(1)}, bf16[256,128]{1,0:T(8,128)(2,1)S(1)}, u32[]{:S(2)}, u32[]{:S(2)}) collective-permute-start(bf16[256,128]{1,0:T(8,128)(2,1)S(1)} %add_convert_fusion), channel_id=1, source_target_pairs={{0,20},{1,21},{2,22},{3,23},{4,16},{5,17},{6,18},{7,19},{8,11},{9,... | collective-permute-start | bytes 196616 | tf_op jit(solution)/shard_map/ppermute | solution.py:543
  28.0 0.3 collective-permute-start.11
  28.3 0.5 %collective-permute-start.10 = (bf16[256,128]{1,0:T(8,128)(2,1)S(1)}, bf16[256,128]{1,0:T(8,128)(2,1)S(1)}, u32[]{:S(2)}, u32[]{:S(2)}) collective-permute-start(bf16[256,128]{1,0:T(8,128)(2,1)S(1)} %add_convert_fusion), channel_id=1, source_target_pairs={{0,16},{1,17},{2,18},{3,19},{4,20},{5,21},{6,22},{7,23},{8,9},{9,8... | collective-permute-start | bytes 196616 | tf_op jit(solution)/shard_map/ppermute | solution.py:543
  28.8 0.5 %collective-permute-start.5 = (bf16[2,2,4,32,128]{4,3,2,1,0:T(8,128)(2,1)S(1)}, bf16[2,2,4,32,128]{4,3,2,1,0:T(8,128)(2,1)S(1)}, u32[]{:S(2)}, u32[]{:S(2)}) collective-permute-start(bf16[2,2,4,32,128]{4,3,2,1,0:T(8,128)(2,1)S(1)} %collective-permute-done.3.refs_1_), channel_id=1, source_target_pairs={{0,8},{1,9},{2,10},{3,11},{4,12},{5,13},{6,14},{7,15},{8,0},{9,1},... | collective-permute-start | bytes 393224 | tf_op jit(solution)/shard_map/ppermute | solution.py:543
  29.3 1.2 %collective-permute-done.12 = bf16[256,128]{1,0:T(8,128)(2,1)S(1)} collective-permute-done((bf16[256,128]{1,0:T(8,128)(2,1)S(1)}, bf16[256,128]{1,0:T(8,128)(2,1)S(1)}, u32[]{:S(2)}, u32[]{:S(2)}) %collective-permute-start.12) | collective-permute-done | bytes 65568 | tf_op jit(solution)/shard_map/ppermute | solution.py:543
  30.5 1.7 %collective-permute-done.11 = bf16[256,128]{1,0:T(8,128)(2,1)S(1)} collective-permute-done((bf16[256,128]{1,0:T(8,128)(2,1)S(1)}, bf16[256,128]{1,0:T(8,128)(2,1)S(1)}, u32[]{:S(2)}, u32[]{:S(2)}) %collective-permute-start.11) | collective-permute-done | bytes 65568 | tf_op jit(solution)/shard_map/ppermute | solution.py:543
  32.2 0.3 collective-permute-done.10
  32.6 0.1 collective-permute-start.13
  32.7 1.1 %join.1 = (bf16[2,32,2,8,128]{4,3,2,1,0:T(8,128)(2,1)}, bf16[2,32,2,8,128]{4,3,2,1,0:T(8,128)(2,1)}) custom-call(bf16[2,2,4,32,128]{4,3,2,1,0:T(8,128)(2,1)S(1)} %get-tuple-element.35.refs_0_, bf16[2,2,4,32,128]{4,3,2,1,0:T(8,128)(2,1)S(1)} %collective-permute-done.3.refs_1_, bf16[2,2,4,32,128]{4,3,2,1,0:T(8,128)(2,1)S(1)} %collective-permute-done.4.refs_2_, ...), custom_call_target="tpu_custom_call" | custom-call | tf_op jit(solution)/shard_map/join/pallas_call | solution.py:657
  33.8 0.3 collective-permute-done.13.other_ref
  34.0 0.9 %unpack.1 = (f32[27,4,32]{2,1,0:T(4,128)}, f32[27,32,64]{2,1,0:T(8,128)}) custom-call(f32[256,128]{1,0:T(8,128)S(1)} %add_add_fusion.own_ref, f32[256,128]{1,0:T(8,128)S(1)} %collective-permute-done.13.other_ref), custom_call_target="tpu_custom_call" | custom-call | tf_op jit(solution)/shard_map/unpack/pallas_call | solution.py:665
  (11 shorter events, 0.1 us)
Async XLA Ops:
  1.9 8.8 %collective-permute-start.2 = (bf16[640,128]{1,0:T(8,128)(2,1)S(1)}, bf16[640,128]{1,0:T(8,128)(2,1)S(1)}, u32[]{:S(2)}, u32[]{:S(2)}) collective-permute-start(bf16[640,128]{1,0:T(8,128)(2,1)S(1)} %get-tuple-element.28), channel_id=1, source_target_pairs={{0,4},{1,5},{2,6},{3,7},{4,0},{5,1},{6,2},{7,3},{8,12},{9,13},{10,... | collective-permute-start | bytes 491528 | tf_op jit(solution)/shard_map/ppermute | solution.py:41
  4.9 4.3 %collective-permute-start = (bf16[256,128]{1,0:T(8,128)(2,1)S(1)}, bf16[256,128]{1,0:T(8,128)(2,1)S(1)}, u32[]{:S(2)}, u32[]{:S(2)}) collective-permute-start(bf16[256,128]{1,0:T(8,128)(2,1)S(1)} %get-tuple-element.26), channel_id=1, source_target_pairs={{0,16},{1,12},{2,13},{3,14},{4,20},{5,8},{6,9},{7,10},{8,5},{9,6},... | collective-permute-start | bytes 196616 | tf_op jit(solution)/shard_map/ppermute | solution.py:41
  6.4 4.3 %collective-permute-start.1 = (bf16[256,128]{1,0:T(8,128)(2,1)S(1)}, bf16[256,128]{1,0:T(8,128)(2,1)S(1)}, u32[]{:S(2)}, u32[]{:S(2)}) collective-permute-start(bf16[256,128]{1,0:T(8,128)(2,1)S(1)} %get-tuple-element.27), channel_id=1, source_target_pairs={{0,16},{1,8},{2,9},{3,10},{4,20},{5,12},{6,13},{7,14},{8,1},{9,2},... | collective-permute-start | bytes 196616 | tf_op jit(solution)/shard_map/ppermute | solution.py:41
  6.9 0.9 %copy-start = (bf16[64,32,3,3,3]{0,1,4,3,2:T(8,128)(2,1)S(1)}, bf16[64,32,3,3,3]{0,1,4,3,2:T(8,128)(2,1)}, u32[]{:S(2)}) copy-start(bf16[64,32,3,3,3]{0,1,4,3,2:T(8,128)(2,1)} %param.6) | copy-start | bytes 331780
  7.8 0.7 %copy-start.1 = (bf16[32,4,3,3,3]{0,1,4,3,2:T(4,128)(2,1)S(1)}, bf16[32,4,3,3,3]{0,1,4,3,2:T(4,128)(2,1)}, u32[]{:S(2)}) copy-start(bf16[32,4,3,3,3]{0,1,4,3,2:T(4,128)(2,1)} %param.5) | copy-start | bytes 20740
  13.7 1.8 %collective-permute-start.6 = (bf16[224,128]{1,0:T(8,128)(2,1)S(1)}, bf16[224,128]{1,0:T(8,128)(2,1)S(1)}, u32[]{:S(2)}, u32[]{:S(2)}) collective-permute-start(bf16[224,128]{1,0:T(8,128)(2,1)S(1)} %get-tuple-element.40), channel_id=1, source_target_pairs={{0,8},{1,9},{2,10},{3,11},{4,12},{5,13},{6,14},{7,15},{8,0},{9,1},... | collective-permute-start | bytes 172040 | tf_op jit(solution)/shard_map/ppermute | solution.py:543
  15.5 5.8 %collective-permute-start.8 = (bf16[256,128]{1,0:T(8,128)(2,1)S(1)}, bf16[256,128]{1,0:T(8,128)(2,1)S(1)}, u32[]{:S(2)}, u32[]{:S(2)}) collective-permute-start(bf16[256,128]{1,0:T(8,128)(2,1)S(1)} %pad_maximum_fusion), channel_id=1, source_target_pairs={{0,2},{1,3},{2,0},{3,1},{4,6},{5,7},{6,4},{7,5},{8,12},{9,13},{10,... | collective-permute-start | bytes 196616 | tf_op jit(solution)/shard_map/ppermute | solution.py:543
  18.3 4.3 %collective-permute-start.7 = (bf16[256,128]{1,0:T(8,128)(2,1)S(1)}, bf16[256,128]{1,0:T(8,128)(2,1)S(1)}, u32[]{:S(2)}, u32[]{:S(2)}) collective-permute-start(bf16[256,128]{1,0:T(8,128)(2,1)S(1)} %pad_maximum_fusion), channel_id=1, source_target_pairs={{0,1},{1,0},{2,3},{3,2},{4,5},{5,4},{6,7},{7,6},{8,24},{9,25},{10,... | collective-permute-start | bytes 196616 | tf_op jit(solution)/shard_map/ppermute | solution.py:543
  19.1 6.1 %collective-permute-start.9 = (bf16[256,128]{1,0:T(8,128)(2,1)S(1)}, bf16[256,128]{1,0:T(8,128)(2,1)S(1)}, u32[]{:S(2)}, u32[]{:S(2)}) collective-permute-start(bf16[256,128]{1,0:T(8,128)(2,1)S(1)} %pad_maximum_fusion), channel_id=1, source_target_pairs={{0,3},{1,2},{2,1},{3,0},{4,7},{5,6},{6,5},{7,4},{8,28},{9,29},{10,... | collective-permute-start | bytes 196616 | tf_op jit(solution)/shard_map/ppermute | solution.py:543
  20.0 8.8 %collective-permute-start.3 = (bf16[2,2,4,32,128]{4,3,2,1,0:T(8,128)(2,1)S(1)}, bf16[2,2,4,32,128]{4,3,2,1,0:T(8,128)(2,1)S(1)}, u32[]{:S(2)}, u32[]{:S(2)}) collective-permute-start(bf16[2,2,4,32,128]{4,3,2,1,0:T(8,128)(2,1)S(1)} %get-tuple-element.36), channel_id=1, source_target_pairs={{0,4},{1,5},{2,6},{3,7},{4,0},{5,1},{6,2},{7,3},{8,12},{9,13},{10,... | collective-permute-start | bytes 393224 | tf_op jit(solution)/shard_map/ppermute | solution.py:543
  25.2 5.2 %collective-permute-start.12 = (bf16[256,128]{1,0:T(8,128)(2,1)S(1)}, bf16[256,128]{1,0:T(8,128)(2,1)S(1)}, u32[]{:S(2)}, u32[]{:S(2)}) collective-permute-start(bf16[256,128]{1,0:T(8,128)(2,1)S(1)} %add_convert_fusion), channel_id=1, source_target_pairs={{0,20},{1,21},{2,22},{3,23},{4,16},{5,17},{6,18},{7,19},{8,11},{9,... | collective-permute-start | bytes 196616 | tf_op jit(solution)/shard_map/ppermute | solution.py:543
  28.0 4.3 %collective-permute-start.11 = (bf16[256,128]{1,0:T(8,128)(2,1)S(1)}, bf16[256,128]{1,0:T(8,128)(2,1)S(1)}, u32[]{:S(2)}, u32[]{:S(2)}) collective-permute-start(bf16[256,128]{1,0:T(8,128)(2,1)S(1)} %add_convert_fusion), channel_id=1, source_target_pairs={{0,4},{1,5},{2,6},{3,7},{4,0},{5,1},{6,2},{7,3},{8,10},{9,11},{10,... | collective-permute-start | bytes 196616 | tf_op jit(solution)/shard_map/ppermute | solution.py:543
  28.3 4.3 %collective-permute-start.10 = (bf16[256,128]{1,0:T(8,128)(2,1)S(1)}, bf16[256,128]{1,0:T(8,128)(2,1)S(1)}, u32[]{:S(2)}, u32[]{:S(2)}) collective-permute-start(bf16[256,128]{1,0:T(8,128)(2,1)S(1)} %add_convert_fusion), channel_id=1, source_target_pairs={{0,16},{1,17},{2,18},{3,19},{4,20},{5,21},{6,22},{7,23},{8,9},{9,8... | collective-permute-start | bytes 196616 | tf_op jit(solution)/shard_map/ppermute | solution.py:543
  28.8 3.9 %collective-permute-start.4 = (bf16[2,2,4,32,128]{4,3,2,1,0:T(8,128)(2,1)S(1)}, bf16[2,2,4,32,128]{4,3,2,1,0:T(8,128)(2,1)S(1)}, u32[]{:S(2)}, u32[]{:S(2)}) collective-permute-start(bf16[2,2,4,32,128]{4,3,2,1,0:T(8,128)(2,1)S(1)} %get-tuple-element.35.refs_0_), channel_id=1, source_target_pairs={{0,8},{1,9},{2,10},{3,11},{4,12},{5,13},{6,14},{7,15},{8,0},{9,1},... | collective-permute-start | bytes 393224 | tf_op jit(solution)/shard_map/ppermute | solution.py:543
  28.8 3.9 %collective-permute-start.5 = (bf16[2,2,4,32,128]{4,3,2,1,0:T(8,128)(2,1)S(1)}, bf16[2,2,4,32,128]{4,3,2,1,0:T(8,128)(2,1)S(1)}, u32[]{:S(2)}, u32[]{:S(2)}) collective-permute-start(bf16[2,2,4,32,128]{4,3,2,1,0:T(8,128)(2,1)S(1)} %collective-permute-done.3.refs_1_), channel_id=1, source_target_pairs={{0,8},{1,9},{2,10},{3,11},{4,12},{5,13},{6,14},{7,15},{8,0},{9,1},... | collective-permute-start | bytes 393224 | tf_op jit(solution)/shard_map/ppermute | solution.py:543
  32.6 1.4 %collective-permute-start.13 = (f32[256,128]{1,0:T(8,128)S(1)}, f32[256,128]{1,0:T(8,128)S(1)}, u32[]{:S(2)}, u32[]{:S(2)}) collective-permute-start(f32[256,128]{1,0:T(8,128)S(1)} %add_add_fusion.own_ref), channel_id=1, source_target_pairs={{0,8},{1,9},{2,10},{3,11},{4,12},{5,13},{6,14},{7,15},{8,0},{9,1},... | collective-permute-start | bytes 393224 | tf_op jit(solution)/shard_map/ppermute | solution.py:543

commit v3 on v2

--- a/solution.py
+++ b/solution.py
@@ -101,12 +101,17 @@
     def blocks(self, kind):
         z_kind, y_kind = kind
         nz, nc = (self.z, self.cz) if z_kind is None or self.split else (self.h, 1)
-        ny, np_ = (self.y, self.cy // 2) if y_kind is None else (REACH, 1)
-        return nz, ny, nc, np_
+        if y_kind is not None:
+            ny, nr = REACH, 1
+        elif z_kind is not None and self.split:
+            ny, nr = self.r + REACH, self.r // 2 + 1
+        else:
+            ny, nr = self.y, self.cy
+        return nz, ny, nc, nr
 
     def rows(self, kind):
-        nz, ny, nc, np_ = self.blocks(kind)
-        return nz * ny * self.fold + nc * np_ * self.c_two
+        nz, ny, nc, nr = self.blocks(kind)
+        return nz * ny * self.fold + nc * nr * self.c_two // 2
 
 
 def message_key(plan, kind):
@@ -118,34 +123,35 @@
 
 def pack_kernel(plan, keys, vol_hbm, cot_hbm, *refs):
     out_refs, (vol_ref, cot_ref, cells, cots, sems) = refs[: len(keys)], refs[len(keys) :]
-    count = vol_ref.shape[0]
     me, my_z, my_y = lax.axis_index("pipe"), lax.axis_index("gz"), lax.axis_index("gy")
-    first = 0 if plan.split else me
-    loads = [
-        pltpu.make_async_copy(vol_hbm.at[pl.ds(first, count)], vol_ref, sems.at[0]),
-        pltpu.make_async_copy(cot_hbm.at[pl.ds(first, count)], cot_ref, sems.at[1]),
-    ]
+    first = [my_z, 1 - my_z] if plan.split else [me]
+    loads = []
+    for v, volume in enumerate(first):
+        loads.append(pltpu.make_async_copy(vol_hbm.at[volume], vol_ref.at[v], sems.at[2 * v]))
+        loads.append(pltpu.make_async_copy(cot_hbm.at[volume], cot_ref.at[v], sems.at[2 * v + 1]))
     for load in loads:
         load.start()
-    loads[0].wait()
-    for v in range(count):
+    half = plan.c_two // 2
+    for v in range(len(first)):
+        loads[2 * v].wait()
         for z in range(plan.z):
             block = jnp.swapaxes(vol_ref[v, :, z].astype(F32), 0, 1).astype(BF16)
             for y in range(plan.y):
                 cells[v, z, y] = block[y]
-    loads[1].wait()
-    for v in range(count):
+        loads[2 * v + 1].wait()
         for z in range(plan.cz):
             block = jnp.swapaxes(cot_ref[v, :, z].astype(F32), 0, 1)
-            for m in range(plan.cy // 2):
-                pair = jnp.concatenate([block[2 * m], block[2 * m + 1]], axis=1)
-                cots[v, z, m] = pair.astype(BF16)
+            for r in range(plan.cy):
+                row = jnp.concatenate([block[r][:half], block[r][half:]], axis=1)
+                cots[v, z, r] = row.astype(BF16)
     for key, out_ref in zip(keys, out_refs):
-        nz, ny, nc, np_ = plan.blocks(key)
-        v = z0 = c0 = y0 = p0 = 0
+        nz, ny, nc, nr = plan.blocks(key)
+        z0 = c0 = y0 = r0 = 0
+        v = 1 if plan.split and key[0] is not None else 0
+        y_low = None
         if plan.split:
-            v = my_z if key[0] is None else 1 - my_z
-            y_low = me == 0
+            if key != (None, None):
+                y_low = me == 0
         else:
             if key[0] is not None:
                 z_low = my_z % 2 == 1 - key[0]
@@ -153,21 +159,29 @@
                 c0 = jnp.where(z_low, 0, plan.cz - nc)
             if key[1] is not None:
                 y_low = my_y % 2 == 1 - key[1]
-        if key[1] is not None:
+        if y_low is not None:
             y0 = jnp.where(y_low, 0, plan.y - ny)
-            p0 = jnp.where(y_low, 0, plan.cy // 2 - np_)
+            r0 = jnp.where(y_low, 0, plan.cy - nr)
         at = 0
         for i in range(nz):
             for j in range(ny):
                 out_ref[at : at + plan.fold] = cells[v, z0 + i, y0 + j]
                 at += plan.fold
         for i in range(nc):
-            for j in range(np_):
-                out_ref[at : at + plan.c_two] = cots[v, c0 + i, p0 + j]
-                at += plan.c_two
-
-
-def weight_kernel(plan, one_ref, two_ref, w1_ref, w2_ref, wb_ref):
+            for j in range(nr):
+                out_ref[at : at + half] = cots[v, c0 + i, r0 + j]
+                at += half
+
+
+def weight_kernel(plan, one_hbm, two_hbm, w1_ref, w2_ref, wb_ref, one_ref, two_ref, sems):
+    loads = [
+        pltpu.make_async_copy(one_hbm, one_ref, sems.at[0]),
+        pltpu.make_async_copy(two_hbm, two_ref, sems.at[1]),
+    ]
+    for load in loads:
+        load.start()
+    for load in loads:
+        load.wait()
     c_in, c_one, c_two = plan.c_in, plan.c_one, plan.c_two
     none = jnp.zeros((c_in, c_one), F32)
     pairs_x = {}
@@ -235,7 +249,7 @@
     if not plan.split:
         cot[...] = jnp.zeros_like(cot)
     for kind, msg in zip(plan.kinds, msgs):
-        nz, ny, nc, np_ = plan.blocks(kind)
+        nz, ny, nc, nr = plan.blocks(kind)
         z_kind, y_kind = kind
         below, used = None, None
         if plan.split:
@@ -252,7 +266,11 @@
                 c0 = jnp.where(before, 0, plan.cz + 1)
             if y_kind is not None:
                 below = my_y % 2 == 1 - y_kind
-        y0 = REACH if y_kind is None else jnp.where(below, 0, Y + REACH)
+        y0, r0 = REACH, 0
+        if y_kind is not None:
+            y0 = jnp.where(below, 0, Y + REACH)
+        elif z_kind is not None and plan.split:
+            y0, r0 = REACH + me * (Y - ny), me * (plan.cy - nr)
         at = 0
         for i in range(nz):
             for j in range(ny):
@@ -261,22 +279,23 @@
                     block = jnp.where(used, block, jnp.zeros_like(block))
                 cells[z0 + i, y0 + j] = block
                 at += fold
+        part = c_two // 2
+        up = jnp.dot(msg[at : at + nc * nr * part], pick, preferred_element_type=F32)
+        if used is not None:
+            up = jnp.where(used, up, 0.0)
+        up = up.astype(BF16)
         for i in range(nc):
-            for j in range(np_):
-                up = jnp.dot(msg[at : at + c_two], pick, preferred_element_type=F32)
-                if used is not None:
-                    up = jnp.where(used, up, 0.0)
-                up = up.astype(BF16)
-                at += c_two
-                one, two = up[:, :X], up[:, X:]
+            for j in range(nr):
+                row = up[(i * nr + j) * part : (i * nr + j + 1) * part]
                 if y_kind is None:
-                    for r, piece in enumerate((one, one, two, two)):
-                        lane = (4 * j + r + 2) * X
-                        cot[c0 + i, :, lane : lane + X] = piece
+                    lanes = [(2 * (r0 + j) + 2) * X, (2 * (r0 + j) + 3) * X]
                 else:
-                    piece = jnp.where(below, two, one)
-                    lane = pl.multiple_of(jnp.where(below, X, (Y + 2) * X), X)
-                    cot[c0 + i, :, pl.ds(lane, X)] = piece
+                    lanes = [jnp.where(below, X, (Y + 2) * X)]
+                for lane in lanes:
+                    if not isinstance(lane, int):
+                        lane = pl.multiple_of(lane, X)
+                    cot[c0 + i, :part, pl.ds(lane, X)] = row[:, :X]
+                    cot[c0 + i, part:, pl.ds(lane, X)] = row[:, X:]
 
     quarter = 2 * c_in
     fine[0 : 8 * quarter] = jnp.zeros((8 * quarter, plan.mid * X), BF16)
@@ -402,7 +421,7 @@
     quarter = 2 * c_in
     own, first_sg = plan.at_z()
     wb = wb_ref[...]
-    grad_one = None
+    tall = []
     for i in range(plan.o):
         w, j = own + i, own + i - first_sg
         for q in range(R // 2):
@@ -418,17 +437,18 @@
             for g in range(8):
                 t = tan[w, g * c_one : (g + 1) * c_one, lane : lane + 2 * X]
                 slope = (LEAK + 1.0) / 2 + ((1.0 - LEAK) / 2) * t
-                first[g * c_one : (g + 1) * c_one, lane : lane + 2 * X] = (slope * grad).astype(BF16)
+                at = (i * R + 2 * q) * X
+                first[g * c_one : (g + 1) * c_one, at : at + 2 * X] = (slope * grad).astype(BF16)
         top = w * 16 * quarter
         if not isinstance(top, int):
             top = pl.multiple_of(top, 8 * quarter)
-        term = lax.dot_general(
-            fine[pl.ds(top, 32 * quarter), 2 * X : (2 + R) * X],
-            first[...],
-            (((1,), (1,)), ((), ())),
-            preferred_element_type=F32,
-        )
-        grad_one = term if grad_one is None else grad_one + term
+        tall.append(fine[pl.ds(top, 32 * quarter), 2 * X : (2 + R) * X])
+    grad_one = lax.dot_general(
+        jnp.concatenate(tall, axis=1),
+        first[...],
+        (((1,), (1,)), ((), ())),
+        preferred_element_type=F32,
+    )
     half = 4 * c_one
     third = 8 * quarter
     folded = grad_one[: 3 * third, :half] + grad_one[third:, half:]
@@ -577,8 +597,8 @@
             pltpu.VMEM((count,) + volumes.shape[1:], BF16),
             pltpu.VMEM((count,) + cotangent.shape[1:], BF16),
             pltpu.VMEM((count, Z, Y, plan.fold, X), BF16),
-            pltpu.VMEM((count, plan.cz, plan.cy // 2, c_two, X), BF16),
-            pltpu.SemaphoreType.DMA((2,)),
+            pltpu.VMEM((count, plan.cz, plan.cy, c_two // 2, X), BF16),
+            pltpu.SemaphoreType.DMA((2 * count,)),
         ],
         compiler_params=PARAMS,
         name="pack",
@@ -596,14 +616,23 @@
             shape((3 * c_two, 9 * c_one), BF16),
             shape((3 * c_one, 9 * c_two), BF16),
         ],
-        in_specs=vmem(2),
+        in_specs=[pl.BlockSpec(memory_space=pltpu.HBM)] * 2,
         out_specs=vmem(3),
+        scratch_shapes=[
+            pltpu.VMEM((27, c_in, c_one), BF16),
+            pltpu.VMEM((27, c_one, c_two), BF16),
+            pltpu.SemaphoreType.DMA((2,)),
+        ],
         compiler_params=PARAMS,
         cost_estimate=pl.CostEstimate(flops=10**7, bytes_accessed=10**6, transcendentals=0),
         name="weights",
     )(
-        conv_one.transpose(2, 3, 4, 1, 0).reshape(27, c_in, c_one),
-        conv_two.transpose(2, 3, 4, 1, 0).reshape(27, c_one, c_two),
+        *[
+            pltpu.with_memory_space_constraint(
+                w.transpose(2, 3, 4, 1, 0).reshape(27, w.shape[1], w.shape[0]), pltpu.HBM
+            )
+            for w in (conv_one, conv_two)
+        ]
     )
 
     wide = 2 * c_two
@@ -641,7 +670,7 @@
         out_specs=vmem(3 if plan.split else 2),
         scratch_shapes=[
             pltpu.VMEM((plan.o, c_one, R * X), BF16),
-            pltpu.VMEM((8 * c_one, R * X), BF16),
+            pltpu.VMEM((8 * c_one, plan.o * R * X), BF16),
         ],
         compiler_params=PARAMS,
         cost_estimate=pl.CostEstimate(flops=10**9, bytes_accessed=10**7, transcendentals=0),

time: 35.2 us -> 34.1 us (0.969)
  local copies, waits for them, and re-layouts: 1.68 us -> 0 us
  Pallas kernels: 8.29 us -> 8.89 us
  waiting for transfers between devices: 9.13 us -> 9.5 us
    unnamed x4 -> x0, local copies, waits for them, and re-layouts: 1.68 us -> none
    pallas_call x1, Pallas kernels: 0.34 us -> 1.32 us  [per_device(): pl.pallas_call(functools.partial(weight_kernel, plan), out_shape=[shape((...]
    ppermute x3, waiting for transfers between devices: 1.73 us -> 2.35 us  [swap(): return lax.ppermute(cells, AXES, perm)]
  transfers between devices with their start and end apart: 14 -> 14, of which waited for: 8 -> 9; matrix products, arithmetic and copies ran while one was open for 0% -> 0% of each run, Pallas kernels for 9% -> 11%
where the time goes in v3:
time: 34.1 us; the launch traced here: 34 us
  starting transfers between devices  14.7 us (43%)
  waiting for transfers between devices  9.5 us (28%)
  Pallas kernels  8.89 us (26%)
  between operations  0.73 us (2%)
    ppermute x11, starting transfers between devices, partner(): return lax.ppermute(part, AXES, perm)  9.71 us
    ppermute x11, waiting for transfers between devices, partner(): return lax.ppermute(part, AXES, perm)  7.15 us
    ppermute x3, starting transfers between devices, swap(): return lax.ppermute(cells, AXES, perm)  5.03 us
    pallas_call x1, Pallas kernels, per_device(): pl.pallas_call(functools.partial(forward_kernel, plan, len(msgs)), out_sh...  2.99 us
    ppermute x3, waiting for transfers between devices, swap(): return lax.ppermute(cells, AXES, perm)  2.35 us
    pallas_call x1, Pallas kernels, per_device(): pl.pallas_call(functools.partial(backward_kernel, plan), out_shape=[shape...  1.33 us
    pallas_call x1, Pallas kernels, per_device(): pl.pallas_call(functools.partial(weight_kernel, plan), out_shape=[shape((...  1.32 us
    pallas_call x1, Pallas kernels, per_device(): pl.pallas_call(functools.partial(pack_kernel, plan, keys), out_shape=[sha...  1.27 us
  transfers between devices with their start and end apart: 14, of which 9 were waited for; matrix products, arithmetic and copies ran while one was open for 0% of the time, Pallas kernels for 11%

profile of v3, /device:TPU:0, one launch (start us, length us, event | category | flops | bytes accessed | tf_op | source)
XLA Modules:
  0.0 34.0 jit_solution(8725143604005941886)
XLA Ops:
  0.6 1.3 %pack.1 = (bf16[224,128]{1,0:T(8,128)(2,1)S(1)}, bf16[544,128]{1,0:T(8,128)(2,1)S(1)}, bf16[224,128]{1,0:T(8,128)(2,1)S(1)}, bf16[640,128]{1,0:T(8,128)(2,1)S(1)}) custom-call(bf16[2,32,2,8,128]{4,3,2,1,0:T(8,128)(2,1)} %vol_hbm.1, bf16[2,64,1,4,64]{4,3,2,1,0:T(4,128)(2,1)} %cot_hbm.1), custom_call_target="tpu_custom_call" | custom-call | tf_op jit(solution)/shard_map/pack/pallas_call | solution.py:591
  1.9 3.0 %collective-permute-start.2 = (bf16[544,128]{1,0:T(8,128)(2,1)S(1)}, bf16[544,128]{1,0:T(8,128)(2,1)S(1)}, u32[]{:S(2)}, u32[]{:S(2)}) collective-permute-start(bf16[544,128]{1,0:T(8,128)(2,1)S(1)} %get-tuple-element.28), channel_id=1, source_target_pairs={{0,4},{1,5},{2,6},{3,7},{4,0},{5,1},{6,2},{7,3},{8,12},{9,13},{10,... | collective-permute-start | bytes 417800 | tf_op jit(solution)/shard_map/ppermute | solution.py:41
  4.9 1.5 %collective-permute-start = (bf16[224,128]{1,0:T(8,128)(2,1)S(1)}, bf16[224,128]{1,0:T(8,128)(2,1)S(1)}, u32[]{:S(2)}, u32[]{:S(2)}) collective-permute-start(bf16[224,128]{1,0:T(8,128)(2,1)S(1)} %get-tuple-element.26), channel_id=1, source_target_pairs={{0,16},{1,12},{2,13},{3,14},{4,20},{5,8},{6,9},{7,10},{8,5},{9,6},... | collective-permute-start | bytes 172040 | tf_op jit(solution)/shard_map/ppermute | solution.py:41
  6.4 0.5 %collective-permute-start.1 = (bf16[224,128]{1,0:T(8,128)(2,1)S(1)}, bf16[224,128]{1,0:T(8,128)(2,1)S(1)}, u32[]{:S(2)}, u32[]{:S(2)}) collective-permute-start(bf16[224,128]{1,0:T(8,128)(2,1)S(1)} %get-tuple-element.27), channel_id=1, source_target_pairs={{0,16},{1,8},{2,9},{3,10},{4,20},{5,12},{6,13},{7,14},{8,1},{9,2},... | collective-permute-start | bytes 172040 | tf_op jit(solution)/shard_map/ppermute | solution.py:41
  6.9 1.3 %weights.1 = (bf16[256,256]{1,0:T(8,128)(2,1)S(1)}, bf16[192,288]{1,0:T(8,128)(2,1)S(1)}, bf16[96,576]{1,0:T(8,128)(2,1)S(1)}) custom-call(bf16[27,4,32]{2,1,0:T(4,128)(2,1)} %bitcast.13, bf16[27,32,64]{2,1,0:T(8,128)(2,1)} %bitcast.12), custom_call_target="tpu_custom_call" | custom-call | flops 10000000 | bytes 1000000 | tf_op jit(solution)/shard_map/weights/pallas_call | solution.py:612
  8.3 0.8 %collective-permute-done.refs_1_ = bf16[224,128]{1,0:T(8,128)(2,1)S(1)} collective-permute-done((bf16[224,128]{1,0:T(8,128)(2,1)S(1)}, bf16[224,128]{1,0:T(8,128)(2,1)S(1)}, u32[]{:S(2)}, u32[]{:S(2)}) %collective-permute-start) | collective-permute-done | bytes 57376 | tf_op jit(solution)/shard_map/ppermute | solution.py:41
  9.1 1.5 %collective-permute-done.1.refs_2_ = bf16[224,128]{1,0:T(8,128)(2,1)S(1)} collective-permute-done((bf16[224,128]{1,0:T(8,128)(2,1)S(1)}, bf16[224,128]{1,0:T(8,128)(2,1)S(1)}, u32[]{:S(2)}, u32[]{:S(2)}) %collective-permute-start.1) | collective-permute-done | bytes 57376 | tf_op jit(solution)/shard_map/ppermute | solution.py:41
  10.6 0.0 collective-permute-done.2.refs_3_
  10.6 3.0 %forward.1 = (f32[224,128]{1,0:T(8,128)S(1)}, bf16[224,128]{1,0:T(8,128)(2,1)S(1)}, bf16[640,1024]{1,0:T(8,128)(2,1)S(1)}, bf16[6,32,1024]{2,1,0:T(8,128)(2,1)S(...) custom-call(bf16[640,128]{1,0:T(8,128)(2,1)S(1)} %get-tuple-element.25.refs_0_, ...), custom_call_target="tpu_custom_call" | custom-call | tf_op jit(solution)/shard_map/forward/pallas_call | solution.py:641
  13.6 0.1 collective-permute-start.6
  13.7 1.3 %backward.1 = (f32[32,128]{1,0:T(8,128)S(1)}, bf16[2,2,4,32,128]{4,3,2,1,0:T(8,128)(2,1)S(1)}, bf16[2,2,4,32,128]{4,3,2,1,0:T(8,128)(2,1)S(1)}) custom-call(bf16[96,576]{1,0:T(8,128)(2,1)S(1)} %get-tuple-element.24.wb_ref, bf16[640,1024]{1,0:T(8,128)(2,1)S(1)} %get-tuple-element.31.fine, bf16[6,32,1024]{2,1,0:T(8,128)(2,1)S(1)} %get-tuple-element.32.act, ...), custom_call_target="tpu_custom_call" | custom-call | flops 1000000000 | bytes 10000000 | tf_op jit(solution)/shard_map/backward/pallas_call | solution.py:666
  15.0 0.0 collective-permute-done.6
  15.1 2.2 %collective-permute-start.8 = (bf16[256,128]{1,0:T(8,128)(2,1)S(1)}, bf16[256,128]{1,0:T(8,128)(2,1)S(1)}, u32[]{:S(2)}, u32[]{:S(2)}) collective-permute-start(bf16[256,128]{1,0:T(8,128)(2,1)S(1)} %pad_maximum_fusion), channel_id=1, source_target_pairs={{0,2},{1,3},{2,0},{3,1},{4,6},{5,7},{6,4},{7,5},{8,12},{9,13},{10,... | collective-permute-start | bytes 196616 | tf_op jit(solution)/shard_map/ppermute | solution.py:563
  17.3 0.9 %collective-permute-start.7 = (bf16[256,128]{1,0:T(8,128)(2,1)S(1)}, bf16[256,128]{1,0:T(8,128)(2,1)S(1)}, u32[]{:S(2)}, u32[]{:S(2)}) collective-permute-start(bf16[256,128]{1,0:T(8,128)(2,1)S(1)} %pad_maximum_fusion), channel_id=1, source_target_pairs={{0,1},{1,0},{2,3},{3,2},{4,5},{5,4},{6,7},{7,6},{8,24},{9,25},{10,... | collective-permute-start | bytes 196616 | tf_op jit(solution)/shard_map/ppermute | solution.py:563
  18.2 1.4 %collective-permute-start.9 = (bf16[256,128]{1,0:T(8,128)(2,1)S(1)}, bf16[256,128]{1,0:T(8,128)(2,1)S(1)}, u32[]{:S(2)}, u32[]{:S(2)}) collective-permute-start(bf16[256,128]{1,0:T(8,128)(2,1)S(1)} %pad_maximum_fusion), channel_id=1, source_target_pairs={{0,3},{1,2},{2,1},{3,0},{4,7},{5,6},{6,5},{7,4},{8,28},{9,29},{10,... | collective-permute-start | bytes 196616 | tf_op jit(solution)/shard_map/ppermute | solution.py:563
  19.5 1.1 %collective-permute-start.3 = (bf16[2,2,4,32,128]{4,3,2,1,0:T(8,128)(2,1)S(1)}, bf16[2,2,4,32,128]{4,3,2,1,0:T(8,128)(2,1)S(1)}, u32[]{:S(2)}, u32[]{:S(2)}) collective-permute-start(bf16[2,2,4,32,128]{4,3,2,1,0:T(8,128)(2,1)S(1)} %get-tuple-element.36), channel_id=1, source_target_pairs={{0,4},{1,5},{2,6},{3,7},{4,0},{5,1},{6,2},{7,3},{8,12},{9,13},{10,... | collective-permute-start | bytes 393224 | tf_op jit(solution)/shard_map/ppermute | solution.py:563
  20.6 0.5 %collective-permute-done.8 = bf16[256,128]{1,0:T(8,128)(2,1)S(1)} collective-permute-done((bf16[256,128]{1,0:T(8,128)(2,1)S(1)}, bf16[256,128]{1,0:T(8,128)(2,1)S(1)}, u32[]{:S(2)}, u32[]{:S(2)}) %collective-permute-start.8) | collective-permute-done | bytes 65568 | tf_op jit(solution)/shard_map/ppermute | solution.py:563
  21.1 0.5 %collective-permute-done.7 = bf16[256,128]{1,0:T(8,128)(2,1)S(1)} collective-permute-done((bf16[256,128]{1,0:T(8,128)(2,1)S(1)}, bf16[256,128]{1,0:T(8,128)(2,1)S(1)}, u32[]{:S(2)}, u32[]{:S(2)}) %collective-permute-start.7) | collective-permute-done | bytes 65568 | tf_op jit(solution)/shard_map/ppermute | solution.py:563
  21.6 2.6 %collective-permute-done.9 = bf16[256,128]{1,0:T(8,128)(2,1)S(1)} collective-permute-done((bf16[256,128]{1,0:T(8,128)(2,1)S(1)}, bf16[256,128]{1,0:T(8,128)(2,1)S(1)}, u32[]{:S(2)}, u32[]{:S(2)}) %collective-permute-start.9) | collective-permute-done | bytes 65568 | tf_op jit(solution)/shard_map/ppermute | solution.py:563
  24.3 2.6 %collective-permute-start.12 = (bf16[256,128]{1,0:T(8,128)(2,1)S(1)}, bf16[256,128]{1,0:T(8,128)(2,1)S(1)}, u32[]{:S(2)}, u32[]{:S(2)}) collective-permute-start(bf16[256,128]{1,0:T(8,128)(2,1)S(1)} %add_convert_fusion), channel_id=1, source_target_pairs={{0,20},{1,21},{2,22},{3,23},{4,16},{5,17},{6,18},{7,19},{8,11},{9,... | collective-permute-start | bytes 196616 | tf_op jit(solution)/shard_map/ppermute | solution.py:563
  26.9 0.5 %collective-permute-start.11 = (bf16[256,128]{1,0:T(8,128)(2,1)S(1)}, bf16[256,128]{1,0:T(8,128)(2,1)S(1)}, u32[]{:S(2)}, u32[]{:S(2)}) collective-permute-start(bf16[256,128]{1,0:T(8,128)(2,1)S(1)} %add_convert_fusion), channel_id=1, source_target_pairs={{0,4},{1,5},{2,6},{3,7},{4,0},{5,1},{6,2},{7,3},{8,10},{9,11},{10,... | collective-permute-start | bytes 196616 | tf_op jit(solution)/shard_map/ppermute | solution.py:563
  27.3 0.5 %collective-permute-start.10 = (bf16[256,128]{1,0:T(8,128)(2,1)S(1)}, bf16[256,128]{1,0:T(8,128)(2,1)S(1)}, u32[]{:S(2)}, u32[]{:S(2)}) collective-permute-start(bf16[256,128]{1,0:T(8,128)(2,1)S(1)} %add_convert_fusion), channel_id=1, source_target_pairs={{0,16},{1,17},{2,18},{3,19},{4,20},{5,21},{6,22},{7,23},{8,9},{9,8... | collective-permute-start | bytes 196616 | tf_op jit(solution)/shard_map/ppermute | solution.py:563
  27.8 0.0 collective-permute-start.4
  27.8 0.0 collective-permute-done.3.refs_1_
  27.8 0.5 %collective-permute-start.5 = (bf16[2,2,4,32,128]{4,3,2,1,0:T(8,128)(2,1)S(1)}, bf16[2,2,4,32,128]{4,3,2,1,0:T(8,128)(2,1)S(1)}, u32[]{:S(2)}, u32[]{:S(2)}) collective-permute-start(bf16[2,2,4,32,128]{4,3,2,1,0:T(8,128)(2,1)S(1)} %collective-permute-done.3.refs_1_), channel_id=1, source_target_pairs={{0,8},{1,9},{2,10},{3,11},{4,12},{5,13},{6,14},{7,15},{8,0},{9,1},... | collective-permute-start | bytes 393224 | tf_op jit(solution)/shard_map/ppermute | solution.py:563
  28.4 1.2 %collective-permute-done.12 = bf16[256,128]{1,0:T(8,128)(2,1)S(1)} collective-permute-done((bf16[256,128]{1,0:T(8,128)(2,1)S(1)}, bf16[256,128]{1,0:T(8,128)(2,1)S(1)}, u32[]{:S(2)}, u32[]{:S(2)}) %collective-permute-start.12) | collective-permute-done | bytes 65568 | tf_op jit(solution)/shard_map/ppermute | solution.py:563
  29.5 1.6 %collective-permute-done.11 = bf16[256,128]{1,0:T(8,128)(2,1)S(1)} collective-permute-done((bf16[256,128]{1,0:T(8,128)(2,1)S(1)}, bf16[256,128]{1,0:T(8,128)(2,1)S(1)}, u32[]{:S(2)}, u32[]{:S(2)}) %collective-permute-start.11) | collective-permute-done | bytes 65568 | tf_op jit(solution)/shard_map/ppermute | solution.py:563
  31.1 0.5 %collective-permute-done.10 = bf16[256,128]{1,0:T(8,128)(2,1)S(1)} collective-permute-done((bf16[256,128]{1,0:T(8,128)(2,1)S(1)}, bf16[256,128]{1,0:T(8,128)(2,1)S(1)}, u32[]{:S(2)}, u32[]{:S(2)}) %collective-permute-start.10) | collective-permute-done | bytes 65568 | tf_op jit(solution)/shard_map/ppermute | solution.py:563
  31.6 0.1 collective-permute-start.13
  31.7 1.1 %join.1 = (bf16[2,32,2,8,128]{4,3,2,1,0:T(8,128)(2,1)}, bf16[2,32,2,8,128]{4,3,2,1,0:T(8,128)(2,1)}) custom-call(bf16[2,2,4,32,128]{4,3,2,1,0:T(8,128)(2,1)S(1)} %get-tuple-element.35.refs_0_, bf16[2,2,4,32,128]{4,3,2,1,0:T(8,128)(2,1)S(1)} %collective-permute-done.3.refs_1_, bf16[2,2,4,32,128]{4,3,2,1,0:T(8,128)(2,1)S(1)} %collective-permute-done.4.refs_2_, ...), custom_call_target="tpu_custom_call" | custom-call | tf_op jit(solution)/shard_map/join/pallas_call | solution.py:686
  32.8 0.3 collective-permute-done.13.other_ref
  33.0 0.9 %unpack.1 = (f32[27,4,32]{2,1,0:T(4,128)}, f32[27,32,64]{2,1,0:T(8,128)}) custom-call(f32[256,128]{1,0:T(8,128)S(1)} %add_add_fusion.own_ref, f32[256,128]{1,0:T(8,128)S(1)} %collective-permute-done.13.other_ref), custom_call_target="tpu_custom_call" | custom-call | tf_op jit(solution)/shard_map/unpack/pallas_call | solution.py:694
  (7 shorter events, 0.1 us)
Async XLA Ops:
  1.9 8.7 %collective-permute-start.2 = (bf16[544,128]{1,0:T(8,128)(2,1)S(1)}, bf16[544,128]{1,0:T(8,128)(2,1)S(1)}, u32[]{:S(2)}, u32[]{:S(2)}) collective-permute-start(bf16[544,128]{1,0:T(8,128)(2,1)S(1)} %get-tuple-element.28), channel_id=1, source_target_pairs={{0,4},{1,5},{2,6},{3,7},{4,0},{5,1},{6,2},{7,3},{8,12},{9,13},{10,... | collective-permute-start | bytes 417800 | tf_op jit(solution)/shard_map/ppermute | solution.py:41
  4.9 4.2 %collective-permute-start = (bf16[224,128]{1,0:T(8,128)(2,1)S(1)}, bf16[224,128]{1,0:T(8,128)(2,1)S(1)}, u32[]{:S(2)}, u32[]{:S(2)}) collective-permute-start(bf16[224,128]{1,0:T(8,128)(2,1)S(1)} %get-tuple-element.26), channel_id=1, source_target_pairs={{0,16},{1,12},{2,13},{3,14},{4,20},{5,8},{6,9},{7,10},{8,5},{9,6},... | collective-permute-start | bytes 172040 | tf_op jit(solution)/shard_map/ppermute | solution.py:41
  6.4 4.2 %collective-permute-start.1 = (bf16[224,128]{1,0:T(8,128)(2,1)S(1)}, bf16[224,128]{1,0:T(8,128)(2,1)S(1)}, u32[]{:S(2)}, u32[]{:S(2)}) collective-permute-start(bf16[224,128]{1,0:T(8,128)(2,1)S(1)} %get-tuple-element.27), channel_id=1, source_target_pairs={{0,16},{1,8},{2,9},{3,10},{4,20},{5,12},{6,13},{7,14},{8,1},{9,2},... | collective-permute-start | bytes 172040 | tf_op jit(solution)/shard_map/ppermute | solution.py:41
  13.6 1.4 %collective-permute-start.6 = (bf16[224,128]{1,0:T(8,128)(2,1)S(1)}, bf16[224,128]{1,0:T(8,128)(2,1)S(1)}, u32[]{:S(2)}, u32[]{:S(2)}) collective-permute-start(bf16[224,128]{1,0:T(8,128)(2,1)S(1)} %get-tuple-element.40), channel_id=1, source_target_pairs={{0,8},{1,9},{2,10},{3,11},{4,12},{5,13},{6,14},{7,15},{8,0},{9,1},... | collective-permute-start | bytes 172040 | tf_op jit(solution)/shard_map/ppermute | solution.py:563
  15.1 6.0 %collective-permute-start.8 = (bf16[256,128]{1,0:T(8,128)(2,1)S(1)}, bf16[256,128]{1,0:T(8,128)(2,1)S(1)}, u32[]{:S(2)}, u32[]{:S(2)}) collective-permute-start(bf16[256,128]{1,0:T(8,128)(2,1)S(1)} %pad_maximum_fusion), channel_id=1, source_target_pairs={{0,2},{1,3},{2,0},{3,1},{4,6},{5,7},{6,4},{7,5},{8,12},{9,13},{10,... | collective-permute-start | bytes 196616 | tf_op jit(solution)/shard_map/ppermute | solution.py:563
  17.3 4.3 %collective-permute-start.7 = (bf16[256,128]{1,0:T(8,128)(2,1)S(1)}, bf16[256,128]{1,0:T(8,128)(2,1)S(1)}, u32[]{:S(2)}, u32[]{:S(2)}) collective-permute-start(bf16[256,128]{1,0:T(8,128)(2,1)S(1)} %pad_maximum_fusion), channel_id=1, source_target_pairs={{0,1},{1,0},{2,3},{3,2},{4,5},{5,4},{6,7},{7,6},{8,24},{9,25},{10,... | collective-permute-start | bytes 196616 | tf_op jit(solution)/shard_map/ppermute | solution.py:563
  18.2 6.1 %collective-permute-start.9 = (bf16[256,128]{1,0:T(8,128)(2,1)S(1)}, bf16[256,128]{1,0:T(8,128)(2,1)S(1)}, u32[]{:S(2)}, u32[]{:S(2)}) collective-permute-start(bf16[256,128]{1,0:T(8,128)(2,1)S(1)} %pad_maximum_fusion), channel_id=1, source_target_pairs={{0,3},{1,2},{2,1},{3,0},{4,7},{5,6},{6,5},{7,4},{8,28},{9,29},{10,... | collective-permute-start | bytes 196616 | tf_op jit(solution)/shard_map/ppermute | solution.py:563
  19.5 8.3 %collective-permute-start.3 = (bf16[2,2,4,32,128]{4,3,2,1,0:T(8,128)(2,1)S(1)}, bf16[2,2,4,32,128]{4,3,2,1,0:T(8,128)(2,1)S(1)}, u32[]{:S(2)}, u32[]{:S(2)}) collective-permute-start(bf16[2,2,4,32,128]{4,3,2,1,0:T(8,128)(2,1)S(1)} %get-tuple-element.36), channel_id=1, source_target_pairs={{0,4},{1,5},{2,6},{3,7},{4,0},{5,1},{6,2},{7,3},{8,12},{9,13},{10,... | collective-permute-start | bytes 393224 | tf_op jit(solution)/shard_map/ppermute | solution.py:563
  24.3 5.2 %collective-permute-start.12 = (bf16[256,128]{1,0:T(8,128)(2,1)S(1)}, bf16[256,128]{1,0:T(8,128)(2,1)S(1)}, u32[]{:S(2)}, u32[]{:S(2)}) collective-permute-start(bf16[256,128]{1,0:T(8,128)(2,1)S(1)} %add_convert_fusion), channel_id=1, source_target_pairs={{0,20},{1,21},{2,22},{3,23},{4,16},{5,17},{6,18},{7,19},{8,11},{9,... | collective-permute-start | bytes 196616 | tf_op jit(solution)/shard_map/ppermute | solution.py:563
  26.9 4.3 %collective-permute-start.11 = (bf16[256,128]{1,0:T(8,128)(2,1)S(1)}, bf16[256,128]{1,0:T(8,128)(2,1)S(1)}, u32[]{:S(2)}, u32[]{:S(2)}) collective-permute-start(bf16[256,128]{1,0:T(8,128)(2,1)S(1)} %add_convert_fusion), channel_id=1, source_target_pairs={{0,4},{1,5},{2,6},{3,7},{4,0},{5,1},{6,2},{7,3},{8,10},{9,11},{10,... | collective-permute-start | bytes 196616 | tf_op jit(solution)/shard_map/ppermute | solution.py:563
  27.3 4.3 %collective-permute-start.10 = (bf16[256,128]{1,0:T(8,128)(2,1)S(1)}, bf16[256,128]{1,0:T(8,128)(2,1)S(1)}, u32[]{:S(2)}, u32[]{:S(2)}) collective-permute-start(bf16[256,128]{1,0:T(8,128)(2,1)S(1)} %add_convert_fusion), channel_id=1, source_target_pairs={{0,16},{1,17},{2,18},{3,19},{4,20},{5,21},{6,22},{7,23},{8,9},{9,8... | collective-permute-start | bytes 196616 | tf_op jit(solution)/shard_map/ppermute | solution.py:563
  27.8 3.9 %collective-permute-start.4 = (bf16[2,2,4,32,128]{4,3,2,1,0:T(8,128)(2,1)S(1)}, bf16[2,2,4,32,128]{4,3,2,1,0:T(8,128)(2,1)S(1)}, u32[]{:S(2)}, u32[]{:S(2)}) collective-permute-start(bf16[2,2,4,32,128]{4,3,2,1,0:T(8,128)(2,1)S(1)} %get-tuple-element.35.refs_0_), channel_id=1, source_target_pairs={{0,8},{1,9},{2,10},{3,11},{4,12},{5,13},{6,14},{7,15},{8,0},{9,1},... | collective-permute-start | bytes 393224 | tf_op jit(solution)/shard_map/ppermute | solution.py:563
  27.8 3.9 %collective-permute-start.5 = (bf16[2,2,4,32,128]{4,3,2,1,0:T(8,128)(2,1)S(1)}, bf16[2,2,4,32,128]{4,3,2,1,0:T(8,128)(2,1)S(1)}, u32[]{:S(2)}, u32[]{:S(2)}) collective-permute-start(bf16[2,2,4,32,128]{4,3,2,1,0:T(8,128)(2,1)S(1)} %collective-permute-done.3.refs_1_), channel_id=1, source_target_pairs={{0,8},{1,9},{2,10},{3,11},{4,12},{5,13},{6,14},{7,15},{8,0},{9,1},... | collective-permute-start | bytes 393224 | tf_op jit(solution)/shard_map/ppermute | solution.py:563
  31.6 1.4 %collective-permute-start.13 = (f32[256,128]{1,0:T(8,128)S(1)}, f32[256,128]{1,0:T(8,128)S(1)}, u32[]{:S(2)}, u32[]{:S(2)}) collective-permute-start(f32[256,128]{1,0:T(8,128)S(1)} %add_add_fusion.own_ref), channel_id=1, source_target_pairs={{0,8},{1,9},{2,10},{3,11},{4,12},{5,13},{6,14},{7,15},{8,0},{9,1},... | collective-permute-start | bytes 393224 | tf_op jit(solution)/shard_map/ppermute | solution.py:563

commit v4 on v3

--- a/solution.py
+++ b/solution.py
@@ -8,6 +8,7 @@
 from jax.sharding import PartitionSpec as P
 
 LEAK = 0.3
+STEP = 3
 REACH = 3
 AXES = ("dp", "pipe", "gz", "gy")
 F32 = jnp.float32
@@ -43,6 +44,10 @@
     y_list = [(i, i) for i in range(plan.gy)] if y_kind is None else pairs(plan.gy, y_kind)
     perm = [(a * plan.gy + c, b * plan.gy + d) for a, b in z_list for c, d in y_list]
     return lax.ppermute(cells, ("gz", "gy"), perm)
+
+
+def aligned(at, step):
+    return at if isinstance(at, int) else pl.multiple_of(at, step)
 
 
 def shift(block, step, width):
@@ -129,21 +134,22 @@
     for v, volume in enumerate(first):
         loads.append(pltpu.make_async_copy(vol_hbm.at[volume], vol_ref.at[v], sems.at[2 * v]))
         loads.append(pltpu.make_async_copy(cot_hbm.at[volume], cot_ref.at[v], sems.at[2 * v + 1]))
-    for load in loads:
+    for load in loads[1::2] + loads[::2]:
         load.start()
     half = plan.c_two // 2
+    for v in range(len(first)):
+        loads[2 * v + 1].wait()
+        for z in range(plan.cz):
+            block = jnp.swapaxes(cot_ref[v, :, z].astype(F32), 0, 1)
+            for r in range(plan.cy):
+                row = jnp.concatenate([block[r][:half], block[r][half:]], axis=1)
+                cots[v, z, r] = row.astype(BF16)
     for v in range(len(first)):
         loads[2 * v].wait()
         for z in range(plan.z):
             block = jnp.swapaxes(vol_ref[v, :, z].astype(F32), 0, 1).astype(BF16)
             for y in range(plan.y):
                 cells[v, z, y] = block[y]
-        loads[2 * v + 1].wait()
-        for z in range(plan.cz):
-            block = jnp.swapaxes(cot_ref[v, :, z].astype(F32), 0, 1)
-            for r in range(plan.cy):
-                row = jnp.concatenate([block[r][:half], block[r][half:]], axis=1)
-                cots[v, z, r] = row.astype(BF16)
     for key, out_ref in zip(keys, out_refs):
         nz, ny, nc, nr = plan.blocks(key)
         z0 = c0 = y0 = r0 = 0
@@ -226,6 +232,14 @@
         ],
         axis=0,
     )
+
+
+def each(plan, count, body):
+    if plan.split:
+        for i in range(count):
+            body(i, 0)
+    else:
+        lax.fori_loop(0, count, body, 0)
 
 
 def forward_kernel(plan, count, *refs):
@@ -292,8 +306,7 @@
                 else:
                     lanes = [jnp.where(below, X, (Y + 2) * X)]
                 for lane in lanes:
-                    if not isinstance(lane, int):
-                        lane = pl.multiple_of(lane, X)
+                    lane = aligned(lane, X)
                     cot[c0 + i, :part, pl.ds(lane, X)] = row[:, :X]
                     cot[c0 + i, part:, pl.ds(lane, X)] = row[:, X:]
 
@@ -304,7 +317,7 @@
     is_c = (lax.broadcasted_iota(jnp.int32, (fold, X), 0) // c_in) % 2 == 1
 
     def spread(w, carry):
-        base = pl.multiple_of(8 * quarter + w * 16 * quarter, 8 * quarter)
+        base = aligned(8 * quarter + w * 16 * quarter, 8 * quarter)
         kept = []
         for r in range(plan.wide):
             mid = cells[w, row0 + r].astype(F32)
@@ -326,7 +339,7 @@
                     fine[pl.ds(row + 2 * quarter, 2 * quarter), lane : lane + X] = far.astype(BF16)
         return carry
 
-    lax.fori_loop(0, plan.win, spread, 0, unroll=True)
+    each(plan, plan.win, spread)
 
     w1 = w1_ref[...]
     last_q = plan.mid // 2 - 1
@@ -334,7 +347,7 @@
     act[plan.win + 1] = jnp.zeros(act.shape[1:], BF16)
 
     def first_section(w, carry):
-        top = pl.multiple_of(w * 16 * quarter, 8 * quarter)
+        top = aligned(w * 16 * quarter, 8 * quarter)
         z_abs = my_z * Z + w - own
         z_ok = None if plan.split else (z_abs >= 0) & (z_abs < plan.gz * Z)
         for q in range(plan.mid // 2):
@@ -359,7 +372,7 @@
             act[w + 1, :, lane : lane + 2 * X] = mean.astype(BF16)
         return carry
 
-    lax.fori_loop(0, plan.win, first_section, 0, unroll=True)
+    each(plan, plan.win, first_section)
 
     w2 = w2_ref[...]
     sg[0] = jnp.zeros(sg.shape[1:], BF16)
@@ -382,7 +395,7 @@
             sg[j + 1, :, lane : lane + 2 * X] = (slope * part).astype(BF16)
         return carry
 
-    lax.fori_loop(0, plan.planes, second_section, 0, unroll=True)
+    each(plan, plan.planes, second_section)
 
     grad_two = None
     for i in range(plan.o):
@@ -439,9 +452,7 @@
                 slope = (LEAK + 1.0) / 2 + ((1.0 - LEAK) / 2) * t
                 at = (i * R + 2 * q) * X
                 first[g * c_one : (g + 1) * c_one, at : at + 2 * X] = (slope * grad).astype(BF16)
-        top = w * 16 * quarter
-        if not isinstance(top, int):
-            top = pl.multiple_of(top, 8 * quarter)
+        top = aligned(w * 16 * quarter, 8 * quarter)
         tall.append(fine[pl.ds(top, 32 * quarter), 2 * X : (2 + R) * X])
     grad_one = lax.dot_general(
         jnp.concatenate(tall, axis=1),
@@ -512,7 +523,7 @@
                     out_ref[at, :, i] = jnp.swapaxes(lines, 0, 1).astype(BF16)
 
 
-def unpack_kernel(plan, own_ref, other_ref, one_ref, two_ref, full):
+def unpack_kernel(plan, own_ref, other_ref, one_hbm, two_hbm, one_ref, two_ref, full, sems):
     c_in, c_one, c_two = plan.c_in, plan.c_one, plan.c_two
     me = lax.axis_index("pipe")
     rows = full.shape[0] // 2
@@ -520,22 +531,31 @@
     full[pl.ds(pl.multiple_of(me * rows, rows), rows)] = own_ref[:rows] * scale
     full[pl.ds(pl.multiple_of((1 - me) * rows, rows), rows)] = other_ref[:rows] * scale
     nine = 9 * c_one
+    part = c_one // 2
+    stores = []
     for zy in range(9):
         block = full[zy * c_one : (zy + 1) * c_one]
         two_ref[zy * 3] = block[:, :c_two]
         two_ref[zy * 3 + 1] = block[:, c_two:]
-    part = c_one // 2
-    for p in range(18):
-        at = nine + (p % 9) * part
-        lane = (p // 9) * c_two
-        two_ref[(p // 2) * 3 + 2, (p % 2) * part : (p % 2 + 1) * part] = full[
-            at : at + part, lane : lane + c_two
-        ]
+        for p in (2 * zy, 2 * zy + 1):
+            at = nine + (p % 9) * part
+            lane = (p // 9) * c_two
+            two_ref[zy * 3 + 2, (p % 2) * part : (p % 2 + 1) * part] = full[
+                at : at + part, lane : lane + c_two
+            ]
+        if zy % STEP == STEP - 1:
+            at = pl.ds((zy - STEP + 1) * 3, 3 * STEP)
+            stores.append(pltpu.make_async_copy(two_ref.at[at], two_hbm.at[at], sems.at[len(stores)]))
+            stores[-1].start()
     ones = (own_ref[rows:] + other_ref[rows:]) * scale
     per = ones.shape[1] // c_one
     for t in range(27):
         row, lane = t // per * c_in, t % per * c_one
         one_ref[t] = ones[row : row + c_in, lane : lane + c_one]
+    stores.append(pltpu.make_async_copy(one_ref, one_hbm, sems.at[len(stores)]))
+    stores[-1].start()
+    for store in stores:
+        store.wait()
 
 
 def vmem(count):
@@ -695,8 +715,13 @@
         functools.partial(unpack_kernel, plan),
         out_shape=[shape((27, c_in, c_one), F32), shape((27, c_one, c_two), F32)],
         in_specs=vmem(2),
-        out_specs=vmem(2),
-        scratch_shapes=[pltpu.VMEM((2 * two_rows, wide), F32)],
+        out_specs=[pl.BlockSpec(memory_space=pltpu.HBM)] * 2,
+        scratch_shapes=[
+            pltpu.VMEM((27, c_in, c_one), F32),
+            pltpu.VMEM((27, c_one, c_two), F32),
+            pltpu.VMEM((2 * two_rows, wide), F32),
+            pltpu.SemaphoreType.DMA((9 // STEP + 1,)),
+        ],
         compiler_params=PARAMS,
         name="unpack",
     )(part, rest)

time: 34.1 us -> 34 us (level)
  no operation moved by 1% of the time
where the time goes in v4:
time: 34 us; the launch traced here: 33.9 us
  starting transfers between devices  14.7 us (43%)
  waiting for transfers between devices  9.48 us (28%)
  Pallas kernels  8.84 us (26%)
  between operations  0.73 us (2%)
    ppermute x11, starting transfers between devices, partner(): return lax.ppermute(part, AXES, perm)  9.7 us
    ppermute x11, waiting for transfers between devices, partner(): return lax.ppermute(part, AXES, perm)  7.13 us
    ppermute x3, starting transfers between devices, swap(): return lax.ppermute(cells, AXES, perm)  5.03 us
    pallas_call x1, Pallas kernels, per_device(): pl.pallas_call(functools.partial(forward_kernel, plan, len(msgs)), out_sh...  3 us
    ppermute x3, waiting for transfers between devices, swap(): return lax.ppermute(cells, AXES, perm)  2.35 us
    pallas_call x1, Pallas kernels, per_device(): pl.pallas_call(functools.partial(backward_kernel, plan), out_shape=[shape...  1.34 us
    pallas_call x1, Pallas kernels, per_device(): pl.pallas_call(functools.partial(weight_kernel, plan), out_shape=[shape((...  1.32 us
    pallas_call x1, Pallas kernels, per_device(): pl.pallas_call(functools.partial(pack_kernel, plan, keys), out_shape=[sha...  1.22 us
  transfers between devices with their start and end apart: 14, of which 9 were waited for; matrix products, arithmetic and copies ran while one was open for 0% of the time, Pallas kernels for 11%

profile of v4, /device:TPU:0, one launch (start us, length us, event | category | flops | bytes accessed | tf_op | source)
XLA Modules:
  0.0 33.9 jit_solution(7300713545737742084)
XLA Ops:
  0.6 1.2 %pack.1 = (bf16[224,128]{1,0:T(8,128)(2,1)S(1)}, bf16[544,128]{1,0:T(8,128)(2,1)S(1)}, bf16[224,128]{1,0:T(8,128)(2,1)S(1)}, bf16[640,128]{1,0:T(8,128)(2,1)S(1)}) custom-call(bf16[2,32,2,8,128]{4,3,2,1,0:T(8,128)(2,1)} %vol_hbm.1, bf16[2,64,1,4,64]{4,3,2,1,0:T(4,128)(2,1)} %cot_hbm.1), custom_call_target="tpu_custom_call" | custom-call | tf_op jit(solution)/shard_map/pack/pallas_call | solution.py:611
  1.9 3.0 %collective-permute-start.2 = (bf16[544,128]{1,0:T(8,128)(2,1)S(1)}, bf16[544,128]{1,0:T(8,128)(2,1)S(1)}, u32[]{:S(2)}, u32[]{:S(2)}) collective-permute-start(bf16[544,128]{1,0:T(8,128)(2,1)S(1)} %get-tuple-element.28), channel_id=1, source_target_pairs={{0,4},{1,5},{2,6},{3,7},{4,0},{5,1},{6,2},{7,3},{8,12},{9,13},{10,... | collective-permute-start | bytes 417800 | tf_op jit(solution)/shard_map/ppermute | solution.py:42
  4.9 1.5 %collective-permute-start = (bf16[224,128]{1,0:T(8,128)(2,1)S(1)}, bf16[224,128]{1,0:T(8,128)(2,1)S(1)}, u32[]{:S(2)}, u32[]{:S(2)}) collective-permute-start(bf16[224,128]{1,0:T(8,128)(2,1)S(1)} %get-tuple-element.26), channel_id=1, source_target_pairs={{0,16},{1,12},{2,13},{3,14},{4,20},{5,8},{6,9},{7,10},{8,5},{9,6},... | collective-permute-start | bytes 172040 | tf_op jit(solution)/shard_map/ppermute | solution.py:42
  6.4 0.5 %collective-permute-start.1 = (bf16[224,128]{1,0:T(8,128)(2,1)S(1)}, bf16[224,128]{1,0:T(8,128)(2,1)S(1)}, u32[]{:S(2)}, u32[]{:S(2)}) collective-permute-start(bf16[224,128]{1,0:T(8,128)(2,1)S(1)} %get-tuple-element.27), channel_id=1, source_target_pairs={{0,16},{1,8},{2,9},{3,10},{4,20},{5,12},{6,13},{7,14},{8,1},{9,2},... | collective-permute-start | bytes 172040 | tf_op jit(solution)/shard_map/ppermute | solution.py:42
  6.9 1.3 %weights.1 = (bf16[256,256]{1,0:T(8,128)(2,1)S(1)}, bf16[192,288]{1,0:T(8,128)(2,1)S(1)}, bf16[96,576]{1,0:T(8,128)(2,1)S(1)}) custom-call(bf16[27,4,32]{2,1,0:T(4,128)(2,1)} %bitcast.13, bf16[27,32,64]{2,1,0:T(8,128)(2,1)} %bitcast.12), custom_call_target="tpu_custom_call" | custom-call | flops 10000000 | bytes 1000000 | tf_op jit(solution)/shard_map/weights/pallas_call | solution.py:632
  8.2 0.8 %collective-permute-done.refs_1_ = bf16[224,128]{1,0:T(8,128)(2,1)S(1)} collective-permute-done((bf16[224,128]{1,0:T(8,128)(2,1)S(1)}, bf16[224,128]{1,0:T(8,128)(2,1)S(1)}, u32[]{:S(2)}, u32[]{:S(2)}) %collective-permute-start) | collective-permute-done | bytes 57376 | tf_op jit(solution)/shard_map/ppermute | solution.py:42
  9.0 1.5 %collective-permute-done.1.refs_2_ = bf16[224,128]{1,0:T(8,128)(2,1)S(1)} collective-permute-done((bf16[224,128]{1,0:T(8,128)(2,1)S(1)}, bf16[224,128]{1,0:T(8,128)(2,1)S(1)}, u32[]{:S(2)}, u32[]{:S(2)}) %collective-permute-start.1) | collective-permute-done | bytes 57376 | tf_op jit(solution)/shard_map/ppermute | solution.py:42
  10.6 0.0 collective-permute-done.2.refs_3_
  10.6 3.0 %forward.1 = (f32[224,128]{1,0:T(8,128)S(1)}, bf16[224,128]{1,0:T(8,128)(2,1)S(1)}, bf16[640,1024]{1,0:T(8,128)(2,1)S(1)}, bf16[6,32,1024]{2,1,0:T(8,128)(2,1)S(...) custom-call(bf16[640,128]{1,0:T(8,128)(2,1)S(1)} %get-tuple-element.25.refs_0_, ...), custom_call_target="tpu_custom_call" | custom-call | tf_op jit(solution)/shard_map/forward/pallas_call | solution.py:661
  13.6 0.1 collective-permute-start.6
  13.6 1.3 %backward.1 = (f32[32,128]{1,0:T(8,128)S(1)}, bf16[2,2,4,32,128]{4,3,2,1,0:T(8,128)(2,1)S(1)}, bf16[2,2,4,32,128]{4,3,2,1,0:T(8,128)(2,1)S(1)}) custom-call(bf16[96,576]{1,0:T(8,128)(2,1)S(1)} %get-tuple-element.24.wb_ref, bf16[640,1024]{1,0:T(8,128)(2,1)S(1)} %get-tuple-element.31.fine, bf16[6,32,1024]{2,1,0:T(8,128)(2,1)S(1)} %get-tuple-element.32.act, ...), custom_call_target="tpu_custom_call" | custom-call | flops 1000000000 | bytes 10000000 | tf_op jit(solution)/shard_map/backward/pallas_call | solution.py:686
  15.0 0.0 collective-permute-done.6
  15.0 2.2 %collective-permute-start.8 = (bf16[256,128]{1,0:T(8,128)(2,1)S(1)}, bf16[256,128]{1,0:T(8,128)(2,1)S(1)}, u32[]{:S(2)}, u32[]{:S(2)}) collective-permute-start(bf16[256,128]{1,0:T(8,128)(2,1)S(1)} %pad_maximum_fusion), channel_id=1, source_target_pairs={{0,2},{1,3},{2,0},{3,1},{4,6},{5,7},{6,4},{7,5},{8,12},{9,13},{10,... | collective-permute-start | bytes 196616 | tf_op jit(solution)/shard_map/ppermute | solution.py:583
  17.2 0.9 %collective-permute-start.7 = (bf16[256,128]{1,0:T(8,128)(2,1)S(1)}, bf16[256,128]{1,0:T(8,128)(2,1)S(1)}, u32[]{:S(2)}, u32[]{:S(2)}) collective-permute-start(bf16[256,128]{1,0:T(8,128)(2,1)S(1)} %pad_maximum_fusion), channel_id=1, source_target_pairs={{0,1},{1,0},{2,3},{3,2},{4,5},{5,4},{6,7},{7,6},{8,24},{9,25},{10,... | collective-permute-start | bytes 196616 | tf_op jit(solution)/shard_map/ppermute | solution.py:583
  18.1 1.4 %collective-permute-start.9 = (bf16[256,128]{1,0:T(8,128)(2,1)S(1)}, bf16[256,128]{1,0:T(8,128)(2,1)S(1)}, u32[]{:S(2)}, u32[]{:S(2)}) collective-permute-start(bf16[256,128]{1,0:T(8,128)(2,1)S(1)} %pad_maximum_fusion), channel_id=1, source_target_pairs={{0,3},{1,2},{2,1},{3,0},{4,7},{5,6},{6,5},{7,4},{8,28},{9,29},{10,... | collective-permute-start | bytes 196616 | tf_op jit(solution)/shard_map/ppermute | solution.py:583
  19.5 1.0 %collective-permute-start.3 = (bf16[2,2,4,32,128]{4,3,2,1,0:T(8,128)(2,1)S(1)}, bf16[2,2,4,32,128]{4,3,2,1,0:T(8,128)(2,1)S(1)}, u32[]{:S(2)}, u32[]{:S(2)}) collective-permute-start(bf16[2,2,4,32,128]{4,3,2,1,0:T(8,128)(2,1)S(1)} %get-tuple-element.36), channel_id=1, source_target_pairs={{0,4},{1,5},{2,6},{3,7},{4,0},{5,1},{6,2},{7,3},{8,12},{9,13},{10,... | collective-permute-start | bytes 393224 | tf_op jit(solution)/shard_map/ppermute | solution.py:583
  20.5 0.5 %collective-permute-done.8 = bf16[256,128]{1,0:T(8,128)(2,1)S(1)} collective-permute-done((bf16[256,128]{1,0:T(8,128)(2,1)S(1)}, bf16[256,128]{1,0:T(8,128)(2,1)S(1)}, u32[]{:S(2)}, u32[]{:S(2)}) %collective-permute-start.8) | collective-permute-done | bytes 65568 | tf_op jit(solution)/shard_map/ppermute | solution.py:583
  21.1 0.5 %collective-permute-done.7 = bf16[256,128]{1,0:T(8,128)(2,1)S(1)} collective-permute-done((bf16[256,128]{1,0:T(8,128)(2,1)S(1)}, bf16[256,128]{1,0:T(8,128)(2,1)S(1)}, u32[]{:S(2)}, u32[]{:S(2)}) %collective-permute-start.7) | collective-permute-done | bytes 65568 | tf_op jit(solution)/shard_map/ppermute | solution.py:583
  21.6 2.6 %collective-permute-done.9 = bf16[256,128]{1,0:T(8,128)(2,1)S(1)} collective-permute-done((bf16[256,128]{1,0:T(8,128)(2,1)S(1)}, bf16[256,128]{1,0:T(8,128)(2,1)S(1)}, u32[]{:S(2)}, u32[]{:S(2)}) %collective-permute-start.9) | collective-permute-done | bytes 65568 | tf_op jit(solution)/shard_map/ppermute | solution.py:583
  24.2 2.6 %collective-permute-start.12 = (bf16[256,128]{1,0:T(8,128)(2,1)S(1)}, bf16[256,128]{1,0:T(8,128)(2,1)S(1)}, u32[]{:S(2)}, u32[]{:S(2)}) collective-permute-start(bf16[256,128]{1,0:T(8,128)(2,1)S(1)} %add_convert_fusion), channel_id=1, source_target_pairs={{0,20},{1,21},{2,22},{3,23},{4,16},{5,17},{6,18},{7,19},{8,11},{9,... | collective-permute-start | bytes 196616 | tf_op jit(solution)/shard_map/ppermute | solution.py:583
  26.8 0.5 %collective-permute-start.11 = (bf16[256,128]{1,0:T(8,128)(2,1)S(1)}, bf16[256,128]{1,0:T(8,128)(2,1)S(1)}, u32[]{:S(2)}, u32[]{:S(2)}) collective-permute-start(bf16[256,128]{1,0:T(8,128)(2,1)S(1)} %add_convert_fusion), channel_id=1, source_target_pairs={{0,4},{1,5},{2,6},{3,7},{4,0},{5,1},{6,2},{7,3},{8,10},{9,11},{10,... | collective-permute-start | bytes 196616 | tf_op jit(solution)/shard_map/ppermute | solution.py:583
  27.3 0.5 %collective-permute-start.10 = (bf16[256,128]{1,0:T(8,128)(2,1)S(1)}, bf16[256,128]{1,0:T(8,128)(2,1)S(1)}, u32[]{:S(2)}, u32[]{:S(2)}) collective-permute-start(bf16[256,128]{1,0:T(8,128)(2,1)S(1)} %add_convert_fusion), channel_id=1, source_target_pairs={{0,16},{1,17},{2,18},{3,19},{4,20},{5,21},{6,22},{7,23},{8,9},{9,8... | collective-permute-start | bytes 196616 | tf_op jit(solution)/shard_map/ppermute | solution.py:583
  27.8 0.0 collective-permute-start.4
  27.8 0.0 collective-permute-done.3.refs_1_
  27.8 0.5 %collective-permute-start.5 = (bf16[2,2,4,32,128]{4,3,2,1,0:T(8,128)(2,1)S(1)}, bf16[2,2,4,32,128]{4,3,2,1,0:T(8,128)(2,1)S(1)}, u32[]{:S(2)}, u32[]{:S(2)}) collective-permute-start(bf16[2,2,4,32,128]{4,3,2,1,0:T(8,128)(2,1)S(1)} %collective-permute-done.3.refs_1_), channel_id=1, source_target_pairs={{0,8},{1,9},{2,10},{3,11},{4,12},{5,13},{6,14},{7,15},{8,0},{9,1},... | collective-permute-start | bytes 393224 | tf_op jit(solution)/shard_map/ppermute | solution.py:583
  28.3 1.2 %collective-permute-done.12 = bf16[256,128]{1,0:T(8,128)(2,1)S(1)} collective-permute-done((bf16[256,128]{1,0:T(8,128)(2,1)S(1)}, bf16[256,128]{1,0:T(8,128)(2,1)S(1)}, u32[]{:S(2)}, u32[]{:S(2)}) %collective-permute-start.12) | collective-permute-done | bytes 65568 | tf_op jit(solution)/shard_map/ppermute | solution.py:583
  29.5 1.6 %collective-permute-done.11 = bf16[256,128]{1,0:T(8,128)(2,1)S(1)} collective-permute-done((bf16[256,128]{1,0:T(8,128)(2,1)S(1)}, bf16[256,128]{1,0:T(8,128)(2,1)S(1)}, u32[]{:S(2)}, u32[]{:S(2)}) %collective-permute-start.11) | collective-permute-done | bytes 65568 | tf_op jit(solution)/shard_map/ppermute | solution.py:583
  31.1 0.5 %collective-permute-done.10 = bf16[256,128]{1,0:T(8,128)(2,1)S(1)} collective-permute-done((bf16[256,128]{1,0:T(8,128)(2,1)S(1)}, bf16[256,128]{1,0:T(8,128)(2,1)S(1)}, u32[]{:S(2)}, u32[]{:S(2)}) %collective-permute-start.10) | collective-permute-done | bytes 65568 | tf_op jit(solution)/shard_map/ppermute | solution.py:583
  31.6 0.1 collective-permute-start.13
  31.7 1.1 %join.1 = (bf16[2,32,2,8,128]{4,3,2,1,0:T(8,128)(2,1)}, bf16[2,32,2,8,128]{4,3,2,1,0:T(8,128)(2,1)}) custom-call(bf16[2,2,4,32,128]{4,3,2,1,0:T(8,128)(2,1)S(1)} %get-tuple-element.35.refs_0_, bf16[2,2,4,32,128]{4,3,2,1,0:T(8,128)(2,1)S(1)} %collective-permute-done.3.refs_1_, bf16[2,2,4,32,128]{4,3,2,1,0:T(8,128)(2,1)S(1)} %collective-permute-done.4.refs_2_, ...), custom_call_target="tpu_custom_call" | custom-call | tf_op jit(solution)/shard_map/join/pallas_call | solution.py:706
  32.7 0.3 collective-permute-done.13.other_ref
  33.0 0.9 %unpack.1 = (f32[27,4,32]{2,1,0:T(4,128)}, f32[27,32,64]{2,1,0:T(8,128)}) custom-call(f32[256,128]{1,0:T(8,128)S(1)} %add_add_fusion.own_ref, f32[256,128]{1,0:T(8,128)S(1)} %collective-permute-done.13.other_ref), custom_call_target="tpu_custom_call" | custom-call | tf_op jit(solution)/shard_map/unpack/pallas_call | solution.py:714
  (7 shorter events, 0.1 us)
Async XLA Ops:
  1.9 8.7 %collective-permute-start.2 = (bf16[544,128]{1,0:T(8,128)(2,1)S(1)}, bf16[544,128]{1,0:T(8,128)(2,1)S(1)}, u32[]{:S(2)}, u32[]{:S(2)}) collective-permute-start(bf16[544,128]{1,0:T(8,128)(2,1)S(1)} %get-tuple-element.28), channel_id=1, source_target_pairs={{0,4},{1,5},{2,6},{3,7},{4,0},{5,1},{6,2},{7,3},{8,12},{9,13},{10,... | collective-permute-start | bytes 417800 | tf_op jit(solution)/shard_map/ppermute | solution.py:42
  4.9 4.2 %collective-permute-start = (bf16[224,128]{1,0:T(8,128)(2,1)S(1)}, bf16[224,128]{1,0:T(8,128)(2,1)S(1)}, u32[]{:S(2)}, u32[]{:S(2)}) collective-permute-start(bf16[224,128]{1,0:T(8,128)(2,1)S(1)} %get-tuple-element.26), channel_id=1, source_target_pairs={{0,16},{1,12},{2,13},{3,14},{4,20},{5,8},{6,9},{7,10},{8,5},{9,6},... | collective-permute-start | bytes 172040 | tf_op jit(solution)/shard_map/ppermute | solution.py:42
  6.4 4.2 %collective-permute-start.1 = (bf16[224,128]{1,0:T(8,128)(2,1)S(1)}, bf16[224,128]{1,0:T(8,128)(2,1)S(1)}, u32[]{:S(2)}, u32[]{:S(2)}) collective-permute-start(bf16[224,128]{1,0:T(8,128)(2,1)S(1)} %get-tuple-element.27), channel_id=1, source_target_pairs={{0,16},{1,8},{2,9},{3,10},{4,20},{5,12},{6,13},{7,14},{8,1},{9,2},... | collective-permute-start | bytes 172040 | tf_op jit(solution)/shard_map/ppermute | solution.py:42
  13.6 1.4 %collective-permute-start.6 = (bf16[224,128]{1,0:T(8,128)(2,1)S(1)}, bf16[224,128]{1,0:T(8,128)(2,1)S(1)}, u32[]{:S(2)}, u32[]{:S(2)}) collective-permute-start(bf16[224,128]{1,0:T(8,128)(2,1)S(1)} %get-tuple-element.40), channel_id=1, source_target_pairs={{0,8},{1,9},{2,10},{3,11},{4,12},{5,13},{6,14},{7,15},{8,0},{9,1},... | collective-permute-start | bytes 172040 | tf_op jit(solution)/shard_map/ppermute | solution.py:583
  15.0 6.0 %collective-permute-start.8 = (bf16[256,128]{1,0:T(8,128)(2,1)S(1)}, bf16[256,128]{1,0:T(8,128)(2,1)S(1)}, u32[]{:S(2)}, u32[]{:S(2)}) collective-permute-start(bf16[256,128]{1,0:T(8,128)(2,1)S(1)} %pad_maximum_fusion), channel_id=1, source_target_pairs={{0,2},{1,3},{2,0},{3,1},{4,6},{5,7},{6,4},{7,5},{8,12},{9,13},{10,... | collective-permute-start | bytes 196616 | tf_op jit(solution)/shard_map/ppermute | solution.py:583
  17.2 4.3 %collective-permute-start.7 = (bf16[256,128]{1,0:T(8,128)(2,1)S(1)}, bf16[256,128]{1,0:T(8,128)(2,1)S(1)}, u32[]{:S(2)}, u32[]{:S(2)}) collective-permute-start(bf16[256,128]{1,0:T(8,128)(2,1)S(1)} %pad_maximum_fusion), channel_id=1, source_target_pairs={{0,1},{1,0},{2,3},{3,2},{4,5},{5,4},{6,7},{7,6},{8,24},{9,25},{10,... | collective-permute-start | bytes 196616 | tf_op jit(solution)/shard_map/ppermute | solution.py:583
  18.1 6.1 %collective-permute-start.9 = (bf16[256,128]{1,0:T(8,128)(2,1)S(1)}, bf16[256,128]{1,0:T(8,128)(2,1)S(1)}, u32[]{:S(2)}, u32[]{:S(2)}) collective-permute-start(bf16[256,128]{1,0:T(8,128)(2,1)S(1)} %pad_maximum_fusion), channel_id=1, source_target_pairs={{0,3},{1,2},{2,1},{3,0},{4,7},{5,6},{6,5},{7,4},{8,28},{9,29},{10,... | collective-permute-start | bytes 196616 | tf_op jit(solution)/shard_map/ppermute | solution.py:583
  19.5 8.3 %collective-permute-start.3 = (bf16[2,2,4,32,128]{4,3,2,1,0:T(8,128)(2,1)S(1)}, bf16[2,2,4,32,128]{4,3,2,1,0:T(8,128)(2,1)S(1)}, u32[]{:S(2)}, u32[]{:S(2)}) collective-permute-start(bf16[2,2,4,32,128]{4,3,2,1,0:T(8,128)(2,1)S(1)} %get-tuple-element.36), channel_id=1, source_target_pairs={{0,4},{1,5},{2,6},{3,7},{4,0},{5,1},{6,2},{7,3},{8,12},{9,13},{10,... | collective-permute-start | bytes 393224 | tf_op jit(solution)/shard_map/ppermute | solution.py:583
  24.2 5.2 %collective-permute-start.12 = (bf16[256,128]{1,0:T(8,128)(2,1)S(1)}, bf16[256,128]{1,0:T(8,128)(2,1)S(1)}, u32[]{:S(2)}, u32[]{:S(2)}) collective-permute-start(bf16[256,128]{1,0:T(8,128)(2,1)S(1)} %add_convert_fusion), channel_id=1, source_target_pairs={{0,20},{1,21},{2,22},{3,23},{4,16},{5,17},{6,18},{7,19},{8,11},{9,... | collective-permute-start | bytes 196616 | tf_op jit(solution)/shard_map/ppermute | solution.py:583
  26.8 4.3 %collective-permute-start.11 = (bf16[256,128]{1,0:T(8,128)(2,1)S(1)}, bf16[256,128]{1,0:T(8,128)(2,1)S(1)}, u32[]{:S(2)}, u32[]{:S(2)}) collective-permute-start(bf16[256,128]{1,0:T(8,128)(2,1)S(1)} %add_convert_fusion), channel_id=1, source_target_pairs={{0,4},{1,5},{2,6},{3,7},{4,0},{5,1},{6,2},{7,3},{8,10},{9,11},{10,... | collective-permute-start | bytes 196616 | tf_op jit(solution)/shard_map/ppermute | solution.py:583
  27.3 4.3 %collective-permute-start.10 = (bf16[256,128]{1,0:T(8,128)(2,1)S(1)}, bf16[256,128]{1,0:T(8,128)(2,1)S(1)}, u32[]{:S(2)}, u32[]{:S(2)}) collective-permute-start(bf16[256,128]{1,0:T(8,128)(2,1)S(1)} %add_convert_fusion), channel_id=1, source_target_pairs={{0,16},{1,17},{2,18},{3,19},{4,20},{5,21},{6,22},{7,23},{8,9},{9,8... | collective-permute-start | bytes 196616 | tf_op jit(solution)/shard_map/ppermute | solution.py:583
  27.8 3.9 %collective-permute-start.4 = (bf16[2,2,4,32,128]{4,3,2,1,0:T(8,128)(2,1)S(1)}, bf16[2,2,4,32,128]{4,3,2,1,0:T(8,128)(2,1)S(1)}, u32[]{:S(2)}, u32[]{:S(2)}) collective-permute-start(bf16[2,2,4,32,128]{4,3,2,1,0:T(8,128)(2,1)S(1)} %get-tuple-element.35.refs_0_), channel_id=1, source_target_pairs={{0,8},{1,9},{2,10},{3,11},{4,12},{5,13},{6,14},{7,15},{8,0},{9,1},... | collective-permute-start | bytes 393224 | tf_op jit(solution)/shard_map/ppermute | solution.py:583
  27.8 3.9 %collective-permute-start.5 = (bf16[2,2,4,32,128]{4,3,2,1,0:T(8,128)(2,1)S(1)}, bf16[2,2,4,32,128]{4,3,2,1,0:T(8,128)(2,1)S(1)}, u32[]{:S(2)}, u32[]{:S(2)}) collective-permute-start(bf16[2,2,4,32,128]{4,3,2,1,0:T(8,128)(2,1)S(1)} %collective-permute-done.3.refs_1_), channel_id=1, source_target_pairs={{0,8},{1,9},{2,10},{3,11},{4,12},{5,13},{6,14},{7,15},{8,0},{9,1},... | collective-permute-start | bytes 393224 | tf_op jit(solution)/shard_map/ppermute | solution.py:583
  31.6 1.4 %collective-permute-start.13 = (f32[256,128]{1,0:T(8,128)S(1)}, f32[256,128]{1,0:T(8,128)S(1)}, u32[]{:S(2)}, u32[]{:S(2)}) collective-permute-start(f32[256,128]{1,0:T(8,128)S(1)} %add_add_fusion.own_ref), channel_id=1, source_target_pairs={{0,8},{1,9},{2,10},{3,11},{4,12},{5,13},{6,14},{7,15},{8,0},{9,1},... | collective-permute-start | bytes 393224 | tf_op jit(solution)/shard_map/ppermute | solution.py:583

commit v5 on v4

--- a/solution.py
+++ b/solution.py
@@ -381,18 +381,16 @@
     def second_section(j, carry):
         w = first_sg + j
         c_at = (w - own + 2) // 2
-        for q in range(plan.slim // 2):
-            lane = 2 * q * X
-            taps = jnp.dot(w2, around(act, w, lane + X, 2 * X, X, 1), preferred_element_type=F32)
-            half = (
-                taps[c_two : 2 * c_two]
-                + shift(taps[:c_two], 1, X)
-                + shift(taps[2 * c_two :], -1, X)
-            )
-            slope = (LEAK + 1.0) / 2 + ((1.0 - LEAK) / 2) * jnp.tanh(half)
-            near = pl.multiple_of((row0 + 1) * X + lane, X)
-            part = cot[c_at, :, pl.ds(near, 2 * X)].astype(F32)
-            sg[j + 1, :, lane : lane + 2 * X] = (slope * part).astype(BF16)
+        taps = jnp.dot(w2, around(act, w, X, plan.slim * X, X, 1), preferred_element_type=F32)
+        half = (
+            taps[c_two : 2 * c_two]
+            + shift(taps[:c_two], 1, X)
+            + shift(taps[2 * c_two :], -1, X)
+        )
+        slope = (LEAK + 1.0) / 2 + ((1.0 - LEAK) / 2) * jnp.tanh(half)
+        near = pl.multiple_of((row0 + 1) * X, X)
+        part = cot[c_at, :, pl.ds(near, plan.slim * X)].astype(F32)
+        sg[j + 1] = (slope * part).astype(BF16)
         return carry
 
     each(plan, plan.planes, second_section)

time: 34 us -> 34 us (level)
  no operation moved by 1% of the time
where the time goes in v5:
time: 34 us; the launch traced here: 33.9 us
  starting transfers between devices  14.7 us (43%)
  waiting for transfers between devices  9.48 us (28%)
  Pallas kernels  8.81 us (26%)
  between operations  0.73 us (2%)
    ppermute x11, starting transfers between devices, partner(): return lax.ppermute(part, AXES, perm)  9.7 us
    ppermute x11, waiting for transfers between devices, partner(): return lax.ppermute(part, AXES, perm)  7.14 us
    ppermute x3, starting transfers between devices, swap(): return lax.ppermute(cells, AXES, perm)  5.03 us
    pallas_call x1, Pallas kernels, per_device(): pl.pallas_call(functools.partial(forward_kernel, plan, len(msgs)), out_sh...  2.96 us
    ppermute x3, waiting for transfers between devices, swap(): return lax.ppermute(cells, AXES, perm)  2.35 us
    pallas_call x1, Pallas kernels, per_device(): pl.pallas_call(functools.partial(backward_kernel, plan), out_shape=[shape...  1.35 us
    pallas_call x1, Pallas kernels, per_device(): pl.pallas_call(functools.partial(weight_kernel, plan), out_shape=[shape((...  1.32 us
    pallas_call x1, Pallas kernels, per_device(): pl.pallas_call(functools.partial(pack_kernel, plan, keys), out_shape=[sha...  1.22 us
  transfers between devices with their start and end apart: 14, of which 9 were waited for; matrix products, arithmetic and copies ran while one was open for 0% of the time, Pallas kernels for 11%

profile of v5, /device:TPU:0, one launch (start us, length us, event | category | flops | bytes accessed | tf_op | source)
XLA Modules:
  0.0 33.9 jit_solution(16376294955832478808)
XLA Ops:
  0.6 1.2 %pack.1 = (bf16[224,128]{1,0:T(8,128)(2,1)S(1)}, bf16[544,128]{1,0:T(8,128)(2,1)S(1)}, bf16[224,128]{1,0:T(8,128)(2,1)S(1)}, bf16[640,128]{1,0:T(8,128)(2,1)S(1)}) custom-call(bf16[2,32,2,8,128]{4,3,2,1,0:T(8,128)(2,1)} %vol_hbm.1, bf16[2,64,1,4,64]{4,3,2,1,0:T(4,128)(2,1)} %cot_hbm.1), custom_call_target="tpu_custom_call" | custom-call | tf_op jit(solution)/shard_map/pack/pallas_call | solution.py:609
  1.9 3.0 %collective-permute-start.2 = (bf16[544,128]{1,0:T(8,128)(2,1)S(1)}, bf16[544,128]{1,0:T(8,128)(2,1)S(1)}, u32[]{:S(2)}, u32[]{:S(2)}) collective-permute-start(bf16[544,128]{1,0:T(8,128)(2,1)S(1)} %get-tuple-element.28), channel_id=1, source_target_pairs={{0,4},{1,5},{2,6},{3,7},{4,0},{5,1},{6,2},{7,3},{8,12},{9,13},{10,... | collective-permute-start | bytes 417800 | tf_op jit(solution)/shard_map/ppermute | solution.py:42
  4.9 1.5 %collective-permute-start = (bf16[224,128]{1,0:T(8,128)(2,1)S(1)}, bf16[224,128]{1,0:T(8,128)(2,1)S(1)}, u32[]{:S(2)}, u32[]{:S(2)}) collective-permute-start(bf16[224,128]{1,0:T(8,128)(2,1)S(1)} %get-tuple-element.26), channel_id=1, source_target_pairs={{0,16},{1,12},{2,13},{3,14},{4,20},{5,8},{6,9},{7,10},{8,5},{9,6},... | collective-permute-start | bytes 172040 | tf_op jit(solution)/shard_map/ppermute | solution.py:42
  6.4 0.5 %collective-permute-start.1 = (bf16[224,128]{1,0:T(8,128)(2,1)S(1)}, bf16[224,128]{1,0:T(8,128)(2,1)S(1)}, u32[]{:S(2)}, u32[]{:S(2)}) collective-permute-start(bf16[224,128]{1,0:T(8,128)(2,1)S(1)} %get-tuple-element.27), channel_id=1, source_target_pairs={{0,16},{1,8},{2,9},{3,10},{4,20},{5,12},{6,13},{7,14},{8,1},{9,2},... | collective-permute-start | bytes 172040 | tf_op jit(solution)/shard_map/ppermute | solution.py:42
  6.9 1.3 %weights.1 = (bf16[256,256]{1,0:T(8,128)(2,1)S(1)}, bf16[192,288]{1,0:T(8,128)(2,1)S(1)}, bf16[96,576]{1,0:T(8,128)(2,1)S(1)}) custom-call(bf16[27,4,32]{2,1,0:T(4,128)(2,1)} %bitcast.13, bf16[27,32,64]{2,1,0:T(8,128)(2,1)} %bitcast.12), custom_call_target="tpu_custom_call" | custom-call | flops 10000000 | bytes 1000000 | tf_op jit(solution)/shard_map/weights/pallas_call | solution.py:630
  8.2 0.8 %collective-permute-done.refs_1_ = bf16[224,128]{1,0:T(8,128)(2,1)S(1)} collective-permute-done((bf16[224,128]{1,0:T(8,128)(2,1)S(1)}, bf16[224,128]{1,0:T(8,128)(2,1)S(1)}, u32[]{:S(2)}, u32[]{:S(2)}) %collective-permute-start) | collective-permute-done | bytes 57376 | tf_op jit(solution)/shard_map/ppermute | solution.py:42
  9.0 1.5 %collective-permute-done.1.refs_2_ = bf16[224,128]{1,0:T(8,128)(2,1)S(1)} collective-permute-done((bf16[224,128]{1,0:T(8,128)(2,1)S(1)}, bf16[224,128]{1,0:T(8,128)(2,1)S(1)}, u32[]{:S(2)}, u32[]{:S(2)}) %collective-permute-start.1) | collective-permute-done | bytes 57376 | tf_op jit(solution)/shard_map/ppermute | solution.py:42
  10.6 0.0 collective-permute-done.2.refs_3_
  10.6 3.0 %forward.1 = (f32[224,128]{1,0:T(8,128)S(1)}, bf16[224,128]{1,0:T(8,128)(2,1)S(1)}, bf16[640,1024]{1,0:T(8,128)(2,1)S(1)}, bf16[6,32,1024]{2,1,0:T(8,128)(2,1)S(...) custom-call(bf16[640,128]{1,0:T(8,128)(2,1)S(1)} %get-tuple-element.25.refs_0_, ...), custom_call_target="tpu_custom_call" | custom-call | tf_op jit(solution)/shard_map/forward/pallas_call | solution.py:659
  13.5 0.1 collective-permute-start.6
  13.6 1.3 %backward.1 = (f32[32,128]{1,0:T(8,128)S(1)}, bf16[2,2,4,32,128]{4,3,2,1,0:T(8,128)(2,1)S(1)}, bf16[2,2,4,32,128]{4,3,2,1,0:T(8,128)(2,1)S(1)}) custom-call(bf16[96,576]{1,0:T(8,128)(2,1)S(1)} %get-tuple-element.24.wb_ref, bf16[640,1024]{1,0:T(8,128)(2,1)S(1)} %get-tuple-element.31.fine, bf16[6,32,1024]{2,1,0:T(8,128)(2,1)S(1)} %get-tuple-element.32.act, ...), custom_call_target="tpu_custom_call" | custom-call | flops 1000000000 | bytes 10000000 | tf_op jit(solution)/shard_map/backward/pallas_call | solution.py:684
  15.0 0.0 collective-permute-done.6
  15.0 2.2 %collective-permute-start.8 = (bf16[256,128]{1,0:T(8,128)(2,1)S(1)}, bf16[256,128]{1,0:T(8,128)(2,1)S(1)}, u32[]{:S(2)}, u32[]{:S(2)}) collective-permute-start(bf16[256,128]{1,0:T(8,128)(2,1)S(1)} %pad_maximum_fusion), channel_id=1, source_target_pairs={{0,2},{1,3},{2,0},{3,1},{4,6},{5,7},{6,4},{7,5},{8,12},{9,13},{10,... | collective-permute-start | bytes 196616 | tf_op jit(solution)/shard_map/ppermute | solution.py:581
  17.2 0.9 %collective-permute-start.7 = (bf16[256,128]{1,0:T(8,128)(2,1)S(1)}, bf16[256,128]{1,0:T(8,128)(2,1)S(1)}, u32[]{:S(2)}, u32[]{:S(2)}) collective-permute-start(bf16[256,128]{1,0:T(8,128)(2,1)S(1)} %pad_maximum_fusion), channel_id=1, source_target_pairs={{0,1},{1,0},{2,3},{3,2},{4,5},{5,4},{6,7},{7,6},{8,24},{9,25},{10,... | collective-permute-start | bytes 196616 | tf_op jit(solution)/shard_map/ppermute | solution.py:581
  18.1 1.4 %collective-permute-start.9 = (bf16[256,128]{1,0:T(8,128)(2,1)S(1)}, bf16[256,128]{1,0:T(8,128)(2,1)S(1)}, u32[]{:S(2)}, u32[]{:S(2)}) collective-permute-start(bf16[256,128]{1,0:T(8,128)(2,1)S(1)} %pad_maximum_fusion), channel_id=1, source_target_pairs={{0,3},{1,2},{2,1},{3,0},{4,7},{5,6},{6,5},{7,4},{8,28},{9,29},{10,... | collective-permute-start | bytes 196616 | tf_op jit(solution)/shard_map/ppermute | solution.py:581
  19.5 1.0 %collective-permute-start.3 = (bf16[2,2,4,32,128]{4,3,2,1,0:T(8,128)(2,1)S(1)}, bf16[2,2,4,32,128]{4,3,2,1,0:T(8,128)(2,1)S(1)}, u32[]{:S(2)}, u32[]{:S(2)}) collective-permute-start(bf16[2,2,4,32,128]{4,3,2,1,0:T(8,128)(2,1)S(1)} %get-tuple-element.36), channel_id=1, source_target_pairs={{0,4},{1,5},{2,6},{3,7},{4,0},{5,1},{6,2},{7,3},{8,12},{9,13},{10,... | collective-permute-start | bytes 393224 | tf_op jit(solution)/shard_map/ppermute | solution.py:581
  20.5 0.5 %collective-permute-done.8 = bf16[256,128]{1,0:T(8,128)(2,1)S(1)} collective-permute-done((bf16[256,128]{1,0:T(8,128)(2,1)S(1)}, bf16[256,128]{1,0:T(8,128)(2,1)S(1)}, u32[]{:S(2)}, u32[]{:S(2)}) %collective-permute-start.8) | collective-permute-done | bytes 65568 | tf_op jit(solution)/shard_map/ppermute | solution.py:581
  21.0 0.5 %collective-permute-done.7 = bf16[256,128]{1,0:T(8,128)(2,1)S(1)} collective-permute-done((bf16[256,128]{1,0:T(8,128)(2,1)S(1)}, bf16[256,128]{1,0:T(8,128)(2,1)S(1)}, u32[]{:S(2)}, u32[]{:S(2)}) %collective-permute-start.7) | collective-permute-done | bytes 65568 | tf_op jit(solution)/shard_map/ppermute | solution.py:581
  21.5 2.6 %collective-permute-done.9 = bf16[256,128]{1,0:T(8,128)(2,1)S(1)} collective-permute-done((bf16[256,128]{1,0:T(8,128)(2,1)S(1)}, bf16[256,128]{1,0:T(8,128)(2,1)S(1)}, u32[]{:S(2)}, u32[]{:S(2)}) %collective-permute-start.9) | collective-permute-done | bytes 65568 | tf_op jit(solution)/shard_map/ppermute | solution.py:581
  24.2 2.6 %collective-permute-start.12 = (bf16[256,128]{1,0:T(8,128)(2,1)S(1)}, bf16[256,128]{1,0:T(8,128)(2,1)S(1)}, u32[]{:S(2)}, u32[]{:S(2)}) collective-permute-start(bf16[256,128]{1,0:T(8,128)(2,1)S(1)} %add_convert_fusion), channel_id=1, source_target_pairs={{0,20},{1,21},{2,22},{3,23},{4,16},{5,17},{6,18},{7,19},{8,11},{9,... | collective-permute-start | bytes 196616 | tf_op jit(solution)/shard_map/ppermute | solution.py:581
  26.8 0.5 %collective-permute-start.11 = (bf16[256,128]{1,0:T(8,128)(2,1)S(1)}, bf16[256,128]{1,0:T(8,128)(2,1)S(1)}, u32[]{:S(2)}, u32[]{:S(2)}) collective-permute-start(bf16[256,128]{1,0:T(8,128)(2,1)S(1)} %add_convert_fusion), channel_id=1, source_target_pairs={{0,4},{1,5},{2,6},{3,7},{4,0},{5,1},{6,2},{7,3},{8,10},{9,11},{10,... | collective-permute-start | bytes 196616 | tf_op jit(solution)/shard_map/ppermute | solution.py:581
  27.2 0.5 %collective-permute-start.10 = (bf16[256,128]{1,0:T(8,128)(2,1)S(1)}, bf16[256,128]{1,0:T(8,128)(2,1)S(1)}, u32[]{:S(2)}, u32[]{:S(2)}) collective-permute-start(bf16[256,128]{1,0:T(8,128)(2,1)S(1)} %add_convert_fusion), channel_id=1, source_target_pairs={{0,16},{1,17},{2,18},{3,19},{4,20},{5,21},{6,22},{7,23},{8,9},{9,8... | collective-permute-start | bytes 196616 | tf_op jit(solution)/shard_map/ppermute | solution.py:581
  27.7 0.0 collective-permute-start.4
  27.8 0.0 collective-permute-done.3.refs_1_
  27.8 0.5 %collective-permute-start.5 = (bf16[2,2,4,32,128]{4,3,2,1,0:T(8,128)(2,1)S(1)}, bf16[2,2,4,32,128]{4,3,2,1,0:T(8,128)(2,1)S(1)}, u32[]{:S(2)}, u32[]{:S(2)}) collective-permute-start(bf16[2,2,4,32,128]{4,3,2,1,0:T(8,128)(2,1)S(1)} %collective-permute-done.3.refs_1_), channel_id=1, source_target_pairs={{0,8},{1,9},{2,10},{3,11},{4,12},{5,13},{6,14},{7,15},{8,0},{9,1},... | collective-permute-start | bytes 393224 | tf_op jit(solution)/shard_map/ppermute | solution.py:581
  28.3 1.2 %collective-permute-done.12 = bf16[256,128]{1,0:T(8,128)(2,1)S(1)} collective-permute-done((bf16[256,128]{1,0:T(8,128)(2,1)S(1)}, bf16[256,128]{1,0:T(8,128)(2,1)S(1)}, u32[]{:S(2)}, u32[]{:S(2)}) %collective-permute-start.12) | collective-permute-done | bytes 65568 | tf_op jit(solution)/shard_map/ppermute | solution.py:581
  29.4 1.6 %collective-permute-done.11 = bf16[256,128]{1,0:T(8,128)(2,1)S(1)} collective-permute-done((bf16[256,128]{1,0:T(8,128)(2,1)S(1)}, bf16[256,128]{1,0:T(8,128)(2,1)S(1)}, u32[]{:S(2)}, u32[]{:S(2)}) %collective-permute-start.11) | collective-permute-done | bytes 65568 | tf_op jit(solution)/shard_map/ppermute | solution.py:581
  31.0 0.5 %collective-permute-done.10 = bf16[256,128]{1,0:T(8,128)(2,1)S(1)} collective-permute-done((bf16[256,128]{1,0:T(8,128)(2,1)S(1)}, bf16[256,128]{1,0:T(8,128)(2,1)S(1)}, u32[]{:S(2)}, u32[]{:S(2)}) %collective-permute-start.10) | collective-permute-done | bytes 65568 | tf_op jit(solution)/shard_map/ppermute | solution.py:581
  31.5 0.1 collective-permute-start.13
  31.6 1.1 %join.1 = (bf16[2,32,2,8,128]{4,3,2,1,0:T(8,128)(2,1)}, bf16[2,32,2,8,128]{4,3,2,1,0:T(8,128)(2,1)}) custom-call(bf16[2,2,4,32,128]{4,3,2,1,0:T(8,128)(2,1)S(1)} %get-tuple-element.35.refs_0_, bf16[2,2,4,32,128]{4,3,2,1,0:T(8,128)(2,1)S(1)} %collective-permute-done.3.refs_1_, bf16[2,2,4,32,128]{4,3,2,1,0:T(8,128)(2,1)S(1)} %collective-permute-done.4.refs_2_, ...), custom_call_target="tpu_custom_call" | custom-call | tf_op jit(solution)/shard_map/join/pallas_call | solution.py:704
  32.7 0.3 collective-permute-done.13.other_ref
  33.0 0.9 %unpack.1 = (f32[27,4,32]{2,1,0:T(4,128)}, f32[27,32,64]{2,1,0:T(8,128)}) custom-call(f32[256,128]{1,0:T(8,128)S(1)} %add_add_fusion.own_ref, f32[256,128]{1,0:T(8,128)S(1)} %collective-permute-done.13.other_ref), custom_call_target="tpu_custom_call" | custom-call | tf_op jit(solution)/shard_map/unpack/pallas_call | solution.py:712
  (7 shorter events, 0.1 us)
Async XLA Ops:
  1.9 8.7 %collective-permute-start.2 = (bf16[544,128]{1,0:T(8,128)(2,1)S(1)}, bf16[544,128]{1,0:T(8,128)(2,1)S(1)}, u32[]{:S(2)}, u32[]{:S(2)}) collective-permute-start(bf16[544,128]{1,0:T(8,128)(2,1)S(1)} %get-tuple-element.28), channel_id=1, source_target_pairs={{0,4},{1,5},{2,6},{3,7},{4,0},{5,1},{6,2},{7,3},{8,12},{9,13},{10,... | collective-permute-start | bytes 417800 | tf_op jit(solution)/shard_map/ppermute | solution.py:42
  4.9 4.2 %collective-permute-start = (bf16[224,128]{1,0:T(8,128)(2,1)S(1)}, bf16[224,128]{1,0:T(8,128)(2,1)S(1)}, u32[]{:S(2)}, u32[]{:S(2)}) collective-permute-start(bf16[224,128]{1,0:T(8,128)(2,1)S(1)} %get-tuple-element.26), channel_id=1, source_target_pairs={{0,16},{1,12},{2,13},{3,14},{4,20},{5,8},{6,9},{7,10},{8,5},{9,6},... | collective-permute-start | bytes 172040 | tf_op jit(solution)/shard_map/ppermute | solution.py:42
  6.4 4.2 %collective-permute-start.1 = (bf16[224,128]{1,0:T(8,128)(2,1)S(1)}, bf16[224,128]{1,0:T(8,128)(2,1)S(1)}, u32[]{:S(2)}, u32[]{:S(2)}) collective-permute-start(bf16[224,128]{1,0:T(8,128)(2,1)S(1)} %get-tuple-element.27), channel_id=1, source_target_pairs={{0,16},{1,8},{2,9},{3,10},{4,20},{5,12},{6,13},{7,14},{8,1},{9,2},... | collective-permute-start | bytes 172040 | tf_op jit(solution)/shard_map/ppermute | solution.py:42
  13.5 1.4 %collective-permute-start.6 = (bf16[224,128]{1,0:T(8,128)(2,1)S(1)}, bf16[224,128]{1,0:T(8,128)(2,1)S(1)}, u32[]{:S(2)}, u32[]{:S(2)}) collective-permute-start(bf16[224,128]{1,0:T(8,128)(2,1)S(1)} %get-tuple-element.40), channel_id=1, source_target_pairs={{0,8},{1,9},{2,10},{3,11},{4,12},{5,13},{6,14},{7,15},{8,0},{9,1},... | collective-permute-start | bytes 172040 | tf_op jit(solution)/shard_map/ppermute | solution.py:581
  15.0 6.0 %collective-permute-start.8 = (bf16[256,128]{1,0:T(8,128)(2,1)S(1)}, bf16[256,128]{1,0:T(8,128)(2,1)S(1)}, u32[]{:S(2)}, u32[]{:S(2)}) collective-permute-start(bf16[256,128]{1,0:T(8,128)(2,1)S(1)} %pad_maximum_fusion), channel_id=1, source_target_pairs={{0,2},{1,3},{2,0},{3,1},{4,6},{5,7},{6,4},{7,5},{8,12},{9,13},{10,... | collective-permute-start | bytes 196616 | tf_op jit(solution)/shard_map/ppermute | solution.py:581
  17.2 4.3 %collective-permute-start.7 = (bf16[256,128]{1,0:T(8,128)(2,1)S(1)}, bf16[256,128]{1,0:T(8,128)(2,1)S(1)}, u32[]{:S(2)}, u32[]{:S(2)}) collective-permute-start(bf16[256,128]{1,0:T(8,128)(2,1)S(1)} %pad_maximum_fusion), channel_id=1, source_target_pairs={{0,1},{1,0},{2,3},{3,2},{4,5},{5,4},{6,7},{7,6},{8,24},{9,25},{10,... | collective-permute-start | bytes 196616 | tf_op jit(solution)/shard_map/ppermute | solution.py:581
  18.1 6.1 %collective-permute-start.9 = (bf16[256,128]{1,0:T(8,128)(2,1)S(1)}, bf16[256,128]{1,0:T(8,128)(2,1)S(1)}, u32[]{:S(2)}, u32[]{:S(2)}) collective-permute-start(bf16[256,128]{1,0:T(8,128)(2,1)S(1)} %pad_maximum_fusion), channel_id=1, source_target_pairs={{0,3},{1,2},{2,1},{3,0},{4,7},{5,6},{6,5},{7,4},{8,28},{9,29},{10,... | collective-permute-start | bytes 196616 | tf_op jit(solution)/shard_map/ppermute | solution.py:581
  19.5 8.3 %collective-permute-start.3 = (bf16[2,2,4,32,128]{4,3,2,1,0:T(8,128)(2,1)S(1)}, bf16[2,2,4,32,128]{4,3,2,1,0:T(8,128)(2,1)S(1)}, u32[]{:S(2)}, u32[]{:S(2)}) collective-permute-start(bf16[2,2,4,32,128]{4,3,2,1,0:T(8,128)(2,1)S(1)} %get-tuple-element.36), channel_id=1, source_target_pairs={{0,4},{1,5},{2,6},{3,7},{4,0},{5,1},{6,2},{7,3},{8,12},{9,13},{10,... | collective-permute-start | bytes 393224 | tf_op jit(solution)/shard_map/ppermute | solution.py:581
  24.2 5.2 %collective-permute-start.12 = (bf16[256,128]{1,0:T(8,128)(2,1)S(1)}, bf16[256,128]{1,0:T(8,128)(2,1)S(1)}, u32[]{:S(2)}, u32[]{:S(2)}) collective-permute-start(bf16[256,128]{1,0:T(8,128)(2,1)S(1)} %add_convert_fusion), channel_id=1, source_target_pairs={{0,20},{1,21},{2,22},{3,23},{4,16},{5,17},{6,18},{7,19},{8,11},{9,... | collective-permute-start | bytes 196616 | tf_op jit(solution)/shard_map/ppermute | solution.py:581
  26.8 4.3 %collective-permute-start.11 = (bf16[256,128]{1,0:T(8,128)(2,1)S(1)}, bf16[256,128]{1,0:T(8,128)(2,1)S(1)}, u32[]{:S(2)}, u32[]{:S(2)}) collective-permute-start(bf16[256,128]{1,0:T(8,128)(2,1)S(1)} %add_convert_fusion), channel_id=1, source_target_pairs={{0,4},{1,5},{2,6},{3,7},{4,0},{5,1},{6,2},{7,3},{8,10},{9,11},{10,... | collective-permute-start | bytes 196616 | tf_op jit(solution)/shard_map/ppermute | solution.py:581
  27.2 4.3 %collective-permute-start.10 = (bf16[256,128]{1,0:T(8,128)(2,1)S(1)}, bf16[256,128]{1,0:T(8,128)(2,1)S(1)}, u32[]{:S(2)}, u32[]{:S(2)}) collective-permute-start(bf16[256,128]{1,0:T(8,128)(2,1)S(1)} %add_convert_fusion), channel_id=1, source_target_pairs={{0,16},{1,17},{2,18},{3,19},{4,20},{5,21},{6,22},{7,23},{8,9},{9,8... | collective-permute-start | bytes 196616 | tf_op jit(solution)/shard_map/ppermute | solution.py:581
  27.7 3.9 %collective-permute-start.4 = (bf16[2,2,4,32,128]{4,3,2,1,0:T(8,128)(2,1)S(1)}, bf16[2,2,4,32,128]{4,3,2,1,0:T(8,128)(2,1)S(1)}, u32[]{:S(2)}, u32[]{:S(2)}) collective-permute-start(bf16[2,2,4,32,128]{4,3,2,1,0:T(8,128)(2,1)S(1)} %get-tuple-element.35.refs_0_), channel_id=1, source_target_pairs={{0,8},{1,9},{2,10},{3,11},{4,12},{5,13},{6,14},{7,15},{8,0},{9,1},... | collective-permute-start | bytes 393224 | tf_op jit(solution)/shard_map/ppermute | solution.py:581
  27.8 3.9 %collective-permute-start.5 = (bf16[2,2,4,32,128]{4,3,2,1,0:T(8,128)(2,1)S(1)}, bf16[2,2,4,32,128]{4,3,2,1,0:T(8,128)(2,1)S(1)}, u32[]{:S(2)}, u32[]{:S(2)}) collective-permute-start(bf16[2,2,4,32,128]{4,3,2,1,0:T(8,128)(2,1)S(1)} %collective-permute-done.3.refs_1_), channel_id=1, source_target_pairs={{0,8},{1,9},{2,10},{3,11},{4,12},{5,13},{6,14},{7,15},{8,0},{9,1},... | collective-permute-start | bytes 393224 | tf_op jit(solution)/shard_map/ppermute | solution.py:581
  31.5 1.4 %collective-permute-start.13 = (f32[256,128]{1,0:T(8,128)S(1)}, f32[256,128]{1,0:T(8,128)S(1)}, u32[]{:S(2)}, u32[]{:S(2)}) collective-permute-start(f32[256,128]{1,0:T(8,128)S(1)} %add_add_fusion.own_ref), channel_id=1, source_target_pairs={{0,8},{1,9},{2,10},{3,11},{4,12},{5,13},{6,14},{7,15},{8,0},{9,1},... | collective-permute-start | bytes 393224 | tf_op jit(solution)/shard_map/ppermute | solution.py:581
